TPU v7x, 512 devices: a whole 4x4x16 slice. The times are simulated.
512 devices in a mesh: row: 16 (over z), col: 32 (over y, x, core).
Axes of the slice: x: 4, y: 4, z: 16, core: 2. Of those that a mesh axis runs over, the one named last changes fastest.
Arguments:
- matrix: float32 [4, 16, 256, 2, 32, 256], P(None, 'row', None, None, 'col'), may hold values from -6 to 6
- panel_t: float32 [256, 4, 16, 256], P('col', None, 'row'), may hold values from -3 to 3
Outputs:
- updated: float32 [4, 16, 256, 2, 32, 256], P(None, 'row', None, None, 'col')
- vectors: float32 [256, 4, 16, 256], P('col', None, 'row')
- band_block: float32 [256, 256], replicated
- reflector_factor: float32 [256, 256], replicated
All inputs are finite; a program needn't handle non-finite values.
Results may differ from a plain program's by a relative error of at most 0.00017.
Values sent between devices are 32-bit elements; how exact they have to be, the bound alone decides.
No kernel may reach another device: no remote copies, remote signals or barrier semaphores. Data moves between devices by JAX's collectives and lax.ppermute only.
A program may use at most 64 MiB of HBM per device.

v0:
```python
import jax
import jax.numpy as jnp
from jax import lax
from jax.sharding import PartitionSpec as P


def from_root(value, axis, source):
    kept = jnp.where(lax.axis_index(axis) == source, value, 0).astype(value.dtype)
    return lax.psum(kept, axis)


def matmul(multiplier, multiplicand):
    return jnp.dot(multiplier, multiplicand, precision=lax.Precision.HIGHEST)


def contract_first(multiplier, multiplicand):
    return lax.dot_general(
        multiplier, multiplicand, (((0,), (0,)), ((), ())), precision=lax.Precision.HIGHEST
    )


def contract_last(multiplier, multiplicand):
    return lax.dot_general(
        multiplier, multiplicand, (((1,), (1,)), ((), ())), precision=lax.Precision.HIGHEST
    )


def lower_solve(factor, right_side, transposed):
    return lax.linalg.triangular_solve(
        factor, right_side, left_side=True, lower=True, transpose_a=transposed
    )


def pick_slots(block_t, tile_cols, groups, slot_index):
    leading = block_t.shape[0]
    shaped = block_t.reshape(leading, tile_cols, groups, block_t.shape[1] // (tile_cols * groups))
    picked = lax.dynamic_index_in_dim(shaped, slot_index, 2, keepdims=False)
    return picked.reshape(leading, -1)


def body(matrix, panel_t):
    tile_rows = matrix.shape[0]
    tile_size = matrix.shape[2]
    tile_cols = matrix.shape[3]
    row_count = lax.axis_size("row")
    col_count = lax.axis_size("col")
    row_index = lax.axis_index("row")
    col_index = lax.axis_index("col")
    groups = col_count // row_count
    slot_index = col_index // row_count
    root_row = col_index % row_count
    local_rows = tile_rows * tile_size
    local_cols = tile_cols * tile_size
    stored = matrix.reshape(local_rows, local_cols)
    identity = jnp.eye(tile_size, dtype=jnp.float32)
    gathered = lax.all_gather(panel_t, "col", axis=0, tiled=True)
    panel_rows_t = gathered.reshape(tile_size, local_rows)
    first_gram = lax.psum(matmul(panel_rows_t, panel_rows_t.T), "row")
    first_factor = jnp.linalg.cholesky(first_gram)
    orthonormal = lower_solve(first_factor, panel_rows_t, False)
    band_block = -first_factor.T
    top_flag = (row_index == 0).astype(jnp.float32)
    vectors_t = jnp.concatenate(
        [orthonormal[:, :tile_size] + top_flag * identity, orthonormal[:, tile_size:]], axis=1
    )
    top_block = from_root(orthonormal[:, :tile_size], "row", 0) + identity
    top_factor = jnp.linalg.cholesky(contract_first(top_block, top_block))
    reflector = lower_solve(top_factor, lower_solve(top_factor, top_block.T, False), True)
    vectors_c = from_root(pick_slots(vectors_t, tile_cols, groups, slot_index), "row", root_row)
    row_numbers = jnp.arange(local_rows)
    col_numbers = jnp.arange(local_cols)
    global_row = (
        row_numbers // tile_size * row_count + row_index
    ) * tile_size + row_numbers % tile_size
    global_col = (
        col_numbers // tile_size * col_count + col_index
    ) * tile_size + col_numbers % tile_size
    on_lower = global_row[:, None] >= global_col[None, :]
    lower_part = jnp.where(on_lower, stored, 0.0)
    strict_part = jnp.where(global_row[:, None] > global_col[None, :], stored, 0.0)
    row_terms = contract_last(vectors_c, lower_part)
    mirror_terms = matmul(vectors_t, strict_part)
    column_sums = lax.psum(mirror_terms, "row")
    wanted = ((jnp.arange(groups) == slot_index) & (root_row == row_index)).astype(jnp.float32)
    spread = column_sums.reshape(tile_size, tile_cols, 1, tile_size) * wanted[None, None, :, None]
    products_t = lax.psum(row_terms + spread.reshape(tile_size, local_rows), "col")
    curvature = lax.psum(contract_last(vectors_t, products_t), "row")
    mixed_term = matmul(matmul(reflector.T, curvature), reflector)
    update_rows_t = matmul(reflector.T, products_t) - 0.5 * matmul(mixed_term.T, vectors_t)
    update_cols_t = from_root(
        pick_slots(update_rows_t, tile_cols, groups, slot_index), "row", root_row
    )
    correction = contract_first(vectors_t, update_cols_t) + contract_first(update_rows_t, vectors_c)
    updated = jnp.where(on_lower, stored - correction, 0.0).reshape(matrix.shape)
    vector_rows = tile_size // col_count
    vectors_out = lax.dynamic_slice_in_dim(
        vectors_t, col_index * vector_rows, vector_rows, 0
    ).reshape(panel_t.shape)
    return (updated, vectors_out, band_block, reflector)


def solution(mesh):
    placed = (P(None, "row", None, None, "col", None), P("col", None, "row", None))
    return jax.shard_map(
        body,
        mesh=mesh,
        in_specs=placed,
        out_specs=(P(None, "row", None, None, "col", None), P("col", None, "row", None), P(), P()),
        check_vma=False,
    )
```

profile of v0, /device:TPU:1, one launch (start us, length us, event | category | flops | bytes accessed | tf_op | source)
XLA Modules:
  0.0 942.6 jit_solution(7308873147574783612)
XLA Ops:
  7.2 1.4 copy.12
  8.7 9.0 reduce.8
  17.7 1.8 copy.22
  20.0 55.6 %all-gather.2.cloned.1.call-done = f32[256,4,1,256]{3,0,1,2:T(8,128)} async-done(((f32[8,4,1,256]{3,0,1,2:T(8,128)}), f32[256,4,1,256]{3,0,1,2:T(8,128)}) %all-gather.2.cloned.1.call-update) | async-done | bytes 1048592 | tf_op jit(solution)/shard_map/all_gather | solution.py:56
  75.7 3.4 convolution_bitcast_fusion
  79.3 1.0 fusion.63
  80.3 1.2 copy.15
  81.5 1.2 copy.16
  82.8 121.7 %all-reduce.9.cloned.1.call-done = f32[256,256]{0,1:T(8,128)} async-done(((f32[256,256]{0,1:T(8,128)}), f32[256,256]{0,1:T(8,128)}) %all-reduce.9.cloned.1.call-update) | async-done | bytes 262160 | tf_op jit(solution)/shard_map/psum | solution.py:58
  204.5 1.1 copy.14
  205.6 1.0 fusion.17
  206.6 0.7 copy-done.8
  207.3 11.7 %cholesky.130 = f32[128,128]{1,0:T(8,128)S(1)} custom-call(f32[128,128]{1,0:T(8,128)S(1)} %cholesky.194), custom_call_target="Cholesky" | custom-call | tf_op jit(solution)/shard_map/jit(cholesky)/cholesky | solution.py:59
  219.1 9.8 %custom-call.19 = f32[1,128,128]{1,2,0:T(8,128)S(1)} custom-call(f32[1,128,128]{2,1,0:T(8,128)S(1)} %get-tuple-element.66), custom_call_target="InvertDiagBlocksLowerTriangular" | custom-call | tf_op jit(solution)/shard_map/jit(cholesky)/cholesky | solution.py:59
  228.9 1.0 constant_dynamic-update-slice_fusion.1
  229.9 1.1 convolution_subtract_fusion.4
  231.1 11.7 %cholesky.147 = f32[128,128]{1,0:T(8,128)S(1)} custom-call(f32[128,128]{1,0:T(8,128)S(1)} %convolution_subtract_fusion.4), custom_call_target="Cholesky" | custom-call | tf_op jit(solution)/shard_map/jit(cholesky)/cholesky | solution.py:59
  244.8 1.7 negate_bitcast_fusion
  247.2 4.4 while.2
  248.2 1.4 bitcast_dynamic-update-slice_fusion.4
  250.2 1.4 bitcast_dynamic-update-slice_fusion.4
  252.2 20.5 %custom-call.16 = f32[2,128,128]{1,2,0:T(8,128)S(1)} custom-call(f32[2,128,128]{2,1,0:T(8,128)} %copy-done.12), custom_call_target="InvertDiagBlocksLowerTriangular" | custom-call | tf_op jit(solution)/shard_map/triangular_solve | solution.py:29
  273.4 1.0 convolution_subtract_fusion
  275.0 0.7 broadcast_select_fusion.2
  275.9 1.9 reshape.124
  277.7 3.0 fusion.1
  280.7 2.1 mul.81
  282.8 3.1 fusion.14
  285.9 0.8 copy.23
  286.9 135.7 %all-reduce.17.cloned.1.call-done = (f32[256,512]{1,0:T(8,128)}, f32[256,2,256]{2,1,0:T(2,128)}) async-done(((f32[256,512]{1,0:T(8,128)}, f32[256,2,256]{2,1,0:T(2,128)}), (f32[256,512]{1,0:T(8,128)}, f32[256,2,256]{2,1,0:T(2,128)})) %all-reduce.17.cloned.1.call-update) | async-done | bytes 1048592 | tf_op jit(solution)/shard_map/psum | solution.py:9
  422.6 2.4 mul.82
  424.9 3.0 mul.83
  428.0 4.4 fusion.4
  432.5 141.8 %all-reduce.11.cloned.1.call-done = f32[256,1024]{1,0:T(8,128)} async-done(((f32[256,1024]{1,0:T(8,128)}), f32[256,1024]{1,0:T(8,128)}) %all-reduce.11.cloned.1.call-update) | async-done | bytes 1048592 | tf_op jit(solution)/shard_map/psum | solution.py:86
  574.3 3.0 fusion.65
  577.5 127.3 %all-reduce.15.cloned.1.call-done = (f32[256,256]{1,0:T(8,128)}, f32[256,256]{1,0:T(8,128)}) async-done(((f32[256,256]{1,0:T(8,128)}, f32[256,256]{1,0:T(8,128)}), (f32[256,256]{1,0:T(8,128)}, f32[256,256]{1,0:T(8,128)})) %all-reduce.15.cloned.1.call-update) | async-done | bytes 524304 | tf_op jit(solution)/shard_map/psum | solution.py:9
  704.8 1.6 fusion.20
  706.5 1.7 fusion.19
  708.1 0.8 copy.17
  709.0 1.0 fusion.16
  710.0 0.7 copy-done.9
  710.7 11.7 %cholesky.164 = f32[128,128]{1,0:T(8,128)S(1)} custom-call(f32[128,128]{1,0:T(8,128)S(1)} %cholesky.197), custom_call_target="Cholesky" | custom-call | tf_op jit(solution)/shard_map/jit(cholesky)/cholesky | solution.py:67
  722.5 9.8 %custom-call.20 = f32[1,128,128]{1,2,0:T(8,128)S(1)} custom-call(f32[1,128,128]{2,1,0:T(8,128)S(1)} %get-tuple-element.62), custom_call_target="InvertDiagBlocksLowerTriangular" | custom-call | tf_op jit(solution)/shard_map/jit(cholesky)/cholesky | solution.py:67
  732.3 1.0 constant_dynamic-update-slice_fusion
  733.3 1.1 convolution_subtract_fusion.3
  734.4 11.7 %cholesky.181 = f32[128,128]{1,0:T(8,128)S(1)} custom-call(f32[128,128]{1,0:T(8,128)S(1)} %convolution_subtract_fusion.3), custom_call_target="Cholesky" | custom-call | tf_op jit(solution)/shard_map/jit(cholesky)/cholesky | solution.py:67
  746.9 0.7 compare_reduce_fusion.1
  748.9 1.0 select_select_fusion
  749.9 4.1 while.3
  750.5 1.4 bitcast_dynamic-update-slice_fusion.5
  752.6 1.4 bitcast_dynamic-update-slice_fusion.5
  754.7 20.7 %custom-call.17 = f32[2,128,128]{1,2,0:T(8,128)S(1)} custom-call(f32[2,128,128]{2,1,0:T(8,128)} %copy-done.11), custom_call_target="InvertDiagBlocksLowerTriangular" | custom-call | tf_op jit(solution)/shard_map/triangular_solve | solution.py:29
  775.4 1.3 fusion.21
  776.7 1.3 convolution_subtract_fusion.2
  780.3 1.0 fusion.64
  781.3 2.0 fusion.5
  783.3 3.1 reshape.125
  786.4 3.1 fusion.15
  789.5 0.8 copy.25
  791.0 0.8 copy.19
  791.9 132.2 %all-reduce.13.cloned.1.call-done = f32[256,512]{1,0:T(8,128)} async-done(((f32[256,512]{1,0:T(8,128)}), f32[256,512]{1,0:T(8,128)}) %all-reduce.13.cloned.1.call-update) | async-done | bytes 524304 | tf_op jit(solution)/shard_map/psum | solution.py:9
  924.1 3.0 fusion.68
  927.1 3.7 compare_select_fusion
  930.8 4.7 reshape.167
  (76 shorter events, 11.4 us)
Async XLA Ops:
  7.2 68.5 %all-gather.2.cloned.1.call-start = ((), (), s32[]{:S(2)}) async-start(), calls=%async_computation | async-start | bytes 1081344 | tf_op jit(solution)/shard_map/all_gather | solution.py:56
  8.6 195.9 %all-reduce.9.cloned.1.call-start = ((), (), s32[]{:S(2)}) async-start(), calls=%async_computation.1 | async-start | bytes 524288 | tf_op jit(solution)/shard_map/psum | solution.py:58
  75.7 3.6 copy-start.2
  79.0 343.5 %all-reduce.17.cloned.1.call-start = ((), (), s32[]{:S(2)}) async-start(), calls=%async_computation.5 | async-start | bytes 2097152 | tf_op jit(solution)/shard_map/psum | solution.py:9
  206.6 0.7 copy-start.8
  242.8 1.9 copy-start.6
  251.6 0.7 copy-start.12
  286.8 287.5 %all-reduce.11.cloned.1.call-start = ((), (), s32[]{:S(2)}) async-start(), calls=%async_computation.2 | async-start | bytes 2097152 | tf_op jit(solution)/shard_map/psum | solution.py:86
  432.4 272.4 %all-reduce.15.cloned.1.call-start = ((), (), s32[]{:S(2)}) async-start(), calls=%async_computation.4 | async-start | bytes 1048576 | tf_op jit(solution)/shard_map/psum | solution.py:9
  577.3 346.8 %all-reduce.13.cloned.1.call-start = ((), (), s32[]{:S(2)}) async-start(), calls=%async_computation.3 | async-start | bytes 1048576 | tf_op jit(solution)/shard_map/psum | solution.py:9
  710.0 0.7 copy-start.9
  746.2 2.7 copy-start.5
  754.0 0.7 copy-start.11
  775.4 3.9 copy-start.10
  775.4 4.9 copy-start.3
  779.2 4.1 copy-start.1
  786.4 4.6 copy-start.7
  924.1 3.0 copy-start
  924.1 3.0 copy-start.4
Sparse Core Ops, SparseCore 0:
  11.6 63.9 all-gather.1
  79.2 125.3 all-reduce.8
  286.9 135.6 all-reduce.16
  432.6 141.6 all-reduce.10
  577.4 127.3 all-reduce.14
  790.5 133.5 all-reduce.12
where the time goes:
time: 958 us; the launch traced here: 943 us
  waiting for transfers between devices  714 us (75%)
  other arithmetic  133 us (14%)
  local copies, waits for them, and re-layouts  40.5 us (4%)
  matrix products  36.4 us (4%)
  between operations  17.4 us (2%)
    psum x3, waiting for transfers between devices, from_root(): return lax.psum(kept, axis)  395 us
    psum x1, waiting for transfers between devices, body(): lax.psum(row_terms + spread.reshape(tile_size, local_rows), 'col')  142 us
    psum x1, waiting for transfers between devices, body(): first_gram = lax.psum(matmul(panel_rows_t, panel_rows_t.T), 'row')  122 us
    all_gather x1, waiting for transfers between devices, body(): gathered = lax.all_gather(panel_t, 'col', axis=0, tiled=True)  55.6 us
    another operation x5, other arithmetic, lower_solve(): lax.linalg.triangular_solve(factor, right_side, left_side=True, lower=Tru...  42.7 us
    another operation x7, other arithmetic, body(): top_factor = jnp.linalg.cholesky(contract_first(top_block, top_block))  34.7 us
    another operation x6, other arithmetic, body(): first_factor = jnp.linalg.cholesky(first_gram)  33.9 us
  transfers between devices with their start and end apart: 6, of which 6 were waited for; matrix products, arithmetic and copies ran while one was open for 2% of the time, Pallas kernels for 0%

commit v1 on v0

v1 whole, which is shorter than its diff:
```python
import jax
import jax.numpy as jnp
from jax import lax
from jax.experimental import pallas as pl
from jax.experimental.pallas import tpu as pltpu
from jax.sharding import PartitionSpec as P

NB = 256
TR = 4
TC = 2
N_ROW = 16
N_COL = 32
LANES = 128
BS = 16
SHARE = NB // N_COL
CHUNK = NB // N_ROW
F32 = jnp.float32
VMEM = pl.BlockSpec(memory_space=pltpu.VMEM)
SMEM = pl.BlockSpec(memory_space=pltpu.SMEM)


def call(kernel, outs, scratch=(), n_scalars=0, n_in=1, name=None, flops=0, moved=0):
    return pl.pallas_call(
        kernel,
        out_shape=[jax.ShapeDtypeStruct(shape, F32) for shape in outs],
        in_specs=[SMEM] * n_scalars + [VMEM] * n_in,
        out_specs=[VMEM] * len(outs),
        scratch_shapes=[pltpu.VMEM(shape, F32) for shape in scratch],
        compiler_params=pltpu.CompilerParams(vmem_limit_bytes=40 * 2**20),
        cost_estimate=pl.CostEstimate(flops=flops, bytes_accessed=moved, transcendentals=0),
        name=name,
    )


def exact(a, b, ca=1, cb=0):
    return lax.dot_general(
        a,
        b,
        (((ca,), (cb,)), ((), ())),
        precision=lax.Precision.HIGHEST,
        preferred_element_type=F32,
    )


def split(a):
    high = a.astype(jnp.bfloat16)
    return high, (a - high.astype(F32)).astype(jnp.bfloat16)


def product(a, b, ca=1, cb=0):
    def one(x, y):
        return lax.dot_general(x, y, (((ca,), (cb,)), ((), ())), preferred_element_type=F32)

    return one(a[0], b[0]) + (one(a[0], b[1]) + one(a[1], b[0]))


def linear_tile(ref, tile, tiles):
    halves = NB // LANES
    stride = tiles * halves
    return jnp.concatenate(
        [ref[pl.ds(tile * halves + half, NB, stride), :] for half in range(halves)], axis=1
    )


def matrix_rows(t, u, half):
    return pl.ds((t * NB) * TC * 2 + u * 2 + half, NB, TC * 2)


def matrix_tile(ref, t, u):
    return jnp.concatenate([ref[matrix_rows(t, u, half), :] for half in range(2)], axis=1)


def gram_kernel(place, own_ref, panel_ref, out_ref):
    total = jnp.zeros((SHARE, NB), F32)
    for piece in range(TR * 2):
        total += exact(
            own_ref[pl.ds(piece, SHARE, TR * 2), :], panel_ref[pl.ds(piece, NB, TR * 2), :], 1, 1
        )
    out_ref[:, :NB] = total
    top = jnp.concatenate([own_ref[pl.ds(half, SHARE, TR * 2), :] for half in range(2)], axis=1)
    out_ref[:, NB:] = jnp.where(place[0] == 0, top, 0.0)


def factor_kernel(g_ref, band_ref, linv_ref, refl_ref, a_ref, u_ref):
    n = NB
    steps = n // BS
    rows = lax.broadcasted_iota(jnp.int32, (BS, LANES), 0)
    lanes = lax.broadcasted_iota(jnp.int32, (BS, LANES), 1)
    eye = (rows == lanes).astype(F32)
    wide = lax.broadcasted_iota(jnp.int32, (BS, n), 1)
    full_row = lax.broadcasted_iota(jnp.int32, (n, n), 0)
    full_col = lax.broadcasted_iota(jnp.int32, (n, n), 1)
    a_ref[...] = g_ref[:, :n]

    def advance(base, update, row):
        a_ref[: n - BS, :] = pltpu.roll(base[BS:] - update[BS:], n - BS, 1)
        a_ref[n - BS :, :] = pltpu.roll(row, n - BS, 1)

    def chol_step(step, carry):
        left = n - BS * step
        a = a_ref[...]
        first, second = a[:BS, :LANES], a[:BS, LANES:]
        heads = [jnp.broadcast_to(first[:, k : k + 1], (BS, LANES)) for k in range(BS)]
        inner = eye
        pivots = jnp.ones((BS, LANES), F32)
        for j in range(BS):
            pivot = heads[j][j : j + 1]
            factor = jnp.where(rows > j, heads[j], 0.0) * (1.0 / pivot)
            pivots = jnp.where(rows == j, pivot, pivots)
            for k in range(j + 1, BS):
                heads[k] = heads[k] - factor * heads[k][j : j + 1]
            first = first - factor * first[j : j + 1]
            second = second - factor * second[j : j + 1]
            inner = inner - factor * inner[j : j + 1]
        scale = lax.rsqrt(pivots)
        scale = scale * (1.5 - 0.5 * pivots * scale * scale)
        first, second, inner = first * scale, second * scale, inner * scale
        upper = jnp.concatenate([jnp.where(lanes >= rows, first, 0.0), second], axis=1)
        upper = jnp.where(wide < left, upper, 0.0)
        u_ref[pl.ds(pl.multiple_of(step * BS, BS), BS), :] = pltpu.roll(upper, step * BS, 1)
        row = jnp.concatenate([jnp.where(lanes < BS, inner, first), second], axis=1)
        update = exact(jnp.where(wide >= BS, upper, 0.0), row, 0, 0)
        advance(jnp.where((full_col < BS) & (full_row < left), 0.0, a), update, row)
        return carry

    lax.fori_loop(0, steps, chol_step, 0)
    linv = jnp.where(full_col <= full_row, a_ref[...], 0.0)
    linv_ref[...] = linv
    band_ref[...] = -u_ref[...]
    a_ref[...] = exact(linv, g_ref[:, n:]) + (full_row == full_col).astype(F32)

    def inverse_step(step, carry):
        a = a_ref[...]
        first, second = a[:BS, :LANES], a[:BS, LANES:]
        heads = [jnp.broadcast_to(first[:, k : k + 1], (BS, LANES)) for k in range(BS)]
        first = jnp.where(lanes < BS, eye, first)
        for j in range(BS):
            head = heads[j]
            inverse = 1.0 / head[j : j + 1]

            def put(value):
                scaled = value[j : j + 1] * inverse
                return jnp.where(rows == j, scaled, value - head * scaled)

            for k in range(j + 1, BS):
                heads[k] = put(heads[k])
            first, second = put(first), put(second)
        row = jnp.concatenate([first, second], axis=1)
        update = exact(a[:, :BS], row)
        advance(jnp.where(full_col < BS, 0.0, a), update, row)
        return carry

    lax.fori_loop(0, steps, inverse_step, 0)
    refl_ref[...] = a_ref[...]


def eye_tile():
    return (
        lax.broadcasted_iota(jnp.int32, (NB, NB), 0) == lax.broadcasted_iota(jnp.int32, (NB, NB), 1)
    ).astype(F32)


def symmetric_kernel(
    place, linv_ref, panel_rows_ref, panel_cols_ref, matrix_ref,
    rows_ref, cols_ref, row_terms_ref, mirror_ref, vectors_ref,
):
    row, col = place[0], place[1]
    linv = split(linv_ref[...])
    cols, rows = [], []
    for u in range(TC):
        value = product(linv, split(linear_tile(panel_cols_ref, u, TC)))
        if u == 0:
            value = value + jnp.where(col == 0, eye_tile(), 0.0)
        cols_ref[:, pl.ds(u * NB, NB)] = value
        cols.append(split(value))
    for t in range(TR):
        value = product(linv, split(linear_tile(panel_rows_ref, t, TR)))
        if t == 0:
            value = value + jnp.where(row == 0, eye_tile(), 0.0)
        rows_ref[:, pl.ds(t * NB, NB)] = value
        rows.append(split(value))
    mine = rows_ref[pl.ds(pl.multiple_of(col * SHARE, SHARE), SHARE), :]
    for piece in range(TR * 2):
        vectors_ref[pl.ds(piece, SHARE, TR * 2), :] = mine[:, piece * LANES : (piece + 1) * LANES]

    row_terms_ref[...] = jnp.zeros((NB, TR * NB), F32)
    mirror_ref[...] = jnp.zeros((NB, TC * NB), F32)
    for t in range(TR):
        here = pl.ds(t * NB, NB)
        for u in range(TC):
            there = pl.ds(u * NB, NB)
            i, j = t * N_ROW + row, u * N_COL + col

            @pl.when(i > j)
            def _():
                tile = split(matrix_tile(matrix_ref, t, u))
                row_terms_ref[:, here] += product(cols[u], tile, 1, 1)
                mirror_ref[:, there] += product(rows[t], tile)

            @pl.when(i == j)
            def _():
                tile = matrix_tile(matrix_ref, t, u)
                r = lax.broadcasted_iota(jnp.int32, (NB, NB), 0)
                c = lax.broadcasted_iota(jnp.int32, (NB, NB), 1)
                row_terms_ref[:, here] += product(cols[u], split(jnp.where(r >= c, tile, 0.0)), 1, 1)
                mirror_ref[:, there] += product(rows[t], split(jnp.where(r > c, tile, 0.0)))


def curvature_kernel(share_ref, rows_ref, out_ref):
    out_ref[...] = product(split(share_ref[...]), split(rows_ref[...]), 1, 1)


def update_kernel(
    place, matrix_ref, rows_ref, cols_ref, sums_ref, part_ref, curv_ref, refl_ref, out_ref
):
    row, col = place[0], place[1]
    refl = split(refl_ref[...])
    half_mixed = split(0.5 * product(split(product(refl, split(curv_ref[...]), 0, 0)), refl))
    sides = []
    for u in range(TC):
        span = 2 * CHUNK + SHARE
        summed = jnp.concatenate(
            [part_ref[pl.ds(k * span + u * CHUNK, CHUNK), :] for k in range(N_ROW)], axis=0
        )
        vectors = split(cols_ref[:, pl.ds(u * NB, NB)])
        update = product(refl, split(summed), 0, 0) - product(half_mixed, vectors, 0, 0)
        sides.append((vectors, split(update)))
    for t in range(TR):
        here = pl.ds(t * NB, NB)
        vectors = split(rows_ref[:, here])
        update = split(
            product(refl, split(sums_ref[:, here]), 0, 0) - product(half_mixed, vectors, 0, 0)
        )
        for u in range(TC):
            i, j = t * N_ROW + row, u * N_COL + col

            @pl.when(i >= j)
            def _():
                change = product(vectors, sides[u][1], 0, 0) + product(update, sides[u][0], 0, 0)
                value = matrix_tile(matrix_ref, t, u) - change
                r = lax.broadcasted_iota(jnp.int32, (NB, NB), 0)
                c = lax.broadcasted_iota(jnp.int32, (NB, NB), 1)
                value = jnp.where((r >= c) | (i > j), value, 0.0)
                for half in range(2):
                    out_ref[matrix_rows(t, u, half), :] = value[:, half * LANES : (half + 1) * LANES]

            @pl.when(i < j)
            def _():
                for half in range(2):
                    out_ref[matrix_rows(t, u, half), :] = jnp.zeros((NB, LANES), F32)


def spread(value, axis, count):
    return lax.all_to_all(jnp.tile(value, (count, 1)), axis, 0, 0, tiled=True)


def routes():
    one, two = [], []
    for r in range(N_ROW):
        for c in range(N_COL):
            near = (c // 2) * N_COL + r
            far = near + N_ROW
            one.append((r * N_COL + c, far if c % 2 else near))
            two.append((r * N_COL + c, near if c % 2 else far))
    return one, two


def to_cols(even, odd, col_index):
    one, two = routes()
    flip, low = col_index % 2 == 1, col_index < N_ROW
    first = lax.ppermute(jnp.where(flip, odd, even), ("row", "col"), one)
    second = lax.ppermute(jnp.where(flip, even, odd), ("row", "col"), two)
    return jnp.where(low, first, second), jnp.where(low, second, first)


def to_rows(early, late, col_index):
    one, two = ([(there, here) for here, there in route] for route in routes())
    flip, low = col_index % 2 == 1, col_index < N_ROW
    first = lax.ppermute(jnp.where(low, early, late), ("row", "col"), one)
    second = lax.ppermute(jnp.where(low, late, early), ("row", "col"), two)
    return jnp.where(flip, second, first), jnp.where(flip, first, second)


def body(matrix, panel_t):
    row_index = lax.axis_index("row")
    col_index = lax.axis_index("col")
    place = jnp.stack([row_index, col_index]).astype(jnp.int32)
    stored = matrix.reshape(TR * NB * TC * 2, LANES)
    own = panel_t.reshape(SHARE * TR * 2, LANES)

    with jax.named_scope("panel_rows"):
        panel_rows = spread(own, "col", N_COL)
    with jax.named_scope("panel_cols"):
        by_tile = own.reshape(SHARE, TR, 2, LANES)
        chunk = to_cols(
            by_tile[:, 0::2].reshape(-1, LANES), by_tile[:, 1::2].reshape(-1, LANES), col_index
        )
        panel_cols = spread(jnp.concatenate(chunk, axis=0), "row", N_ROW)
    with jax.named_scope("gram"):
        (partial,) = call(
            gram_kernel, [(SHARE, 2 * NB)], n_scalars=1, n_in=2, name="gram", moved=1 << 20
        )(place, own, panel_rows)
        summed = spread(partial, "row", N_ROW).reshape(N_ROW, SHARE, 2 * NB).sum(0)
        gram = spread(summed, "col", N_COL)
    with jax.named_scope("factor"):
        band, linv, reflector = call(
            factor_kernel,
            [(NB, NB)] * 3,
            scratch=[(NB, NB)] * 2,
            n_in=1,
            name="factor",
            flops=10**10,
            moved=80 << 20,
        )(gram)
    with jax.named_scope("symmetric"):
        rows, cols, row_terms, mirror, vectors = call(
            symmetric_kernel,
            [
                (NB, TR * NB),
                (NB, TC * NB),
                (NB, TR * NB),
                (NB, TC * NB),
                (SHARE * TR * 2, LANES),
            ],
            n_scalars=1,
            n_in=4,
            name="symmetric",
            moved=8 << 20,
        )(place, linv, panel_rows, panel_cols, stored)
    with jax.named_scope("sums"):
        from_cols = (
            lax.all_to_all(mirror, "row", 0, 0, tiled=True).reshape(N_ROW, CHUNK, TC * NB).sum(0)
        )
        from_rows = (
            lax.all_to_all(row_terms, "col", 0, 0, tiled=True).reshape(N_COL, SHARE, TR * NB).sum(0)
        )
        even, odd = to_rows(from_cols[:SHARE], from_cols[SHARE:], col_index)
        tiles = from_rows.reshape(SHARE, TR, NB)
        early, late = to_cols(
            jnp.concatenate([tiles[:, 0], tiles[:, 2]], axis=1),
            jnp.concatenate([tiles[:, 1], tiles[:, 3]], axis=1),
            col_index,
        )
        share = from_rows + jnp.concatenate(
            [even[:, :NB], odd[:, :NB], even[:, NB:], odd[:, NB:]], axis=1
        )
        sums = spread(share, "col", N_COL)
    with jax.named_scope("curvature"):
        (curv,) = call(curvature_kernel, [(SHARE, NB)], n_in=2, name="curvature", moved=1 << 20)(
            share, rows
        )
    with jax.named_scope("sums_cols"):
        chunk = from_cols + jnp.concatenate([early, late], axis=0)
        payload = jnp.concatenate([chunk[:, :NB], chunk[:, NB:], curv], axis=0)
        parts = spread(payload, "row", N_ROW)
    with jax.named_scope("curvature_all"):
        span = 2 * CHUNK + SHARE
        curv = parts.reshape(N_ROW, span, NB)[:, 2 * CHUNK :].sum(0)
        curvature = spread(curv, "col", N_COL)
    with jax.named_scope("update"):
        (updated,) = call(
            update_kernel,
            [(TR * NB * TC * 2, LANES)],
            n_scalars=1,
            n_in=7,
            name="update",
            moved=8 << 20,
        )(place, stored, rows, cols, sums, parts, curvature, reflector)
    return (updated.reshape(matrix.shape), vectors.reshape(panel_t.shape), band, reflector)


def solution(mesh):
    placed = (P(None, "row", None, None, "col", None), P("col", None, "row", None))
    return jax.shard_map(
        body,
        mesh=mesh,
        in_specs=placed,
        out_specs=(P(None, "row", None, None, "col", None), P("col", None, "row", None), P(), P()),
        check_vma=False,
    )
```

time: 958 us -> 315 us (0.33); the launches traced: 943 us -> 313 us
  waiting for transfers between devices: 714 us -> 72.6 us
  other arithmetic: 133 us -> 3.48 us
  blocking collectives: 0 us -> 95.7 us
  starting transfers between devices: 0.6 us -> 93.8 us
  Pallas kernels: 0 us -> 37.2 us
  matrix products: 36.4 us -> 0 us
  local copies, waits for them, and re-layouts: 40.5 us -> 9.79 us
  between operations: 17.4 us -> 0.92 us
    psum x5 -> x0, waiting for transfers between devices: 659 us -> none  [the longest x3 395 us: from_root(): return lax.psum(kept, axis)]
    another operation x18 -> x1, other arithmetic: 111 us -> 0.08 us  [body(): place = jnp.stack([row_index, col_index]).astype(jnp.int32)]
    all_to_all x0 -> x3, blocking collectives: none -> 95.7 us  [the longest x2 69.7 us: spread(): return lax.all_to_all(jnp.tile(value, (count, 1)), axis, 0, 0, tiled=True)]
    all_to_all x0 -> x6, starting transfers between devices: none -> 68.5 us  [the longest x5 59.1 us: spread(): return lax.all_to_all(jnp.tile(value, (count, 1)), axis, 0, 0, tiled=True)]
    all_gather x1 -> x0, waiting for transfers between devices: 55.6 us -> none  [body(): gathered = lax.all_gather(panel_t, 'col', axis=0, tiled=True)]
    all_to_all x0 -> x6, waiting for transfers between devices: none -> 47.5 us  [the longest x5 47.5 us: spread(): return lax.all_to_all(jnp.tile(value, (count, 1)), axis, 0, 0, tiled=True)]
    pallas_call x0 -> x5, Pallas kernels: none -> 37.2 us  [the longest x1 24 us: body(): call(factor_kernel, [(NB, NB)] * 3, scratch=[(NB, NB)] * 2, n_in=1, name=...]
    dot_general x11 -> x0, matrix products: 26.1 us -> none  [the longest x6 10.3 us: matmul(): return jnp.dot(multiplier, multiplicand, precision=lax.Precision.HIGHEST)]
  transfers between devices with their start and end apart: 6 -> 12, of which waited for: 6 -> 6; matrix products, arithmetic and copies ran while one was open for 2% -> 1% of each run, Pallas kernels for 0% -> 8%
where the time goes in v1:
time: 315 us; the launch traced here: 313 us
  blocking collectives  95.7 us (30%)
  starting transfers between devices  93.8 us (30%)
  waiting for transfers between devices  72.6 us (23%)
  Pallas kernels  37.2 us (12%)
  local copies, waits for them, and re-layouts  9.79 us (3%)
  other arithmetic  3.48 us (1%)
    all_to_all x2, blocking collectives, spread(): return lax.all_to_all(jnp.tile(value, (count, 1)), axis, 0, 0, tiled=True)  69.7 us
    all_to_all x5, starting transfers between devices, spread(): return lax.all_to_all(jnp.tile(value, (count, 1)), axis, 0, 0, tiled=True)  59.1 us
    all_to_all x5, waiting for transfers between devices, spread(): return lax.all_to_all(jnp.tile(value, (count, 1)), axis, 0, 0, tiled=True)  47.5 us
    all_to_all x1, blocking collectives, body(): lax.all_to_all(row_terms, 'col', 0, 0, tiled=True)  25.9 us
    pallas_call x1, Pallas kernels, body(): call(factor_kernel, [(NB, NB)] * 3, scratch=[(NB, NB)] * 2, n_in=1, name=...  24 us
    ppermute x2, waiting for transfers between devices, to_cols(): first = lax.ppermute(jnp.where(flip, odd, even), ('row', 'col'), one)  21.8 us
    ppermute x2, starting transfers between devices, to_cols(): first = lax.ppermute(jnp.where(flip, odd, even), ('row', 'col'), one)  12.3 us
    all_to_all x1, starting transfers between devices, body(): lax.all_to_all(mirror, 'row', 0, 0, tiled=True)  9.46 us
  transfers between devices with their start and end apart: 12, of which 6 were waited for; matrix products, arithmetic and copies ran while one was open for 1% of the time, Pallas kernels for 8%

profile of v1, /device:TPU:1, one launch (start us, length us, event | category | flops | bytes accessed | tf_op | source)
XLA Modules:
  0.0 313.4 jit_solution(6645636837129785640)
XLA Ops:
  0.6 0.0 copy-start.9
  0.6 1.9 tile.14
  2.5 10.5 %all-to-all-start = ((f32[32,64,128]{2,1,0:T(8,128)}), f32[32,64,128]{2,1,0:T(8,128)S(1)}, u32[]{:S(2)}, u32[]{:S(2)}) async-start(f32[32,64,128]{2,1,0:T(8,128)} %tile.14), calls=%async_computation | async-start | bytes 2097152 | tf_op jit(solution)/shard_map/panel_rows/all_to_all | solution.py:254
  13.0 0.1 pad_add_fusion.place
  13.1 17.2 %all-to-all-done = f32[32,64,128]{2,1,0:T(8,128)S(1)} async-done(((f32[32,64,128]{2,1,0:T(8,128)}), f32[32,64,128]{2,1,0:T(8,128)S(1)}, u32[]{:S(2)}, u32[]{:S(2)}) %all-to-all-start) | async-done | bytes 1048608 | tf_op jit(solution)/shard_map/panel_rows/all_to_all | solution.py:254
  30.3 0.0 copy-done.9
  30.3 1.5 gram.1
  31.8 0.7 tile.15
  32.5 12.9 %all-to-all-start.1 = ((f32[16,8,512]{2,1,0:T(8,128)}), f32[16,8,512]{2,1,0:T(8,128)S(1)}, u32[]{:S(2)}, u32[]{:S(2)}) async-start(f32[16,8,512]{2,1,0:T(8,128)} %tile.15), calls=%async_computation.1 | async-start | bytes 524288 | tf_op jit(solution)/shard_map/gram/all_to_all | solution.py:254
  45.5 13.9 %all-to-all-done.1 = f32[16,8,512]{2,1,0:T(8,128)S(1)} async-done(((f32[16,8,512]{2,1,0:T(8,128)}), f32[16,8,512]{2,1,0:T(8,128)S(1)}, u32[]{:S(2)}, u32[]{:S(2)}) %all-to-all-start.1) | async-done | bytes 262176 | tf_op jit(solution)/shard_map/gram/all_to_all | solution.py:254
  59.4 0.9 tile.16
  60.2 8.8 %all-to-all-start.2 = ((f32[32,8,512]{2,1,0:T(8,128)}), f32[32,8,512]{2,1,0:T(8,128)S(1)}, u32[]{:S(2)}, u32[]{:S(2)}) async-start(f32[32,8,512]{2,1,0:T(8,128)} %tile.16), calls=%async_computation.2 | async-start | bytes 1048576 | tf_op jit(solution)/shard_map/gram/all_to_all | solution.py:254
  69.1 2.3 collective-permute-start.1
  71.4 9.4 %collective-permute-start = (f32[32,128]{1,0:T(8,128)S(1)}, f32[32,128]{1,0:T(8,128)S(1)}, u32[]{:S(2)}, u32[]{:S(2)}) collective-permute-start(f32[32,128]{1,0:T(8,128)S(1)} %bitcast.40), channel_id=1, source_target_pairs={{0,0},{1,16},{2,32},{3,48},{4,64},{5,80},{6,96},{7,112},{8,128},{9... | collective-permute-start | bytes 49160 | tf_op jit(solution)/shard_map/panel_cols/ppermute | solution.py:271
  80.7 0.0 collective-permute-done.1
  80.7 0.8 collective-permute-done
  81.6 0.0 all-to-all-done.2
  81.6 0.0 copy-start.6
  81.6 0.9 tile.17
  82.5 19.2 %all-to-all-start.3 = ((f32[16,64,128]{2,1,0:T(8,128)}), f32[16,64,128]{2,1,0:T(8,128)}, u32[]{:S(2)}, u32[]{:S(2)}) async-start(f32[16,64,128]{2,1,0:T(8,128)} %tile.17), calls=%async_computation.3 | async-start | bytes 1048576 | tf_op jit(solution)/shard_map/panel_cols/all_to_all | solution.py:254
  101.8 0.0 copy-done.6
  101.8 0.0 copy-start.7
  101.8 1.0 copy-done.7
  102.8 0.0 copy-start
  102.8 24.0 %factor.1 = (f32[256,256]{1,0:T(8,128)}, f32[256,256]{1,0:T(8,128)S(1)}, f32[256,256]{1,0:T(8,128)}) custom-call(f32[256,512]{1,0:T(8,128)S(1)} %bitcast.33), custom_call_target="tpu_custom_call" | custom-call | flops 10000000000 | bytes 83886080 | tf_op jit(solution)/shard_map/factor/factor/pallas_call | solution.py:306
  126.8 0.0 all-to-all-done.3
  126.8 0.0 copy-done
  126.8 4.3 %symmetric.1 = (f32[256,1024]{1,0:T(8,128)S(1)}, f32[256,512]{1,0:T(8,128)S(1)}, f32[256,1024]{1,0:T(8,128)S(1)}, f32[256,512]{1,0:T(8,128)S(1)}, f32[64,128]{1,0:T(8,128)}) custom-call(s32[2]{0:T(128)S(1)} %pad_add_fusion.place, f32[256,256]{1,0:T(8,128)S(1)} %get-tuple-element.12.linv_ref, f32[2048,128]{1,0:T(8,128)S(1)} %bitcast.27, ...), custom_call_target="tpu_custom_call" | custom-call | bytes 8388608 | tf_op jit(solution)/shard_map/symmetric/symmetric/pallas_call | solution.py:316
  131.1 0.0 copy-start.1
  131.1 1.0 copy-done.1
  132.1 0.0 copy-start.4
  132.1 0.0 copy-start.8
  132.1 25.9 %all_to_all.72 = f32[32,8,1024]{2,1,0:T(8,128)} all-to-all(f32[32,8,1024]{2,1,0:T(8,128)S(1)} %bitcast.32), channel_id=1, replica_groups=mesh['row'=16,'col'=32] {'col'}, dimensions={0} | all-to-all | bytes 2097152 | tf_op jit(solution)/shard_map/sums/all_to_all | solution.py:335
  158.0 0.0 copy-done.4
  158.0 0.0 copy-start.2
  158.0 0.0 copy-done.8
  158.0 9.5 %all-to-all-start.5 = ((f32[16,16,512]{2,1,0:T(8,128)}), f32[16,16,512]{2,1,0:T(8,128)}, u32[]{:S(2)}, u32[]{:S(2)}) async-start(f32[16,16,512]{2,1,0:T(8,128)} %bitcast.34), calls=%async_computation.5 | async-start | bytes 1048576 | tf_op jit(solution)/shard_map/sums/all_to_all | solution.py:332
  167.5 1.3 reduce_sum.37
  168.8 3.0 collective-permute-start.4
  171.8 1.9 collective-permute-start.5
  173.7 21.0 %collective-permute-done.4 = f32[8,512]{1,0:T(8,128)S(1)} collective-permute-done((f32[8,512]{1,0:T(8,128)S(1)}, f32[8,512]{1,0:T(8,128)S(1)}, u32[]{:S(2)}, u32[]{:S(2)}) %collective-permute-start.4) | collective-permute-done | bytes 16416 | tf_op jit(solution)/shard_map/sums/ppermute | solution.py:271
  194.7 0.0 collective-permute-done.5
  194.7 0.0 all-to-all-done.5
  194.7 1.1 reduce_sum.38
  195.8 1.9 collective-permute-start.2
  197.8 6.8 %collective-permute-start.3 = (f32[8,512]{1,0:T(8,128)S(1)}, f32[8,512]{1,0:T(8,128)S(1)}, u32[]{:S(2)}, u32[]{:S(2)}) collective-permute-start(f32[8,512]{1,0:T(8,128)S(1)} %get-tuple-element.41), channel_id=1, source_target_pairs={{0,0},{16,1},{32,2},{48,3},{64,4},{80,5},{96,6},{112,7},{128,8},{1... | collective-permute-start | bytes 49160 | tf_op jit(solution)/shard_map/sums/ppermute | solution.py:279
  204.6 0.0 collective-permute-done.2
  204.6 3.3 %collective-permute-done.3 = f32[8,512]{1,0:T(8,128)S(1)} collective-permute-done((f32[8,512]{1,0:T(8,128)S(1)}, f32[8,512]{1,0:T(8,128)S(1)}, u32[]{:S(2)}, u32[]{:S(2)}) %collective-permute-start.3) | collective-permute-done | bytes 16416 | tf_op jit(solution)/shard_map/sums/ppermute | solution.py:279
  207.9 0.0 copy-done.2
  207.9 0.5 curvature.1
  208.4 0.1 tile.19
  208.5 57.2 %all_to_all.73 = f32[16,40,256]{2,1,0:T(8,128)} all-to-all(f32[16,40,256]{2,1,0:T(8,128)S(1)} %tile.19), channel_id=1, replica_groups=mesh['row'=16,'col'=32] {'row'}, dimensions={0} | all-to-all | bytes 1310720 | tf_op jit(solution)/shard_map/sums_cols/all_to_all | solution.py:254
  265.7 0.0 copy-start.10
  265.7 1.1 tile.18
  266.8 7.6 %all-to-all-start.6 = ((f32[32,8,1024]{2,1,0:T(8,128)}), f32[32,8,1024]{2,1,0:T(8,128)}, u32[]{:S(2)}, u32[]{:S(2)}) async-start(f32[32,8,1024]{2,1,0:T(8,128)} %tile.18), calls=%async_computation.6 | async-start | bytes 2097152 | tf_op jit(solution)/shard_map/sums/all_to_all | solution.py:254
  274.4 0.9 slice_reduce_fusion
  275.3 16.4 %all-to-all-done.6 = f32[32,8,1024]{2,1,0:T(8,128)} async-done(((f32[32,8,1024]{2,1,0:T(8,128)}), f32[32,8,1024]{2,1,0:T(8,128)}, u32[]{:S(2)}, u32[]{:S(2)}) %all-to-all-start.6) | async-done | bytes 1048608 | tf_op jit(solution)/shard_map/sums/all_to_all | solution.py:254
  291.7 12.5 %all_to_all.74 = f32[32,8,256]{2,1,0:T(8,128)S(1)} all-to-all(f32[32,8,256]{2,1,0:T(8,128)S(1)} %tile.20), channel_id=1, replica_groups=mesh['row'=16,'col'=32] {'col'}, dimensions={0} | all-to-all | bytes 524288 | tf_op jit(solution)/shard_map/curvature_all/all_to_all | solution.py:254
  304.3 0.0 copy-done.10
  304.3 0.0 copy-start.3
  304.3 1.1 copy-done.3
  305.4 0.0 copy-start.5
  305.4 1.0 copy-done.5
  306.4 7.0 %update.1 = f32[4096,128]{1,0:T(8,128)} custom-call(s32[2]{0:T(128)S(1)} %pad_add_fusion.place, f32[4096,128]{1,0:T(8,128)S(1)} %bitcast.29, f32[256,1024]{1,0:T(8,128)S(1)} %copy-done.2, f32[256,512]{1,0:T(8,128)S(1)} %copy-done.5, f32[256,1024]{1,0:T(8,128)} %bitcast.12.sums_ref, f32[640,256]{1,0:T(8,128)S(1)} %bitcast.30, f32[256,256]{1,0:T(8,128)S(1)} %bitcast.31, ...), custom_call_target="tpu_custom_call" | custom-call | bytes 8388608 | tf_op jit(solution)/shard_map/update/update/pallas_call | solution.py:361
  (15 shorter events, 0.1 us)
Async XLA Ops:
  0.6 29.7 %copy-start.9 = (f32[8,4,1,256]{3,2,1,0:T(1,128)S(1)}, f32[8,4,1,256]{3,2,1,0:T(1,128)}, u32[]{:S(2)}) copy-start(f32[8,4,1,256]{3,2,1,0:T(1,128)} %param.3) | copy-start | bytes 98308
  2.5 27.8 %all-to-all-start = ((f32[32,64,128]{2,1,0:T(8,128)}), f32[32,64,128]{2,1,0:T(8,128)S(1)}, u32[]{:S(2)}, u32[]{:S(2)}) async-start(f32[32,64,128]{2,1,0:T(8,128)} %tile.14), calls=%async_computation | async-start | bytes 2097152 | tf_op jit(solution)/shard_map/panel_rows/all_to_all | solution.py:254
  32.5 26.8 %all-to-all-start.1 = ((f32[16,8,512]{2,1,0:T(8,128)}), f32[16,8,512]{2,1,0:T(8,128)S(1)}, u32[]{:S(2)}, u32[]{:S(2)}) async-start(f32[16,8,512]{2,1,0:T(8,128)} %tile.15), calls=%async_computation.1 | async-start | bytes 524288 | tf_op jit(solution)/shard_map/gram/all_to_all | solution.py:254
  60.2 21.3 %all-to-all-start.2 = ((f32[32,8,512]{2,1,0:T(8,128)}), f32[32,8,512]{2,1,0:T(8,128)S(1)}, u32[]{:S(2)}, u32[]{:S(2)}) async-start(f32[32,8,512]{2,1,0:T(8,128)} %tile.16), calls=%async_computation.2 | async-start | bytes 1048576 | tf_op jit(solution)/shard_map/gram/all_to_all | solution.py:254
  69.1 11.6 %collective-permute-start.1 = (f32[32,128]{1,0:T(8,128)S(1)}, f32[32,128]{1,0:T(8,128)S(1)}, u32[]{:S(2)}, u32[]{:S(2)}) collective-permute-start(f32[32,128]{1,0:T(8,128)S(1)} %bitcast.41), channel_id=1, source_target_pairs={{0,16},{1,0},{2,48},{3,32},{4,80},{5,64},{6,112},{7,96},{8,144},{9... | collective-permute-start | bytes 49160 | tf_op jit(solution)/shard_map/panel_cols/ppermute | solution.py:272
  71.4 10.2 %collective-permute-start = (f32[32,128]{1,0:T(8,128)S(1)}, f32[32,128]{1,0:T(8,128)S(1)}, u32[]{:S(2)}, u32[]{:S(2)}) collective-permute-start(f32[32,128]{1,0:T(8,128)S(1)} %bitcast.40), channel_id=1, source_target_pairs={{0,0},{1,16},{2,32},{3,48},{4,64},{5,80},{6,96},{7,112},{8,128},{9... | collective-permute-start | bytes 49160 | tf_op jit(solution)/shard_map/panel_cols/ppermute | solution.py:271
  81.6 20.2 %copy-start.6 = (f32[32,8,512]{2,1,0:T(8,128)}, f32[32,8,512]{2,1,0:T(8,128)S(1)}, u32[]{:S(2)}) copy-start(f32[32,8,512]{2,1,0:T(8,128)S(1)} %all-to-all-done.2) | copy-start | bytes 1572868
  82.5 44.3 %all-to-all-start.3 = ((f32[16,64,128]{2,1,0:T(8,128)}), f32[16,64,128]{2,1,0:T(8,128)}, u32[]{:S(2)}, u32[]{:S(2)}) async-start(f32[16,64,128]{2,1,0:T(8,128)} %tile.17), calls=%async_computation.3 | async-start | bytes 1048576 | tf_op jit(solution)/shard_map/panel_cols/all_to_all | solution.py:254
  101.8 1.0 copy-start.7
  102.8 24.0 %copy-start = (f32[4,1,256,2,1,256]{5,4,3,2,1,0:T(1,128)S(1)}, f32[4,1,256,2,1,256]{5,4,3,2,1,0:T(1,128)}, u32[]{:S(2)}) copy-start(f32[4,1,256,2,1,256]{5,4,3,2,1,0:T(1,128)} %param.2) | copy-start | bytes 6291460
  131.1 1.0 copy-start.1
  132.1 25.9 %copy-start.4 = (f32[256,512]{1,0:T(8,128)}, f32[256,512]{1,0:T(8,128)S(1)}, u32[]{:S(2)}) copy-start(f32[256,512]{1,0:T(8,128)S(1)} %get-tuple-element.14.cols_ref) | copy-start | bytes 1572868
  132.1 26.0 %copy-start.8 = (f32[256,512]{1,0:T(8,128)}, f32[256,512]{1,0:T(8,128)S(1)}, u32[]{:S(2)}) copy-start(f32[256,512]{1,0:T(8,128)S(1)} %get-tuple-element.16) | copy-start | bytes 1572868
  158.0 49.9 %copy-start.2 = (f32[256,1024]{1,0:T(8,128)S(1)}, f32[256,1024]{1,0:T(8,128)}, u32[]{:S(2)}) copy-start(f32[256,1024]{1,0:T(8,128)} %copy-done.1) | copy-start | bytes 3145732
  158.0 36.7 %all-to-all-start.5 = ((f32[16,16,512]{2,1,0:T(8,128)}), f32[16,16,512]{2,1,0:T(8,128)}, u32[]{:S(2)}, u32[]{:S(2)}) async-start(f32[16,16,512]{2,1,0:T(8,128)} %bitcast.34), calls=%async_computation.5 | async-start | bytes 1048576 | tf_op jit(solution)/shard_map/sums/all_to_all | solution.py:332
  168.8 25.9 %collective-permute-start.4 = (f32[8,512]{1,0:T(8,128)S(1)}, f32[8,512]{1,0:T(8,128)S(1)}, u32[]{:S(2)}, u32[]{:S(2)}) collective-permute-start(f32[8,512]{1,0:T(8,128)S(1)} %get-tuple-element.32), channel_id=1, source_target_pairs={{0,0},{1,16},{2,32},{3,48},{4,64},{5,80},{6,96},{7,112},{8,128},{9... | collective-permute-start | bytes 49160 | tf_op jit(solution)/shard_map/sums/ppermute | solution.py:271
  171.8 22.9 %collective-permute-start.5 = (f32[8,512]{1,0:T(8,128)S(1)}, f32[8,512]{1,0:T(8,128)S(1)}, u32[]{:S(2)}, u32[]{:S(2)}) collective-permute-start(f32[8,512]{1,0:T(8,128)S(1)} %get-tuple-element.33), channel_id=1, source_target_pairs={{0,16},{1,0},{2,48},{3,32},{4,80},{5,64},{6,112},{7,96},{8,144},{9... | collective-permute-start | bytes 49160 | tf_op jit(solution)/shard_map/sums/ppermute | solution.py:272
  195.8 8.8 %collective-permute-start.2 = (f32[8,512]{1,0:T(8,128)S(1)}, f32[8,512]{1,0:T(8,128)S(1)}, u32[]{:S(2)}, u32[]{:S(2)}) collective-permute-start(f32[8,512]{1,0:T(8,128)S(1)} %get-tuple-element.40), channel_id=1, source_target_pairs={{16,0},{0,1},{48,2},{32,3},{80,4},{64,5},{112,6},{96,7},{144,8},{1... | collective-permute-start | bytes 49160 | tf_op jit(solution)/shard_map/sums/ppermute | solution.py:280
  197.8 10.1 %collective-permute-start.3 = (f32[8,512]{1,0:T(8,128)S(1)}, f32[8,512]{1,0:T(8,128)S(1)}, u32[]{:S(2)}, u32[]{:S(2)}) collective-permute-start(f32[8,512]{1,0:T(8,128)S(1)} %get-tuple-element.41), channel_id=1, source_target_pairs={{0,0},{16,1},{32,2},{48,3},{64,4},{80,5},{96,6},{112,7},{128,8},{1... | collective-permute-start | bytes 49160 | tf_op jit(solution)/shard_map/sums/ppermute | solution.py:279
  265.7 38.6 %copy-start.10 = (f32[256,256]{1,0:T(8,128)S(1)}, f32[256,256]{1,0:T(8,128)}, u32[]{:S(2)}) copy-start(f32[256,256]{1,0:T(8,128)} %get-tuple-element.27.refl_ref) | copy-start | bytes 786436
  266.8 25.0 %all-to-all-start.6 = ((f32[32,8,1024]{2,1,0:T(8,128)}), f32[32,8,1024]{2,1,0:T(8,128)}, u32[]{:S(2)}, u32[]{:S(2)}) async-start(f32[32,8,1024]{2,1,0:T(8,128)} %tile.18), calls=%async_computation.6 | async-start | bytes 2097152 | tf_op jit(solution)/shard_map/sums/all_to_all | solution.py:254
  304.3 1.1 copy-start.3
  305.4 1.0 copy-start.5

commit v2 on v1

v2 whole, which is shorter than its diff:
```python
import jax
import jax.numpy as jnp
from jax import lax
from jax.experimental import pallas as pl
from jax.experimental.pallas import tpu as pltpu
from jax.sharding import PartitionSpec as P

NB = 256
TR = 4
TC = 2
N_ROW = 16
N_COL = 32
LANES = 128
BS = 16
SHARE = NB // N_COL
CHUNK = NB // N_ROW
F32 = jnp.float32
VMEM = pl.BlockSpec(memory_space=pltpu.VMEM)
SMEM = pl.BlockSpec(memory_space=pltpu.SMEM)


def call(kernel, outs, scratch=(), n_scalars=0, n_in=1, name=None, flops=0, moved=0):
    return pl.pallas_call(
        kernel,
        out_shape=[jax.ShapeDtypeStruct(shape, F32) for shape in outs],
        in_specs=[SMEM] * n_scalars + [VMEM] * n_in,
        out_specs=[VMEM] * len(outs),
        scratch_shapes=[pltpu.VMEM(shape, F32) for shape in scratch],
        compiler_params=pltpu.CompilerParams(vmem_limit_bytes=60 * 2**20),
        cost_estimate=pl.CostEstimate(flops=flops, bytes_accessed=moved, transcendentals=0),
        name=name,
    )


def exact(a, b, ca=1, cb=0):
    return lax.dot_general(
        a,
        b,
        (((ca,), (cb,)), ((), ())),
        precision=lax.Precision.HIGHEST,
        preferred_element_type=F32,
    )


def split(a):
    high = a.astype(jnp.bfloat16)
    return high, (a - high.astype(F32)).astype(jnp.bfloat16)


def product(a, b, ca=1, cb=0):
    def one(x, y):
        return lax.dot_general(x, y, (((ca,), (cb,)), ((), ())), preferred_element_type=F32)

    return one(a[0], b[0]) + (one(a[0], b[1]) + one(a[1], b[0]))


def linear_tile(ref, t):
    return jnp.concatenate([ref[pl.ds(t * 2 + half, NB, TR * 2), :] for half in range(2)], axis=1)


SPAN = CHUNK * TC * 2 + 4 * SHARE


def gathered_tile(ref, u):
    return jnp.concatenate(
        [
            jnp.concatenate(
                [ref[pl.ds(k * SPAN + u * 2 + half, CHUNK, TC * 2), :] for k in range(N_ROW)], axis=0
            )
            for half in range(2)
        ],
        axis=1,
    )


def matrix_rows(t, u, half):
    return pl.ds((t * NB) * TC * 2 + u * 2 + half, NB, TC * 2)


def matrix_tile(ref, t, u):
    return jnp.concatenate([ref[matrix_rows(t, u, half), :] for half in range(2)], axis=1)


def gram_kernel(place, own_ref, panel_ref, early_ref, late_ref, out_ref):
    total = jnp.zeros((SHARE, NB), F32)
    for piece in range(TR * 2):
        total += exact(
            own_ref[pl.ds(piece, SHARE, TR * 2), :], panel_ref[pl.ds(piece, NB, TR * 2), :], 1, 1
        )
    half_chunk = SHARE * TC * 2
    out_ref[:half_chunk, :] = early_ref[...]
    out_ref[half_chunk : 2 * half_chunk, :] = late_ref[...]
    for half in range(2):
        at = 2 * half_chunk + half * SHARE
        out_ref[pl.ds(at, SHARE), :] = total[:, half * LANES : (half + 1) * LANES]
        top = own_ref[pl.ds(half, SHARE, TR * 2), :]
        out_ref[pl.ds(at + 2 * SHARE, SHARE), :] = jnp.where(place[0] == 0, top, 0.0)


def gathered_columns(g_ref, quarters):
    return jnp.concatenate(
        [
            jnp.concatenate(
                [g_ref[pl.ds((4 * k + q) * SHARE, SHARE), :] for k in range(N_COL)], axis=0
            )
            for q in quarters
        ],
        axis=1,
    )


def factor_kernel(g_ref, band_ref, linv_ref, refl_ref, a_ref, u_ref):
    n = NB
    steps = n // BS
    rows = lax.broadcasted_iota(jnp.int32, (BS, LANES), 0)
    lanes = lax.broadcasted_iota(jnp.int32, (BS, LANES), 1)
    eye = (rows == lanes).astype(F32)
    wide = lax.broadcasted_iota(jnp.int32, (BS, n), 1)
    full_row = lax.broadcasted_iota(jnp.int32, (n, n), 0)
    full_col = lax.broadcasted_iota(jnp.int32, (n, n), 1)
    a_ref[...] = gathered_columns(g_ref, (0, 1))

    def advance(base, update, row):
        a_ref[: n - BS, :] = pltpu.roll(base[BS:] - update[BS:], n - BS, 1)
        a_ref[n - BS :, :] = pltpu.roll(row, n - BS, 1)

    def chol_step(step, carry):
        left = n - BS * step
        a = a_ref[...]
        first, second = a[:BS, :LANES], a[:BS, LANES:]
        heads = [jnp.broadcast_to(first[:, k : k + 1], (BS, LANES)) for k in range(BS)]
        inner = eye
        pivots = jnp.ones((BS, LANES), F32)
        for j in range(BS):
            pivot = heads[j][j : j + 1]
            factor = jnp.where(rows > j, heads[j], 0.0) * (1.0 / pivot)
            pivots = jnp.where(rows == j, pivot, pivots)
            for k in range(j + 1, BS):
                heads[k] = heads[k] - factor * heads[k][j : j + 1]
            first = first - factor * first[j : j + 1]
            second = second - factor * second[j : j + 1]
            inner = inner - factor * inner[j : j + 1]
        scale = lax.rsqrt(pivots)
        scale = scale * (1.5 - 0.5 * pivots * scale * scale)
        first, second, inner = first * scale, second * scale, inner * scale
        upper = jnp.concatenate([jnp.where(lanes >= rows, first, 0.0), second], axis=1)
        upper = jnp.where(wide < left, upper, 0.0)
        u_ref[pl.ds(pl.multiple_of(step * BS, BS), BS), :] = pltpu.roll(upper, step * BS, 1)
        row = jnp.concatenate([jnp.where(lanes < BS, inner, first), second], axis=1)
        update = exact(jnp.where(wide >= BS, upper, 0.0), row, 0, 0)
        advance(jnp.where((full_col < BS) & (full_row < left), 0.0, a), update, row)
        return carry

    lax.fori_loop(0, steps, chol_step, 0)
    linv = jnp.where(full_col <= full_row, a_ref[...], 0.0)
    linv_ref[...] = linv
    band_ref[...] = -u_ref[...]
    a_ref[...] = exact(linv, gathered_columns(g_ref, (2, 3))) + (full_row == full_col).astype(F32)

    def inverse_step(step, carry):
        a = a_ref[...]
        first, second = a[:BS, :LANES], a[:BS, LANES:]
        heads = [jnp.broadcast_to(first[:, k : k + 1], (BS, LANES)) for k in range(BS)]
        first = jnp.where(lanes < BS, eye, first)
        for j in range(BS):
            head = heads[j]
            inverse = 1.0 / head[j : j + 1]

            def put(value):
                scaled = value[j : j + 1] * inverse
                return jnp.where(rows == j, scaled, value - head * scaled)

            for k in range(j + 1, BS):
                heads[k] = put(heads[k])
            first, second = put(first), put(second)
        row = jnp.concatenate([first, second], axis=1)
        update = exact(a[:, :BS], row)
        advance(jnp.where(full_col < BS, 0.0, a), update, row)
        return carry

    lax.fori_loop(0, steps, inverse_step, 0)
    refl_ref[...] = a_ref[...]


def tile_place(place, t, u):
    return t * N_ROW + place[0], u * N_COL + place[1]


def ordering():
    r = lax.broadcasted_iota(jnp.int32, (NB, NB), 0)
    c = lax.broadcasted_iota(jnp.int32, (NB, NB), 1)
    return r, c


def mirror_kernel(place, panel_ref, matrix_ref, out_ref):
    out_ref[...] = jnp.zeros((NB, TC * NB), F32)
    for t in range(TR):
        rows = split(linear_tile(panel_ref, t))
        for u in range(TC):
            here = pl.ds(u * NB, NB)
            i, j = tile_place(place, t, u)

            @pl.when(i > j)
            def _():
                out_ref[:, here] += product(rows, split(matrix_tile(matrix_ref, t, u)))

            @pl.when(i == j)
            def _():
                r, c = ordering()
                tile = jnp.where(r > c, matrix_tile(matrix_ref, t, u), 0.0)
                out_ref[:, here] += product(rows, split(tile))


def symmetric_kernel(place, band_ref, panel_ref, matrix_ref, out_ref):
    factor = -jnp.transpose(band_ref[...])
    out_ref[...] = jnp.zeros((NB, TR * NB), F32)
    cols = []
    for u in range(TC):
        value = gathered_tile(panel_ref, u)
        if u == 0:
            value = value + jnp.where(place[1] == 0, factor, 0.0)
        cols.append(split(value))
    for t in range(TR):
        here = pl.ds(t * NB, NB)
        for u in range(TC):
            i, j = tile_place(place, t, u)

            @pl.when(i > j)
            def _():
                out_ref[:, here] += product(cols[u], split(matrix_tile(matrix_ref, t, u)), 1, 1)

            @pl.when(i == j)
            def _():
                r, c = ordering()
                tile = jnp.where(r >= c, matrix_tile(matrix_ref, t, u), 0.0)
                out_ref[:, here] += product(cols[u], split(tile), 1, 1)

        if t == 0:

            @pl.when((place[0] == 0) & (place[1] == 0))
            def _():
                r, c = ordering()
                tile = jnp.where(r > c, matrix_tile(matrix_ref, 0, 0), 0.0)
                out_ref[:, here] += product(split(factor), split(tile))


def vectors_kernel(
    place, linv_ref, refl_ref, panel_rows_ref, panel_cols_ref,
    rows_ref, cols_ref, both_ref, vectors_ref,
):
    linv = split(linv_ref[...])
    r, c = ordering()
    eye = (r == c).astype(F32)
    both_ref[...] = product(split(refl_ref[...]), linv, 0, 0)
    for u in range(TC):
        value = product(linv, split(gathered_tile(panel_cols_ref, u)))
        if u == 0:
            value = value + jnp.where(place[1] == 0, eye, 0.0)
        cols_ref[:, pl.ds(u * NB, NB)] = value
    for t in range(TR):
        value = product(linv, split(linear_tile(panel_rows_ref, t)))
        if t == 0:
            value = value + jnp.where(place[0] == 0, eye, 0.0)
        rows_ref[:, pl.ds(t * NB, NB)] = value
    mine = rows_ref[pl.ds(pl.multiple_of(place[1] * SHARE, SHARE), SHARE), :]
    for piece in range(TR * 2):
        vectors_ref[pl.ds(piece, SHARE, TR * 2), :] = mine[:, piece * LANES : (piece + 1) * LANES]


PART = (TR + 1) * SHARE
DEAL = (TC + 1 + TR) * SHARE


def share_kernel(recv_ref, even_ref, odd_ref, rows_ref, out_ref):
    total = recv_ref[pl.ds(0, SHARE), :]
    for k in range(1, N_COL):
        total = total + recv_ref[pl.ds(k * SHARE, SHARE), :]
    mirrored = [even_ref[:, :NB], odd_ref[:, :NB], even_ref[:, NB:], odd_ref[:, NB:]]
    total = total + jnp.concatenate(mirrored, axis=1)
    for t in range(TR):
        out_ref[pl.ds(t * SHARE, SHARE), :] = total[:, t * NB : (t + 1) * NB]
    out_ref[pl.ds(TR * SHARE, SHARE), :] = product(split(total), split(rows_ref[...]), 1, 1)


def deal_kernel(own_ref, part_ref, out_ref):
    curved = part_ref[pl.ds(TR * SHARE, SHARE), :]
    for r in range(1, N_ROW):
        curved = curved + part_ref[pl.ds(r * PART + TR * SHARE, SHARE), :]
    own = own_ref[: TR * SHARE, :]
    for c in range(N_COL):
        for u in range(TC):
            t = u * (N_COL // N_ROW) + c // N_ROW
            out_ref[pl.ds(c * DEAL + u * SHARE, SHARE), :] = part_ref[
                pl.ds((c % N_ROW) * PART + t * SHARE, SHARE), :
            ]
        out_ref[pl.ds(c * DEAL + TC * SHARE, SHARE), :] = curved
        out_ref[pl.ds(c * DEAL + (TC + 1) * SHARE, TR * SHARE), :] = own


def dealt(ref, slot):
    return jnp.concatenate(
        [ref[pl.ds(c * DEAL + slot * SHARE, SHARE), :] for c in range(N_COL)], axis=0
    )


def update_kernel(
    place, matrix_ref, rows_ref, cols_ref, dealt_ref, refl_ref, both_ref, out_ref
):
    both = split(both_ref[...])
    curved = split(product(both, split(dealt(dealt_ref, TC))))
    half_mixed = split(0.5 * product(curved, split(refl_ref[...])))
    sides = []
    for u in range(TC):
        vectors = split(cols_ref[:, pl.ds(u * NB, NB)])
        update = product(both, split(dealt(dealt_ref, u))) - product(half_mixed, vectors)
        sides.append((vectors, split(update)))
    for t in range(TR):
        here = pl.ds(t * NB, NB)
        vectors = split(rows_ref[:, here])
        update = split(product(both, split(dealt(dealt_ref, TC + 1 + t))) - product(half_mixed, vectors))
        for u in range(TC):
            i, j = tile_place(place, t, u)

            @pl.when(i >= j)
            def _():
                change = product(vectors, sides[u][1], 0, 0) + product(update, sides[u][0], 0, 0)
                value = matrix_tile(matrix_ref, t, u) - change
                r, c = ordering()
                value = jnp.where((r >= c) | (i > j), value, 0.0)
                for half in range(2):
                    out_ref[matrix_rows(t, u, half), :] = value[:, half * LANES : (half + 1) * LANES]

            @pl.when(i < j)
            def _():
                for half in range(2):
                    out_ref[matrix_rows(t, u, half), :] = jnp.zeros((NB, LANES), F32)


def spread(value, axis, count):
    return lax.all_to_all(jnp.tile(value, (count, 1)), axis, 0, 0, tiled=True)


def routes():
    one, two = [], []
    for r in range(N_ROW):
        for c in range(N_COL):
            near = (c // 2) * N_COL + r
            far = near + N_ROW
            one.append((r * N_COL + c, far if c % 2 else near))
            two.append((r * N_COL + c, near if c % 2 else far))
    return one, two


def to_cols(even, odd, col_index):
    one, two = routes()
    flip, low = col_index % 2 == 1, col_index < N_ROW
    first = lax.ppermute(jnp.where(flip, odd, even), ("row", "col"), one)
    second = lax.ppermute(jnp.where(flip, even, odd), ("row", "col"), two)
    return jnp.where(low, first, second), jnp.where(low, second, first)


def to_rows(early, late, col_index):
    one, two = ([(there, here) for here, there in route] for route in routes())
    flip, low = col_index % 2 == 1, col_index < N_ROW
    first = lax.ppermute(jnp.where(low, early, late), ("row", "col"), one)
    second = lax.ppermute(jnp.where(low, late, early), ("row", "col"), two)
    return jnp.where(flip, second, first), jnp.where(flip, first, second)


def body(matrix, panel_t):
    row_index = lax.axis_index("row")
    col_index = lax.axis_index("col")
    place = jnp.stack([row_index, col_index]).astype(jnp.int32)
    stored = matrix.reshape(TR * NB * TC * 2, LANES)
    own = panel_t.reshape(SHARE * TR * 2, LANES)

    with jax.named_scope("panel"):
        by_tile = own.reshape(SHARE, TR, 2, LANES)
        chunk = to_cols(
            by_tile[:, 0::2].reshape(-1, LANES), by_tile[:, 1::2].reshape(-1, LANES), col_index
        )
        panel_rows, chunk = lax.optimization_barrier((spread(own, "col", N_COL), chunk))
    with jax.named_scope("gram"):
        (payload,) = call(
            gram_kernel, [(SPAN, LANES)], n_scalars=1, n_in=4, name="gram", moved=1 << 20
        )(place, own, panel_rows, *chunk)
        panel_cols = lax.all_gather(payload, "row", tiled=True)
        summed = panel_cols.reshape(N_ROW, SPAN, LANES)[:, CHUNK * TC * 2 :].sum(0)
        gram = spread(summed, "col", N_COL)
    with jax.named_scope("mirror"):
        (mirror,) = call(
            mirror_kernel, [(NB, TC * NB)], n_scalars=1, n_in=2, name="mirror", moved=4 << 20
        )(place, panel_rows, stored)
        gram, mirror = lax.optimization_barrier((gram, mirror))
        from_cols = (
            lax.all_to_all(mirror, "row", 0, 0, tiled=True).reshape(N_ROW, CHUNK, TC * NB).sum(0)
        )
    with jax.named_scope("factor"):
        band, linv, reflector = call(
            factor_kernel,
            [(NB, NB)] * 3,
            scratch=[(NB, NB)] * 2,
            n_in=1,
            name="factor",
            flops=10**10,
            moved=80 << 20,
        )(gram)
    with jax.named_scope("symmetric"):
        (row_terms,) = call(
            symmetric_kernel, [(NB, TR * NB)], n_scalars=1, n_in=3, name="symmetric", moved=4 << 20
        )(place, band, panel_cols, stored)
    with jax.named_scope("vectors"):
        rows, cols, both, vectors = call(
            vectors_kernel,
            [(NB, TR * NB), (NB, TC * NB), (NB, NB), (SHARE * TR * 2, LANES)],
            n_scalars=1,
            n_in=4,
            name="vectors",
            moved=4 << 20,
        )(place, linv, reflector, panel_rows, panel_cols)
    with jax.named_scope("sums"):
        received = lax.all_to_all(row_terms, "col", 0, 0, tiled=True)
        even, odd = to_rows(from_cols[:SHARE], from_cols[SHARE:], col_index)
        (payload,) = call(share_kernel, [(PART, NB)], n_in=4, name="share", moved=2 << 20)(
            received, even, odd, rows
        )
        parts = lax.all_gather(payload, "row", tiled=True)
    with jax.named_scope("deal"):
        (deal,) = call(deal_kernel, [(N_COL * DEAL, NB)], n_in=2, name="deal", moved=3 << 20)(
            payload, parts
        )
        deal = lax.all_to_all(deal, "col", 0, 0, tiled=True)
    with jax.named_scope("update"):
        (updated,) = call(
            update_kernel,
            [(TR * NB * TC * 2, LANES)],
            n_scalars=1,
            n_in=6,
            name="update",
            moved=8 << 20,
        )(place, stored, rows, cols, deal, reflector, both)
    return (updated.reshape(matrix.shape), vectors.reshape(panel_t.shape), band, reflector)


def solution(mesh):
    placed = (P(None, "row", None, None, "col", None), P("col", None, "row", None))
    return jax.shard_map(
        body,
        mesh=mesh,
        in_specs=placed,
        out_specs=(P(None, "row", None, None, "col", None), P("col", None, "row", None), P(), P()),
        check_vma=False,
    )
```

time: 315 us -> 250 us (0.79)
  waiting for transfers between devices: 72.6 us -> 22.2 us
  starting transfers between devices: 93.8 us -> 55.5 us
  Pallas kernels: 37.2 us -> 53.5 us
  blocking collectives: 95.7 us -> 110 us
  local copies, waits for them, and re-layouts: 9.79 us -> 4.8 us
    all_gather x0 -> x2, blocking collectives: none -> 67 us  [the longest x1 33.9 us: body(): parts = lax.all_gather(payload, 'row', tiled=True)]
    all_to_all x3 -> x1, blocking collectives: 95.7 us -> 43 us  [body(): deal = lax.all_to_all(deal, 'col', 0, 0, tiled=True)]
    all_to_all x5 -> x2, waiting for transfers between devices: 47.5 us -> 14.1 us  [spread(): return lax.all_to_all(jnp.tile(value, (count, 1)), axis, 0, 0, tiled=True)]
    all_to_all x5 -> x2, starting transfers between devices: 59.1 us -> 28.7 us  [spread(): return lax.all_to_all(jnp.tile(value, (count, 1)), axis, 0, 0, tiled=True)]
    ppermute x2 -> x1, waiting for transfers between devices: 21.8 us -> 0.01 us  [to_cols(): first = lax.ppermute(jnp.where(flip, odd, even), ('row', 'col'), one)]
    pallas_call x4 -> x7, Pallas kernels: 13.2 us -> 28.5 us  [the longest x1 8.26 us: body(): call(update_kernel, [(TR * NB * TC * 2, LANES)], n_scalars=1, n_in=6, nam...]
    ppermute x2 -> x1, starting transfers between devices: 12.3 us -> 5.15 us  [to_cols(): first = lax.ppermute(jnp.where(flip, odd, even), ('row', 'col'), one)]
    all_to_all x0 -> x1, starting transfers between devices: none -> 5.2 us  [body(): received = lax.all_to_all(row_terms, 'col', 0, 0, tiled=True)]
  transfers between devices with their start and end apart: 12 -> 8, of which waited for: 6 -> 5; matrix products, arithmetic and copies ran while one was open for 1% -> 1% of each run, Pallas kernels for 8% -> 15%
where the time goes in v2:
time: 250 us; the launch traced here: 249 us
  blocking collectives  110 us (44%)
  starting transfers between devices  55.5 us (22%)
  Pallas kernels  53.5 us (21%)
  waiting for transfers between devices  22.2 us (9%)
  local copies, waits for them, and re-layouts  4.8 us (2%)
    all_to_all x1, blocking collectives, body(): deal = lax.all_to_all(deal, 'col', 0, 0, tiled=True)  43 us
    all_gather x1, blocking collectives, body(): parts = lax.all_gather(payload, 'row', tiled=True)  33.9 us
    all_gather x1, blocking collectives, body(): panel_cols = lax.all_gather(payload, 'row', tiled=True)  33.1 us
    all_to_all x2, starting transfers between devices, spread(): return lax.all_to_all(jnp.tile(value, (count, 1)), axis, 0, 0, tiled=True)  28.7 us
    pallas_call x1, Pallas kernels, body(): call(factor_kernel, [(NB, NB)] * 3, scratch=[(NB, NB)] * 2, n_in=1, name=...  25 us
    all_to_all x2, waiting for transfers between devices, spread(): return lax.all_to_all(jnp.tile(value, (count, 1)), axis, 0, 0, tiled=True)  14.1 us
    pallas_call x1, Pallas kernels, body(): call(update_kernel, [(TR * NB * TC * 2, LANES)], n_scalars=1, n_in=6, nam...  8.26 us
    all_to_all x1, starting transfers between devices, body(): lax.all_to_all(mirror, 'row', 0, 0, tiled=True)  7.55 us
  transfers between devices with their start and end apart: 8, of which 5 were waited for; matrix products, arithmetic and copies ran while one was open for 1% of the time, Pallas kernels for 15%

profile of v2, /device:TPU:1, one launch (start us, length us, event | category | flops | bytes accessed | tf_op | source)
XLA Modules:
  0.0 248.7 jit_solution(8791838144028689223)
XLA Ops:
  0.6 0.0 copy-start.4
  0.6 1.9 tile.4
  2.6 10.5 %all-to-all-start = ((f32[32,64,128]{2,1,0:T(8,128)}), f32[32,64,128]{2,1,0:T(8,128)S(1)}, u32[]{:S(2)}, u32[]{:S(2)}) async-start(f32[32,64,128]{2,1,0:T(8,128)} %tile.4), calls=%async_computation | async-start | bytes 2097152 | tf_op jit(solution)/shard_map/panel/all_to_all | solution.py:340
  13.0 0.0 copy-done.4
  13.1 5.1 %collective-permute-start = (f32[32,128]{1,0:T(8,128)S(1)}, f32[32,128]{1,0:T(8,128)S(1)}, u32[]{:S(2)}, u32[]{:S(2)}) collective-permute-start(f32[32,128]{1,0:T(8,128)S(1)} %bitcast.35), channel_id=1, source_target_pairs={{0,0},{1,16},{2,32},{3,48},{4,64},{5,80},{6,96},{7,112},{8,128},{9... | collective-permute-start | bytes 49160 | tf_op jit(solution)/shard_map/panel/ppermute | solution.py:357
  18.2 1.9 collective-permute-start.1
  20.2 0.7 pad_add_fusion.place
  20.8 0.0 collective-permute-done
  20.8 2.2 collective-permute-done.1
  23.0 0.6 broadcast_select_fusion.4
  23.6 6.7 %all-to-all-done = f32[32,64,128]{2,1,0:T(8,128)S(1)} async-done(((f32[32,64,128]{2,1,0:T(8,128)}), f32[32,64,128]{2,1,0:T(8,128)S(1)}, u32[]{:S(2)}, u32[]{:S(2)}) %all-to-all-start) | async-done | bytes 1048608 | tf_op jit(solution)/shard_map/panel/all_to_all | solution.py:340
  30.3 0.0 copy-start
  30.3 1.0 copy-done
  31.3 2.8 %gram.1 = f32[96,128]{1,0:T(8,128)} custom-call(s32[2]{0:T(128)} %pad_add_fusion.place, f32[64,128]{1,0:T(8,128)} %bitcast.32, f32[2048,128]{1,0:T(8,128)} %bitcast.20, f32[32,128]{1,0:T(8,128)} %get-tuple-element.17.early_ref, f32[32,128]{1,0:T(8,128)} %get-tuple-element.18.late_ref), custom_call_target="tpu_custom_call" | custom-call | bytes 1048576 | tf_op jit(solution)/shard_map/gram/gram/pallas_call | solution.py:384
  34.1 33.1 %all_gather.6.panel_cols_ref.panel_ref = f32[1536,128]{1,0:T(8,128)S(1)} all-gather(f32[96,128]{1,0:T(8,128)} %gram.1), channel_id=1, replica_groups=mesh['row'=16,'col'=32] {'row'}, dimensions={0}, use_global_device_ids=true | all-gather | bytes 835584 | tf_op jit(solution)/shard_map/gram/all_gather | solution.py:387
  67.2 0.0 copy-start.1
  67.2 0.9 tile.5
  68.1 18.2 %all-to-all-start.1 = ((f32[32,32,128]{2,1,0:T(8,128)}), f32[32,32,128]{2,1,0:T(8,128)S(1)}, u32[]{:S(2)}, u32[]{:S(2)}) async-start(f32[32,32,128]{2,1,0:T(8,128)} %tile.5), calls=%async_computation.1 | async-start | bytes 1048576 | tf_op jit(solution)/shard_map/gram/all_to_all | solution.py:340
  86.4 4.1 %mirror.1 = f32[256,512]{1,0:T(8,128)} custom-call(s32[2]{0:T(128)} %pad_add_fusion.place, f32[2048,128]{1,0:T(8,128)} %bitcast.21, f32[4096,128]{1,0:T(8,128)} %bitcast.17), custom_call_target="tpu_custom_call" | custom-call | bytes 4194304 | tf_op jit(solution)/shard_map/mirror/mirror/pallas_call | solution.py:391
  90.5 0.0 copy-done.1
  90.5 7.4 %all-to-all-done.1 = f32[32,32,128]{2,1,0:T(8,128)S(1)} async-done(((f32[32,32,128]{2,1,0:T(8,128)}), f32[32,32,128]{2,1,0:T(8,128)S(1)}, u32[]{:S(2)}, u32[]{:S(2)}) %all-to-all-start.1) | async-done | bytes 524320 | tf_op jit(solution)/shard_map/gram/all_to_all | solution.py:340
  98.0 0.0 copy-start.3
  98.0 7.6 %all-to-all-start.3 = ((f32[16,16,512]{2,1,0:T(8,128)}), f32[16,16,512]{2,1,0:T(8,128)S(1)}, u32[]{:S(2)}, u32[]{:S(2)}) async-start(f32[16,16,512]{2,1,0:T(8,128)} %bitcast.28), calls=%async_computation.3 | async-start | bytes 1048576 | tf_op jit(solution)/shard_map/mirror/all_to_all | solution.py:396
  105.5 0.0 copy-done.3
  105.5 25.0 %factor.1 = (f32[256,256]{1,0:T(8,128)}, f32[256,256]{1,0:T(8,128)}, f32[256,256]{1,0:T(8,128)}) custom-call(f32[1024,128]{1,0:T(8,128)} %bitcast.30), custom_call_target="tpu_custom_call" | custom-call | flops 10000000000 | bytes 83886080 | tf_op jit(solution)/shard_map/factor/factor/pallas_call | solution.py:399
  130.5 4.4 %symmetric.1 = f32[256,1024]{1,0:T(8,128)} custom-call(s32[2]{0:T(128)} %pad_add_fusion.place, f32[256,256]{1,0:T(8,128)} %get-tuple-element.30.band_ref, f32[1536,128]{1,0:T(8,128)} %copy-done.1, f32[4096,128]{1,0:T(8,128)} %bitcast.18), custom_call_target="tpu_custom_call" | custom-call | bytes 4194304 | tf_op jit(solution)/shard_map/symmetric/symmetric/pallas_call | solution.py:409
  135.0 0.0 all-to-all-done.3
  135.0 5.2 %all-to-all-start.2 = ((f32[32,8,1024]{2,1,0:T(8,128)}), f32[32,8,1024]{2,1,0:T(8,128)S(1)}, u32[]{:S(2)}, u32[]{:S(2)}) async-start(f32[32,8,1024]{2,1,0:T(8,128)} %bitcast.26), calls=%async_computation.2 | async-start | bytes 2097152 | tf_op jit(solution)/shard_map/sums/all_to_all | solution.py:422
  140.2 3.5 %collective-permute-start.3 = (f32[8,512]{1,0:T(8,128)S(1)}, f32[8,512]{1,0:T(8,128)S(1)}, u32[]{:S(2)}, u32[]{:S(2)}) collective-permute-start(f32[8,512]{1,0:T(8,128)S(1)} %get-tuple-element.34), channel_id=1, source_target_pairs={{0,0},{16,1},{32,2},{48,3},{64,4},{80,5},{96,6},{112,7},{128,8},{1... | collective-permute-start | bytes 49160 | tf_op jit(solution)/shard_map/sums/ppermute | solution.py:365
  143.7 3.5 %collective-permute-start.2 = (f32[8,512]{1,0:T(8,128)S(1)}, f32[8,512]{1,0:T(8,128)S(1)}, u32[]{:S(2)}, u32[]{:S(2)}) collective-permute-start(f32[8,512]{1,0:T(8,128)S(1)} %get-tuple-element.35), channel_id=1, source_target_pairs={{16,0},{0,1},{48,2},{32,3},{80,4},{64,5},{112,6},{96,7},{144,8},{1... | collective-permute-start | bytes 49160 | tf_op jit(solution)/shard_map/sums/ppermute | solution.py:366
  147.2 3.7 %vectors.1 = (f32[256,1024]{1,0:T(8,128)}, f32[256,512]{1,0:T(8,128)}, f32[256,256]{1,0:T(8,128)}, f32[64,128]{1,0:T(8,128)}) custom-call(s32[2]{0:T(128)} %pad_add_fusion.place, f32[256,256]{1,0:T(8,128)} %get-tuple-element.20.linv_ref, f32[256,256]{1,0:T(8,128)} %get-tuple-element.31.refl_ref, f32[2048,128]{1,0:T(8,128)} %bitcast.22, f32[1536,128]{1,0:T(8,128)} %copy-done.1), custom_call_target="tpu_custom_call" | custom-call | bytes 4194304 | tf_op jit(solution)/shard_map/vectors/vectors/pallas_call | solution.py:413
  150.9 1.1 collective-permute-done.3
  152.0 0.0 collective-permute-done.2
  152.0 0.6 broadcast_select_fusion.2
  152.6 4.8 %all-to-all-done.2 = f32[32,8,1024]{2,1,0:T(8,128)S(1)} async-done(((f32[32,8,1024]{2,1,0:T(8,128)}), f32[32,8,1024]{2,1,0:T(8,128)S(1)}, u32[]{:S(2)}, u32[]{:S(2)}) %all-to-all-start.2) | async-done | bytes 1048608 | tf_op jit(solution)/shard_map/sums/all_to_all | solution.py:422
  157.5 0.0 copy-start.2
  157.5 1.0 copy-done.2
  158.4 2.7 %share.1.own_ref = f32[40,256]{1,0:T(8,128)} custom-call(f32[256,1024]{1,0:T(8,128)} %bitcast.27, f32[8,512]{1,0:T(8,128)} %get-tuple-element.33.even_ref, f32[8,512]{1,0:T(8,128)} %get-tuple-element.32.odd_ref, f32[256,1024]{1,0:T(8,128)} %get-tuple-element.22.rows_ref), custom_call_target="tpu_custom_call" | custom-call | bytes 2097152 | tf_op jit(solution)/shard_map/sums/share/pallas_call | solution.py:424
  161.2 33.9 %all_gather.7.part_ref = f32[640,256]{1,0:T(8,128)} all-gather(f32[40,256]{1,0:T(8,128)} %share.1.own_ref), channel_id=1, replica_groups=mesh['row'=16,'col'=32] {'row'}, dimensions={0}, use_global_device_ids=true | all-gather | bytes 696320 | tf_op jit(solution)/shard_map/sums/all_gather | solution.py:427
  195.0 2.5 deal.1
  197.5 43.0 %all_to_all.49 = f32[32,56,256]{2,1,0:T(8,128)} all-to-all(f32[32,56,256]{2,1,0:T(8,128)} %bitcast.24), channel_id=1, replica_groups=mesh['row'=16,'col'=32] {'col'}, dimensions={0} | all-to-all | bytes 3670016 | tf_op jit(solution)/shard_map/deal/all_to_all | solution.py:432
  240.5 8.3 %update.1 = f32[4096,128]{1,0:T(8,128)} custom-call(s32[2]{0:T(128)} %pad_add_fusion.place, f32[4096,128]{1,0:T(8,128)} %bitcast.19, f32[256,1024]{1,0:T(8,128)} %get-tuple-element.22.rows_ref, f32[256,512]{1,0:T(8,128)} %get-tuple-element.23.cols_ref, f32[1792,256]{1,0:T(8,128)} %bitcast.25, f32[256,256]{1,0:T(8,128)} %get-tuple-element.31.refl_ref, ...), custom_call_target="tpu_custom_call" | custom-call | bytes 8388608 | tf_op jit(solution)/shard_map/update/update/pallas_call | solution.py:434
  (4 shorter events, 0.1 us)
Async XLA Ops:
  0.6 12.4 %copy-start.4 = (f32[8,4,1,256]{3,2,1,0:T(1,128)S(1)}, f32[8,4,1,256]{3,2,1,0:T(1,128)}, u32[]{:S(2)}) copy-start(f32[8,4,1,256]{3,2,1,0:T(1,128)} %param.3) | copy-start | bytes 98308
  2.6 27.8 %all-to-all-start = ((f32[32,64,128]{2,1,0:T(8,128)}), f32[32,64,128]{2,1,0:T(8,128)S(1)}, u32[]{:S(2)}, u32[]{:S(2)}) async-start(f32[32,64,128]{2,1,0:T(8,128)} %tile.4), calls=%async_computation | async-start | bytes 2097152 | tf_op jit(solution)/shard_map/panel/all_to_all | solution.py:340
  13.1 7.8 %collective-permute-start = (f32[32,128]{1,0:T(8,128)S(1)}, f32[32,128]{1,0:T(8,128)S(1)}, u32[]{:S(2)}, u32[]{:S(2)}) collective-permute-start(f32[32,128]{1,0:T(8,128)S(1)} %bitcast.35), channel_id=1, source_target_pairs={{0,0},{1,16},{2,32},{3,48},{4,64},{5,80},{6,96},{7,112},{8,128},{9... | collective-permute-start | bytes 49160 | tf_op jit(solution)/shard_map/panel/ppermute | solution.py:357
  18.2 4.8 %collective-permute-start.1 = (f32[32,128]{1,0:T(8,128)S(1)}, f32[32,128]{1,0:T(8,128)S(1)}, u32[]{:S(2)}, u32[]{:S(2)}) collective-permute-start(f32[32,128]{1,0:T(8,128)S(1)} %bitcast.34), channel_id=1, source_target_pairs={{0,16},{1,0},{2,48},{3,32},{4,80},{5,64},{6,112},{7,96},{8,144},{9... | collective-permute-start | bytes 49160 | tf_op jit(solution)/shard_map/panel/ppermute | solution.py:358
  30.3 1.0 copy-start
  67.2 23.4 %copy-start.1 = (f32[1536,128]{1,0:T(8,128)}, f32[1536,128]{1,0:T(8,128)S(1)}, u32[]{:S(2)}) copy-start(f32[1536,128]{1,0:T(8,128)S(1)} %all_gather.6.panel_cols_ref.panel_ref) | copy-start | bytes 2359300
  68.1 29.8 %all-to-all-start.1 = ((f32[32,32,128]{2,1,0:T(8,128)}), f32[32,32,128]{2,1,0:T(8,128)S(1)}, u32[]{:S(2)}, u32[]{:S(2)}) async-start(f32[32,32,128]{2,1,0:T(8,128)} %tile.5), calls=%async_computation.1 | async-start | bytes 1048576 | tf_op jit(solution)/shard_map/gram/all_to_all | solution.py:340
  98.0 7.6 %copy-start.3 = (f32[32,32,128]{2,1,0:T(8,128)}, f32[32,32,128]{2,1,0:T(8,128)S(1)}, u32[]{:S(2)}) copy-start(f32[32,32,128]{2,1,0:T(8,128)S(1)} %all-to-all-done.1) | copy-start | bytes 1572868
  98.0 37.0 %all-to-all-start.3 = ((f32[16,16,512]{2,1,0:T(8,128)}), f32[16,16,512]{2,1,0:T(8,128)S(1)}, u32[]{:S(2)}, u32[]{:S(2)}) async-start(f32[16,16,512]{2,1,0:T(8,128)} %bitcast.28), calls=%async_computation.3 | async-start | bytes 1048576 | tf_op jit(solution)/shard_map/mirror/all_to_all | solution.py:396
  135.0 22.5 %all-to-all-start.2 = ((f32[32,8,1024]{2,1,0:T(8,128)}), f32[32,8,1024]{2,1,0:T(8,128)S(1)}, u32[]{:S(2)}, u32[]{:S(2)}) async-start(f32[32,8,1024]{2,1,0:T(8,128)} %bitcast.26), calls=%async_computation.2 | async-start | bytes 2097152 | tf_op jit(solution)/shard_map/sums/all_to_all | solution.py:422
  140.2 11.8 %collective-permute-start.3 = (f32[8,512]{1,0:T(8,128)S(1)}, f32[8,512]{1,0:T(8,128)S(1)}, u32[]{:S(2)}, u32[]{:S(2)}) collective-permute-start(f32[8,512]{1,0:T(8,128)S(1)} %get-tuple-element.34), channel_id=1, source_target_pairs={{0,0},{16,1},{32,2},{48,3},{64,4},{80,5},{96,6},{112,7},{128,8},{1... | collective-permute-start | bytes 49160 | tf_op jit(solution)/shard_map/sums/ppermute | solution.py:365
  143.7 8.3 %collective-permute-start.2 = (f32[8,512]{1,0:T(8,128)S(1)}, f32[8,512]{1,0:T(8,128)S(1)}, u32[]{:S(2)}, u32[]{:S(2)}) collective-permute-start(f32[8,512]{1,0:T(8,128)S(1)} %get-tuple-element.35), channel_id=1, source_target_pairs={{16,0},{0,1},{48,2},{32,3},{80,4},{64,5},{112,6},{96,7},{144,8},{1... | collective-permute-start | bytes 49160 | tf_op jit(solution)/shard_map/sums/ppermute | solution.py:366
  157.5 1.0 copy-start.2

commit v3 on v2

--- a/solution.py
+++ b/solution.py
@@ -19,14 +19,23 @@
 SMEM = pl.BlockSpec(memory_space=pltpu.SMEM)
 
 
-def call(kernel, outs, scratch=(), n_scalars=0, n_in=1, name=None, flops=0, moved=0):
+ANY = pl.BlockSpec(memory_space=pl.ANY)
+
+
+def call(
+    kernel, outs, scratch=(), n_scalars=0, n_in=1, n_any=0, any_out=False, copies=0,
+    name=None, flops=0, moved=0,
+):
+    buffers = [pltpu.VMEM(shape, F32) for shape in scratch]
+    if copies:
+        buffers.append(pltpu.SemaphoreType.DMA((copies,)))
     return pl.pallas_call(
         kernel,
         out_shape=[jax.ShapeDtypeStruct(shape, F32) for shape in outs],
-        in_specs=[SMEM] * n_scalars + [VMEM] * n_in,
-        out_specs=[VMEM] * len(outs),
-        scratch_shapes=[pltpu.VMEM(shape, F32) for shape in scratch],
-        compiler_params=pltpu.CompilerParams(vmem_limit_bytes=60 * 2**20),
+        in_specs=[SMEM] * n_scalars + [VMEM] * n_in + [ANY] * n_any,
+        out_specs=[ANY if any_out else VMEM] * len(outs),
+        scratch_shapes=buffers,
+        compiler_params=pltpu.CompilerParams(vmem_limit_bytes=40 * 2**20),
         cost_estimate=pl.CostEstimate(flops=flops, bytes_accessed=moved, transcendentals=0),
         name=name,
     )
@@ -81,7 +90,7 @@
     return jnp.concatenate([ref[matrix_rows(t, u, half), :] for half in range(2)], axis=1)
 
 
-def gram_kernel(place, own_ref, panel_ref, early_ref, late_ref, out_ref):
+def gram_kernel(place, own_ref, early_ref, late_ref, panel_ref, out_ref):
     total = jnp.zeros((SHARE, NB), F32)
     for piece in range(TR * 2):
         total += exact(
@@ -109,27 +118,61 @@
     )
 
 
-def factor_kernel(g_ref, band_ref, linv_ref, refl_ref, a_ref, u_ref):
-    n = NB
-    steps = n // BS
+def stacked(a, b):
+    def three(x):
+        high = x.astype(jnp.bfloat16)
+        x = x - high.astype(F32)
+        mid = x.astype(jnp.bfloat16)
+        return high, mid, (x - mid.astype(F32)).astype(jnp.bfloat16)
+
+    a1, a2, a3 = three(a)
+    b1, b2, b3 = three(b)
+    return lax.dot_general(
+        jnp.concatenate([a1, a1, a1, a2, a2, a3], axis=0),
+        jnp.concatenate([b1, b2, b3, b1, b2, b1], axis=0),
+        (((0,), (0,)), ((), ())),
+        preferred_element_type=F32,
+    )
+
+
+def block_iotas():
     rows = lax.broadcasted_iota(jnp.int32, (BS, LANES), 0)
     lanes = lax.broadcasted_iota(jnp.int32, (BS, LANES), 1)
-    eye = (rows == lanes).astype(F32)
-    wide = lax.broadcasted_iota(jnp.int32, (BS, n), 1)
-    full_row = lax.broadcasted_iota(jnp.int32, (n, n), 0)
-    full_col = lax.broadcasted_iota(jnp.int32, (n, n), 1)
-    a_ref[...] = gathered_columns(g_ref, (0, 1))
-
-    def advance(base, update, row):
-        a_ref[: n - BS, :] = pltpu.roll(base[BS:] - update[BS:], n - BS, 1)
-        a_ref[n - BS :, :] = pltpu.roll(row, n - BS, 1)
-
-    def chol_step(step, carry):
-        left = n - BS * step
-        a = a_ref[...]
-        first, second = a[:BS, :LANES], a[:BS, LANES:]
-        heads = [jnp.broadcast_to(first[:, k : k + 1], (BS, LANES)) for k in range(BS)]
-        inner = eye
+    wide = lax.broadcasted_iota(jnp.int32, (BS, NB), 1)
+    return rows, lanes, wide
+
+
+def turn(a_ref, base, row):
+    a_ref[: NB - BS, :] = pltpu.roll(base[BS:], NB - BS, 1)
+    a_ref[NB - BS :, :] = pltpu.roll(row, NB - BS, 1)
+
+
+def unturned(value, a_ref, row_ref):
+    turned = pltpu.roll(value, BS, 1)
+    a_ref[:BS, :] = turned[NB - BS :]
+    a_ref[BS:, :] = turned[: NB - BS]
+    row_ref[...] = turned[NB - BS :]
+
+
+def lane_spread(first):
+    return [jnp.broadcast_to(first[:, k : k + 1], (BS, LANES)) for k in range(BS)]
+
+
+def cholesky(g_ref, band_ref, linv_ref, a_ref, u_ref, row_ref, multiplier_ref):
+    rows, lanes, wide = block_iotas()
+    full_row, full_col = ordering()
+    unturned(gathered_columns(g_ref, (0, 1)), a_ref, row_ref)
+    multiplier_ref[...] = jnp.zeros((BS, NB), F32)
+
+    def step_of(step, carry):
+        left = NB - BS * step
+        begun = step > 0
+        a, last, multiplier = a_ref[...], row_ref[...], multiplier_ref[...]
+        top = jnp.where((wide < BS) & begun, 0.0, a[BS : 2 * BS])
+        top = pltpu.roll(top - stacked(multiplier[:, BS : 2 * BS], last), NB - BS, 1)
+        first, second = top[:, :LANES], top[:, LANES:]
+        heads = lane_spread(first)
+        inner = (rows == lanes).astype(F32)
         pivots = jnp.ones((BS, LANES), F32)
         for j in range(BS):
             pivot = heads[j][j : j + 1]
@@ -146,22 +189,33 @@
         upper = jnp.concatenate([jnp.where(lanes >= rows, first, 0.0), second], axis=1)
         upper = jnp.where(wide < left, upper, 0.0)
         u_ref[pl.ds(pl.multiple_of(step * BS, BS), BS), :] = pltpu.roll(upper, step * BS, 1)
-        row = jnp.concatenate([jnp.where(lanes < BS, inner, first), second], axis=1)
-        update = exact(jnp.where(wide >= BS, upper, 0.0), row, 0, 0)
-        advance(jnp.where((full_col < BS) & (full_row < left), 0.0, a), update, row)
+        row_ref[...] = jnp.concatenate([jnp.where(lanes < BS, inner, first), second], axis=1)
+        multiplier_ref[...] = jnp.where(wide >= BS, upper, 0.0)
+        kept = jnp.where((full_col < BS) & (full_row < left + BS) & begun, 0.0, a)
+        turn(a_ref, kept - stacked(multiplier, last), last)
         return carry
 
-    lax.fori_loop(0, steps, chol_step, 0)
-    linv = jnp.where(full_col <= full_row, a_ref[...], 0.0)
-    linv_ref[...] = linv
+    lax.fori_loop(0, NB // BS, step_of, 0)
+    turn(a_ref, a_ref[...], row_ref[...])
+    linv_ref[...] = jnp.where(full_col <= full_row, a_ref[...], 0.0)
     band_ref[...] = -u_ref[...]
-    a_ref[...] = exact(linv, gathered_columns(g_ref, (2, 3))) + (full_row == full_col).astype(F32)
-
-    def inverse_step(step, carry):
-        a = a_ref[...]
-        first, second = a[:BS, :LANES], a[:BS, LANES:]
-        heads = [jnp.broadcast_to(first[:, k : k + 1], (BS, LANES)) for k in range(BS)]
-        first = jnp.where(lanes < BS, eye, first)
+
+
+def reflector_factor(g_ref, linv_ref, refl_ref, a_ref, row_ref):
+    rows, lanes, _ = block_iotas()
+    full_row, full_col = ordering()
+    top_block = exact(linv_ref[...], gathered_columns(g_ref, (2, 3)))
+    unturned(top_block + (full_row == full_col).astype(F32), a_ref, row_ref)
+
+    def step_of(step, carry):
+        begun = step > 0
+        a, last = a_ref[...], row_ref[...]
+        kept = jnp.where((full_col < BS) & begun, 0.0, a)
+        column = jnp.where(begun, a[:, :BS], 0.0)
+        top = pltpu.roll(kept[BS : 2 * BS] - exact(column[BS : 2 * BS], last), NB - BS, 1)
+        first, second = top[:, :LANES], top[:, LANES:]
+        heads = lane_spread(first)
+        first = jnp.where(lanes < BS, (rows == lanes).astype(F32), first)
         for j in range(BS):
             head = heads[j]
             inverse = 1.0 / head[j : j + 1]
@@ -173,13 +227,19 @@
             for k in range(j + 1, BS):
                 heads[k] = put(heads[k])
             first, second = put(first), put(second)
-        row = jnp.concatenate([first, second], axis=1)
-        update = exact(a[:, :BS], row)
-        advance(jnp.where(full_col < BS, 0.0, a), update, row)
+        row_ref[...] = jnp.concatenate([first, second], axis=1)
+        turn(a_ref, kept - exact(column, last), last)
         return carry
 
-    lax.fori_loop(0, steps, inverse_step, 0)
+    lax.fori_loop(0, NB // BS, step_of, 0)
+    a, last = a_ref[...], row_ref[...]
+    turn(a_ref, jnp.where(full_col < BS, 0.0, a) - exact(a[:, :BS], last), last)
     refl_ref[...] = a_ref[...]
+
+
+def factor_kernel(g_ref, band_ref, linv_ref, refl_ref, a_ref, u_ref, row_ref, multiplier_ref):
+    cholesky(g_ref, band_ref, linv_ref, a_ref, u_ref, row_ref, multiplier_ref)
+    reflector_factor(g_ref, linv_ref, refl_ref, a_ref, row_ref)
 
 
 def tile_place(place, t, u):
@@ -211,9 +271,26 @@
                 out_ref[:, here] += product(rows, split(tile))
 
 
-def symmetric_kernel(place, band_ref, panel_ref, matrix_ref, out_ref):
+def row_copies(matrix_hbm, matrix_ref, sems, first):
+    rows = matrix_ref.shape[0] // TR
+    return [
+        pltpu.make_async_copy(
+            matrix_hbm.at[pl.ds(t * rows, rows)], matrix_ref.at[pl.ds(t * rows, rows)],
+            sems.at[first + t],
+        )
+        for t in range(TR)
+    ]
+
+
+def symmetric_kernel(
+    place, band_ref, matrix_ref, panel_hbm, out_hbm, panel_ref, out_ref, sems
+):
+    panel_copy = pltpu.make_async_copy(panel_hbm, panel_ref, sems.at[0])
+    panel_copy.start()
+    out_copies = []
     factor = -jnp.transpose(band_ref[...])
     out_ref[...] = jnp.zeros((NB, TR * NB), F32)
+    panel_copy.wait()
     cols = []
     for u in range(TC):
         value = gathered_tile(panel_ref, u)
@@ -242,6 +319,13 @@
                 r, c = ordering()
                 tile = jnp.where(r > c, matrix_tile(matrix_ref, 0, 0), 0.0)
                 out_ref[:, here] += product(split(factor), split(tile))
+
+        out_copies.append(
+            pltpu.make_async_copy(out_ref.at[:, here], out_hbm.at[:, here], sems.at[1 + t])
+        )
+        out_copies[t].start()
+    for copy in out_copies:
+        copy.wait()
 
 
 def vectors_kernel(
@@ -282,11 +366,13 @@
     out_ref[pl.ds(TR * SHARE, SHARE), :] = product(split(total), split(rows_ref[...]), 1, 1)
 
 
-def deal_kernel(own_ref, part_ref, out_ref):
+def deal_kernel(own_ref, part_ref, out_hbm, out_ref, sems):
     curved = part_ref[pl.ds(TR * SHARE, SHARE), :]
     for r in range(1, N_ROW):
         curved = curved + part_ref[pl.ds(r * PART + TR * SHARE, SHARE), :]
     own = own_ref[: TR * SHARE, :]
+    copies = []
+    group = N_COL // 4
     for c in range(N_COL):
         for u in range(TC):
             t = u * (N_COL // N_ROW) + c // N_ROW
@@ -295,6 +381,14 @@
             ]
         out_ref[pl.ds(c * DEAL + TC * SHARE, SHARE), :] = curved
         out_ref[pl.ds(c * DEAL + (TC + 1) * SHARE, TR * SHARE), :] = own
+        if c % group == group - 1:
+            at = pl.ds((c + 1 - group) * DEAL, group * DEAL)
+            copies.append(
+                pltpu.make_async_copy(out_ref.at[at], out_hbm.at[at], sems.at[len(copies)])
+            )
+            copies[-1].start()
+    for copy in copies:
+        copy.wait()
 
 
 def dealt(ref, slot):
@@ -304,11 +398,17 @@
 
 
 def update_kernel(
-    place, matrix_ref, rows_ref, cols_ref, dealt_ref, refl_ref, both_ref, out_ref
+    place, refl_ref, both_ref, cols_ref, rows_ref, matrix_ref, dealt_hbm, out_hbm,
+    dealt_ref, out_ref, sems,
 ):
+    dealt_copy = pltpu.make_async_copy(dealt_hbm, dealt_ref, sems.at[0])
+    dealt_copy.start()
+    out_copies = row_copies(out_ref, out_hbm, sems, 1)
     both = split(both_ref[...])
+    refl = split(refl_ref[...])
+    dealt_copy.wait()
     curved = split(product(both, split(dealt(dealt_ref, TC))))
-    half_mixed = split(0.5 * product(curved, split(refl_ref[...])))
+    half_mixed = split(0.5 * product(curved, refl))
     sides = []
     for u in range(TC):
         vectors = split(cols_ref[:, pl.ds(u * NB, NB)])
@@ -317,7 +417,9 @@
     for t in range(TR):
         here = pl.ds(t * NB, NB)
         vectors = split(rows_ref[:, here])
-        update = split(product(both, split(dealt(dealt_ref, TC + 1 + t))) - product(half_mixed, vectors))
+        update = split(
+            product(both, split(dealt(dealt_ref, TC + 1 + t))) - product(half_mixed, vectors)
+        )
         for u in range(TC):
             i, j = tile_place(place, t, u)
 
@@ -334,6 +436,10 @@
             def _():
                 for half in range(2):
                     out_ref[matrix_rows(t, u, half), :] = jnp.zeros((NB, LANES), F32)
+
+        out_copies[t].start()
+    for copy in out_copies:
+        copy.wait()
 
 
 def spread(value, axis, count):
@@ -383,7 +489,7 @@
     with jax.named_scope("gram"):
         (payload,) = call(
             gram_kernel, [(SPAN, LANES)], n_scalars=1, n_in=4, name="gram", moved=1 << 20
-        )(place, own, panel_rows, *chunk)
+        )(place, own, *chunk, panel_rows)
         panel_cols = lax.all_gather(payload, "row", tiled=True)
         summed = panel_cols.reshape(N_ROW, SPAN, LANES)[:, CHUNK * TC * 2 :].sum(0)
         gram = spread(summed, "col", N_COL)
@@ -399,7 +505,7 @@
         band, linv, reflector = call(
             factor_kernel,
             [(NB, NB)] * 3,
-            scratch=[(NB, NB)] * 2,
+            scratch=[(NB, NB)] * 2 + [(BS, NB)] * 2,
             n_in=1,
             name="factor",
             flops=10**10,
@@ -407,8 +513,11 @@
         )(gram)
     with jax.named_scope("symmetric"):
         (row_terms,) = call(
-            symmetric_kernel, [(NB, TR * NB)], n_scalars=1, n_in=3, name="symmetric", moved=4 << 20
-        )(place, band, panel_cols, stored)
+            symmetric_kernel, [(NB, TR * NB)],
+            scratch=[(N_ROW * SPAN, LANES), (NB, TR * NB)],
+            n_scalars=1, n_in=2, n_any=1, any_out=True, copies=1 + TR,
+            name="symmetric", moved=4 << 20,
+        )(place, band, stored, panel_cols)
     with jax.named_scope("vectors"):
         rows, cols, both, vectors = call(
             vectors_kernel,
@@ -426,19 +535,24 @@
         )
         parts = lax.all_gather(payload, "row", tiled=True)
     with jax.named_scope("deal"):
-        (deal,) = call(deal_kernel, [(N_COL * DEAL, NB)], n_in=2, name="deal", moved=3 << 20)(
-            payload, parts
-        )
+        (deal,) = call(
+            deal_kernel, [(N_COL * DEAL, NB)], scratch=[(N_COL * DEAL, NB)], n_in=2, any_out=True,
+            copies=4, name="deal", moved=3 << 20,
+        )(payload, parts)
         deal = lax.all_to_all(deal, "col", 0, 0, tiled=True)
     with jax.named_scope("update"):
         (updated,) = call(
             update_kernel,
             [(TR * NB * TC * 2, LANES)],
+            scratch=[(N_COL * DEAL, NB), (TR * NB * TC * 2, LANES)],
             n_scalars=1,
-            n_in=6,
+            n_in=5,
+            n_any=1,
+            any_out=True,
+            copies=1 + TR,
             name="update",
             moved=8 << 20,
-        )(place, stored, rows, cols, deal, reflector, both)
+        )(place, reflector, both, cols, rows, stored, deal)
     return (updated.reshape(matrix.shape), vectors.reshape(panel_t.shape), band, reflector)
 
 

time: 250 us -> 240 us (0.960)
  Pallas kernels: 53.5 us -> 39.6 us
  local copies, waits for them, and re-layouts: 4.8 us -> 13 us
  blocking collectives: 110 us -> 107 us
    unnamed x10 -> x36, local copies, waits for them, and re-layouts: 1.95 us -> 10.2 us
    pallas_call x4, Pallas kernels: 40.2 us -> 32.2 us  [the longest x1 22.8 us: body(): call(factor_kernel, [(NB, NB)] * 3, scratch=[(NB, NB)] * 2 + [(BS, NB)] *...]
    all_to_all x1, blocking collectives: 43 us -> 39.8 us  [body(): deal = lax.all_to_all(deal, 'col', 0, 0, tiled=True)]
  transfers between devices with their start and end apart: 8 -> 8, of which waited for: 5 -> 4; matrix products, arithmetic and copies ran while one was open for 1% -> 0% of each run, Pallas kernels for 15% -> 12%
where the time goes in v3:
time: 240 us; the launch traced here: 239 us
  blocking collectives  107 us (45%)
  starting transfers between devices  56.1 us (23%)
  Pallas kernels  39.6 us (16%)
  waiting for transfers between devices  21.4 us (9%)
  local copies, waits for them, and re-layouts  13 us (5%)
    all_to_all x1, blocking collectives, body(): deal = lax.all_to_all(deal, 'col', 0, 0, tiled=True)  39.8 us
    all_gather x1, blocking collectives, body(): parts = lax.all_gather(payload, 'row', tiled=True)  34.3 us
    all_gather x1, blocking collectives, body(): panel_cols = lax.all_gather(payload, 'row', tiled=True)  32.8 us
    all_to_all x2, starting transfers between devices, spread(): return lax.all_to_all(jnp.tile(value, (count, 1)), axis, 0, 0, tiled=True)  28.4 us
    pallas_call x1, Pallas kernels, body(): call(factor_kernel, [(NB, NB)] * 3, scratch=[(NB, NB)] * 2 + [(BS, NB)] *...  22.8 us
    all_to_all x2, waiting for transfers between devices, spread(): return lax.all_to_all(jnp.tile(value, (count, 1)), axis, 0, 0, tiled=True)  16 us
    unnamed x36, local copies, waits for them, and re-layouts  10.2 us
    all_to_all x1, starting transfers between devices, body(): lax.all_to_all(mirror, 'row', 0, 0, tiled=True)  7.39 us
  transfers between devices with their start and end apart: 8, of which 4 were waited for; matrix products, arithmetic and copies ran while one was open for 0% of the time, Pallas kernels for 12%

profile of v3, /device:TPU:1, one launch (start us, length us, event | category | flops | bytes accessed | tf_op | source)
XLA Modules:
  0.0 239.2 jit_solution(14805661058583371889)
XLA Ops:
  0.6 0.0 copy-start.12
  0.6 1.9 tile.4
  2.5 10.5 %all-to-all-start = ((f32[32,64,128]{2,1,0:T(8,128)}), f32[32,64,128]{2,1,0:T(8,128)S(1)}, u32[]{:S(2)}, u32[]{:S(2)}) async-start(f32[32,64,128]{2,1,0:T(8,128)} %tile.4), calls=%async_computation | async-start | bytes 2097152 | tf_op jit(solution)/shard_map/panel/all_to_all | solution.py:446
  13.0 0.0 copy-start
  13.0 0.0 copy-done.12
  13.1 5.3 %collective-permute-start = (f32[32,128]{1,0:T(8,128)S(1)}, f32[32,128]{1,0:T(8,128)S(1)}, u32[]{:S(2)}, u32[]{:S(2)}) collective-permute-start(f32[32,128]{1,0:T(8,128)S(1)} %bitcast.33), channel_id=1, source_target_pairs={{0,0},{1,16},{2,32},{3,48},{4,64},{5,80},{6,96},{7,112},{8,128},{9... | collective-permute-start | bytes 49160 | tf_op jit(solution)/shard_map/panel/ppermute | solution.py:463
  18.4 1.9 collective-permute-start.1
  20.3 0.1 pad_add_fusion.place
  20.4 0.0 collective-permute-done
  20.4 2.8 %collective-permute-done.1 = f32[32,128]{1,0:T(8,128)S(1)} collective-permute-done((f32[32,128]{1,0:T(8,128)S(1)}, f32[32,128]{1,0:T(8,128)S(1)}, u32[]{:S(2)}, u32[]{:S(2)}) %collective-permute-start.1) | collective-permute-done | bytes 16416 | tf_op jit(solution)/shard_map/panel/ppermute | solution.py:464
  23.1 7.2 %all-to-all-done = f32[32,64,128]{2,1,0:T(8,128)S(1)} async-done(((f32[32,64,128]{2,1,0:T(8,128)}), f32[32,64,128]{2,1,0:T(8,128)S(1)}, u32[]{:S(2)}, u32[]{:S(2)}) %all-to-all-start) | async-done | bytes 1048608 | tf_op jit(solution)/shard_map/panel/all_to_all | solution.py:446
  30.3 1.5 gram.1
  31.8 32.8 %all_gather.6.panel_cols_ref.panel_hbm = f32[1536,128]{1,0:T(8,128)S(1)} all-gather(f32[96,128]{1,0:T(8,128)S(1)} %gram.1), channel_id=1, replica_groups=mesh['row'=16,'col'=32] {'row'}, dimensions={0}, use_global_device_ids=true | all-gather | bytes 835584 | tf_op jit(solution)/shard_map/gram/all_gather | solution.py:493
  64.6 0.0 copy-start.1
  64.6 0.9 copy-done.1
  65.5 0.9 tile.5
  66.4 17.9 %all-to-all-start.1 = ((f32[32,32,128]{2,1,0:T(8,128)}), f32[32,32,128]{2,1,0:T(8,128)}, u32[]{:S(2)}, u32[]{:S(2)}) async-start(f32[32,32,128]{2,1,0:T(8,128)} %tile.5), calls=%async_computation.1 | async-start | bytes 1048576 | tf_op jit(solution)/shard_map/gram/all_to_all | solution.py:446
  84.3 0.0 copy-done
  84.3 2.0 mirror.1
  86.3 0.0 copy-start.8
  86.3 0.8 copy-done.8
  87.1 8.8 %all-to-all-done.1 = f32[32,32,128]{2,1,0:T(8,128)} async-done(((f32[32,32,128]{2,1,0:T(8,128)}), f32[32,32,128]{2,1,0:T(8,128)}, u32[]{:S(2)}, u32[]{:S(2)}) %all-to-all-start.1) | async-done | bytes 524320 | tf_op jit(solution)/shard_map/gram/all_to_all | solution.py:446
  95.9 7.4 %all-to-all-start.3 = ((f32[16,16,512]{2,1,0:T(8,128)}), f32[16,16,512]{2,1,0:T(8,128)}, u32[]{:S(2)}, u32[]{:S(2)}) async-start(f32[16,16,512]{2,1,0:T(8,128)} %bitcast.27), calls=%async_computation.3 | async-start | bytes 1048576 | tf_op jit(solution)/shard_map/mirror/all_to_all | solution.py:502
  103.3 0.0 copy-start.2
  103.3 22.8 %factor.1 = (f32[256,256]{1,0:T(8,128)}, f32[256,256]{1,0:T(8,128)S(1)}, f32[256,256]{1,0:T(8,128)}) custom-call(f32[1024,128]{1,0:T(8,128)} %bitcast.8.g_ref), custom_call_target="tpu_custom_call" | custom-call | flops 10000000000 | bytes 83886080 | tf_op jit(solution)/shard_map/factor/factor/pallas_call | solution.py:505
  126.1 0.0 copy-start.14
  126.1 0.7 copy-done.14
  126.8 0.0 copy-done.2
  126.8 0.0 copy-start.13
  126.8 0.9 copy-done.13
  127.8 2.3 symmetric.1
  130.1 0.0 copy-start.4
  130.1 1.0 copy-done.4
  131.1 0.0 all-to-all-done.3
  131.1 6.4 %all-to-all-start.2 = ((f32[32,8,1024]{2,1,0:T(8,128)}), f32[32,8,1024]{2,1,0:T(8,128)}, u32[]{:S(2)}, u32[]{:S(2)}) async-start(f32[32,8,1024]{2,1,0:T(8,128)} %bitcast.26), calls=%async_computation.2 | async-start | bytes 2097152 | tf_op jit(solution)/shard_map/sums/all_to_all | solution.py:531
  137.5 1.1 reduce_sum.19
  138.6 3.7 %collective-permute-start.3 = (f32[8,512]{1,0:T(8,128)S(1)}, f32[8,512]{1,0:T(8,128)S(1)}, u32[]{:S(2)}, u32[]{:S(2)}) collective-permute-start(f32[8,512]{1,0:T(8,128)S(1)} %get-tuple-element.34), channel_id=1, source_target_pairs={{0,0},{16,1},{32,2},{48,3},{64,4},{80,5},{96,6},{112,7},{128,8},{1... | collective-permute-start | bytes 49160 | tf_op jit(solution)/shard_map/sums/ppermute | solution.py:471
  142.3 3.1 %collective-permute-start.2 = (f32[8,512]{1,0:T(8,128)S(1)}, f32[8,512]{1,0:T(8,128)S(1)}, u32[]{:S(2)}, u32[]{:S(2)}) collective-permute-start(f32[8,512]{1,0:T(8,128)S(1)} %get-tuple-element.35), channel_id=1, source_target_pairs={{16,0},{0,1},{48,2},{32,3},{80,4},{64,5},{112,6},{96,7},{144,8},{1... | collective-permute-start | bytes 49160 | tf_op jit(solution)/shard_map/sums/ppermute | solution.py:472
  145.4 0.0 copy-done.9
  145.4 0.0 copy-start.3
  145.4 1.1 copy-done.3
  146.5 0.0 copy-start.15
  146.5 0.9 copy-done.15
  147.5 2.2 vectors.1
  149.7 0.0 copy-start.5
  149.7 1.0 copy-done.5
  150.6 0.0 copy-start.10
  150.6 0.8 copy-done.10
  151.5 0.7 copy-done.16
  152.2 0.0 collective-permute-done.3
  152.2 0.0 collective-permute-done.2
  152.2 2.7 %all-to-all-done.2 = f32[32,8,1024]{2,1,0:T(8,128)} async-done(((f32[32,8,1024]{2,1,0:T(8,128)}), f32[32,8,1024]{2,1,0:T(8,128)}, u32[]{:S(2)}, u32[]{:S(2)}) %all-to-all-start.2) | async-done | bytes 1048608 | tf_op jit(solution)/shard_map/sums/all_to_all | solution.py:531
  154.9 1.2 copy-done.6
  156.1 1.8 share.1.own_ref
  157.9 34.3 %all_gather.7.part_ref = f32[640,256]{1,0:T(8,128)S(1)} all-gather(f32[40,256]{1,0:T(8,128)S(1)} %share.1.own_ref), channel_id=1, replica_groups=mesh['row'=16,'col'=32] {'row'}, dimensions={0}, use_global_device_ids=true | all-gather | bytes 696320 | tf_op jit(solution)/shard_map/sums/all_gather | solution.py:536
  192.1 1.3 deal.1
  193.4 0.0 copy-start.7
  193.4 0.0 copy-start.11
  193.4 0.0 copy-start.17
  193.4 39.8 %all_to_all.49 = f32[32,56,256]{2,1,0:T(8,128)S(1)} all-to-all(f32[32,56,256]{2,1,0:T(8,128)S(1)} %bitcast.24), channel_id=1, replica_groups=mesh['row'=16,'col'=32] {'col'}, dimensions={0} | all-to-all | bytes 3670016 | tf_op jit(solution)/shard_map/deal/all_to_all | solution.py:542
  233.2 0.0 copy-done.7
  233.2 0.0 copy-done.11
  233.2 0.0 copy-done.17
  233.2 5.8 %update.1 = f32[4096,128]{1,0:T(8,128)} custom-call(s32[2]{0:T(128)S(1)} %pad_add_fusion.place, f32[256,256]{1,0:T(8,128)S(1)} %copy-done.9, f32[256,256]{1,0:T(8,128)S(1)} %copy-done.17, f32[256,512]{1,0:T(8,128)S(1)} %copy-done.11, f32[256,1024]{1,0:T(8,128)S(1)} %copy-done.7, f32[4096,128]{1,0:T(8,128)S(1)} %bitcast.19, f32[1792,256]{1,0:T(8,128)S(1)} %bitcast.25), custom_call_target="tpu_custom_call" | custom-call | bytes 8388608 | tf_op jit(solution)/shard_map/update/update/pallas_call | solution.py:544
  (8 shorter events, 0.1 us)
Async XLA Ops:
  0.6 12.4 %copy-start.12 = (f32[8,4,1,256]{3,2,1,0:T(1,128)S(1)}, f32[8,4,1,256]{3,2,1,0:T(1,128)}, u32[]{:S(2)}) copy-start(f32[8,4,1,256]{3,2,1,0:T(1,128)} %param.3) | copy-start | bytes 98308
  2.5 27.8 %all-to-all-start = ((f32[32,64,128]{2,1,0:T(8,128)}), f32[32,64,128]{2,1,0:T(8,128)S(1)}, u32[]{:S(2)}, u32[]{:S(2)}) async-start(f32[32,64,128]{2,1,0:T(8,128)} %tile.4), calls=%async_computation | async-start | bytes 2097152 | tf_op jit(solution)/shard_map/panel/all_to_all | solution.py:446
  13.0 71.3 %copy-start = (f32[4,1,256,2,1,256]{5,4,3,2,1,0:T(1,128)S(1)}, f32[4,1,256,2,1,256]{5,4,3,2,1,0:T(1,128)}, u32[]{:S(2)}) copy-start(f32[4,1,256,2,1,256]{5,4,3,2,1,0:T(1,128)} %param.2) | copy-start | bytes 6291460
  13.1 7.3 %collective-permute-start = (f32[32,128]{1,0:T(8,128)S(1)}, f32[32,128]{1,0:T(8,128)S(1)}, u32[]{:S(2)}, u32[]{:S(2)}) collective-permute-start(f32[32,128]{1,0:T(8,128)S(1)} %bitcast.33), channel_id=1, source_target_pairs={{0,0},{1,16},{2,32},{3,48},{4,64},{5,80},{6,96},{7,112},{8,128},{9... | collective-permute-start | bytes 49160 | tf_op jit(solution)/shard_map/panel/ppermute | solution.py:463
  18.4 4.8 %collective-permute-start.1 = (f32[32,128]{1,0:T(8,128)S(1)}, f32[32,128]{1,0:T(8,128)S(1)}, u32[]{:S(2)}, u32[]{:S(2)}) collective-permute-start(f32[32,128]{1,0:T(8,128)S(1)} %bitcast.32), channel_id=1, source_target_pairs={{0,16},{1,0},{2,48},{3,32},{4,80},{5,64},{6,112},{7,96},{8,144},{9... | collective-permute-start | bytes 49160 | tf_op jit(solution)/shard_map/panel/ppermute | solution.py:464
  64.6 0.9 copy-start.1
  66.4 29.5 %all-to-all-start.1 = ((f32[32,32,128]{2,1,0:T(8,128)}), f32[32,32,128]{2,1,0:T(8,128)}, u32[]{:S(2)}, u32[]{:S(2)}) async-start(f32[32,32,128]{2,1,0:T(8,128)} %tile.5), calls=%async_computation.1 | async-start | bytes 1048576 | tf_op jit(solution)/shard_map/gram/all_to_all | solution.py:446
  86.3 0.8 copy-start.8
  95.9 35.2 %all-to-all-start.3 = ((f32[16,16,512]{2,1,0:T(8,128)}), f32[16,16,512]{2,1,0:T(8,128)}, u32[]{:S(2)}, u32[]{:S(2)}) async-start(f32[16,16,512]{2,1,0:T(8,128)} %bitcast.27), calls=%async_computation.3 | async-start | bytes 1048576 | tf_op jit(solution)/shard_map/mirror/all_to_all | solution.py:502
  103.3 23.6 %copy-start.2 = (f32[1536,128]{1,0:T(8,128)S(1)}, f32[1536,128]{1,0:T(8,128)}, u32[]{:S(2)}) copy-start(f32[1536,128]{1,0:T(8,128)} %copy-done.1) | copy-start | bytes 2359300
  126.1 0.7 copy-start.14
  126.8 1.0 copy-start.13
  130.1 1.0 copy-start.4
  131.1 14.3 %copy-start.9 = (f32[256,256]{1,0:T(8,128)S(1)}, f32[256,256]{1,0:T(8,128)}, u32[]{:S(2)}) copy-start(f32[256,256]{1,0:T(8,128)} %get-tuple-element.31.refl_ref) | copy-start | bytes 786436
  131.1 23.8 %all-to-all-start.2 = ((f32[32,8,1024]{2,1,0:T(8,128)}), f32[32,8,1024]{2,1,0:T(8,128)}, u32[]{:S(2)}, u32[]{:S(2)}) async-start(f32[32,8,1024]{2,1,0:T(8,128)} %bitcast.26), calls=%async_computation.2 | async-start | bytes 2097152 | tf_op jit(solution)/shard_map/sums/all_to_all | solution.py:531
  138.6 13.5 %collective-permute-start.3 = (f32[8,512]{1,0:T(8,128)S(1)}, f32[8,512]{1,0:T(8,128)S(1)}, u32[]{:S(2)}, u32[]{:S(2)}) collective-permute-start(f32[8,512]{1,0:T(8,128)S(1)} %get-tuple-element.34), channel_id=1, source_target_pairs={{0,0},{16,1},{32,2},{48,3},{64,4},{80,5},{96,6},{112,7},{128,8},{1... | collective-permute-start | bytes 49160 | tf_op jit(solution)/shard_map/sums/ppermute | solution.py:471
  142.3 9.9 %collective-permute-start.2 = (f32[8,512]{1,0:T(8,128)S(1)}, f32[8,512]{1,0:T(8,128)S(1)}, u32[]{:S(2)}, u32[]{:S(2)}) collective-permute-start(f32[8,512]{1,0:T(8,128)S(1)} %get-tuple-element.35), channel_id=1, source_target_pairs={{16,0},{0,1},{48,2},{32,3},{80,4},{64,5},{112,6},{96,7},{144,8},{1... | collective-permute-start | bytes 49160 | tf_op jit(solution)/shard_map/sums/ppermute | solution.py:472
  145.4 1.1 copy-start.3
  146.5 0.9 copy-start.15
  149.7 1.0 copy-start.5
  150.6 0.8 copy-start.10
  151.5 0.7 copy-start.16
  154.9 1.2 copy-start.6
  193.4 39.9 %copy-start.7 = (f32[256,1024]{1,0:T(8,128)S(1)}, f32[256,1024]{1,0:T(8,128)}, u32[]{:S(2)}) copy-start(f32[256,1024]{1,0:T(8,128)} %copy-done.5) | copy-start | bytes 3145732
  193.4 39.8 %copy-start.11 = (f32[256,512]{1,0:T(8,128)S(1)}, f32[256,512]{1,0:T(8,128)}, u32[]{:S(2)}) copy-start(f32[256,512]{1,0:T(8,128)} %copy-done.10) | copy-start | bytes 1572868
  193.4 39.8 %copy-start.17 = (f32[256,256]{1,0:T(8,128)S(1)}, f32[256,256]{1,0:T(8,128)}, u32[]{:S(2)}) copy-start(f32[256,256]{1,0:T(8,128)} %copy-done.16) | copy-start | bytes 786436

commit v4 on v3

--- a/solution.py
+++ b/solution.py
@@ -237,9 +237,9 @@
     refl_ref[...] = a_ref[...]
 
 
-def factor_kernel(g_ref, band_ref, linv_ref, refl_ref, a_ref, u_ref, row_ref, multiplier_ref):
-    cholesky(g_ref, band_ref, linv_ref, a_ref, u_ref, row_ref, multiplier_ref)
+def reflector_kernel(g_ref, linv_ref, refl_ref, both_ref, a_ref, row_ref):
     reflector_factor(g_ref, linv_ref, refl_ref, a_ref, row_ref)
+    both_ref[...] = product(split(refl_ref[...]), split(linv_ref[...]), 0, 0)
 
 
 def tile_place(place, t, u):
@@ -252,8 +252,8 @@
     return r, c
 
 
-def mirror_kernel(place, panel_ref, matrix_ref, out_ref):
-    out_ref[...] = jnp.zeros((NB, TC * NB), F32)
+def mirror_kernel(place, panel_ref, matrix_ref, keep_ref, send_ref, sum_ref):
+    sum_ref[...] = jnp.zeros((NB, TC * NB), F32)
     for t in range(TR):
         rows = split(linear_tile(panel_ref, t))
         for u in range(TC):
@@ -262,13 +262,22 @@
 
             @pl.when(i > j)
             def _():
-                out_ref[:, here] += product(rows, split(matrix_tile(matrix_ref, t, u)))
+                sum_ref[:, here] += product(rows, split(matrix_tile(matrix_ref, t, u)))
 
             @pl.when(i == j)
             def _():
                 r, c = ordering()
                 tile = jnp.where(r > c, matrix_tile(matrix_ref, t, u), 0.0)
-                out_ref[:, here] += product(rows, split(tile))
+                sum_ref[:, here] += product(rows, split(tile))
+
+    for parity in range(2):
+
+        @pl.when(place[0] % 2 == parity)
+        def _():
+            for k in range(N_ROW // 2):
+                at = pl.ds(k * CHUNK, CHUNK)
+                keep_ref[at, :] = sum_ref[pl.ds((2 * k + parity) * CHUNK, CHUNK), :]
+                send_ref[at, :] = sum_ref[pl.ds((2 * k + 1 - parity) * CHUNK, CHUNK), :]
 
 
 def row_copies(matrix_hbm, matrix_ref, sems, first):
@@ -329,13 +338,11 @@
 
 
 def vectors_kernel(
-    place, linv_ref, refl_ref, panel_rows_ref, panel_cols_ref,
-    rows_ref, cols_ref, both_ref, vectors_ref,
+    place, linv_ref, panel_rows_ref, panel_cols_ref, rows_ref, cols_ref, vectors_ref,
 ):
     linv = split(linv_ref[...])
     r, c = ordering()
     eye = (r == c).astype(F32)
-    both_ref[...] = product(split(refl_ref[...]), linv, 0, 0)
     for u in range(TC):
         value = product(linv, split(gathered_tile(panel_cols_ref, u)))
         if u == 0:
@@ -355,7 +362,12 @@
 DEAL = (TC + 1 + TR) * SHARE
 
 
-def share_kernel(recv_ref, even_ref, odd_ref, rows_ref, out_ref):
+def share_kernel(even_ref, odd_ref, recv_hbm, rows_hbm, out_ref, recv_ref, rows_ref, sems):
+    recv_copy = pltpu.make_async_copy(recv_hbm, recv_ref, sems.at[0])
+    rows_copy = pltpu.make_async_copy(rows_hbm, rows_ref, sems.at[1])
+    recv_copy.start()
+    rows_copy.start()
+    recv_copy.wait()
     total = recv_ref[pl.ds(0, SHARE), :]
     for k in range(1, N_COL):
         total = total + recv_ref[pl.ds(k * SHARE, SHARE), :]
@@ -363,6 +375,7 @@
     total = total + jnp.concatenate(mirrored, axis=1)
     for t in range(TR):
         out_ref[pl.ds(t * SHARE, SHARE), :] = total[:, t * NB : (t + 1) * NB]
+    rows_copy.wait()
     out_ref[pl.ds(TR * SHARE, SHARE), :] = product(split(total), split(rows_ref[...]), 1, 1)
 
 
@@ -398,22 +411,34 @@
 
 
 def update_kernel(
-    place, refl_ref, both_ref, cols_ref, rows_ref, matrix_ref, dealt_hbm, out_hbm,
-    dealt_ref, out_ref, sems,
+    place, matrix_ref, both_hbm, refl_hbm, dealt_hbm, cols_hbm, rows_hbm, out_hbm,
+    both_ref, refl_ref, dealt_ref, cols_ref, rows_ref, out_ref, sems,
 ):
-    dealt_copy = pltpu.make_async_copy(dealt_hbm, dealt_ref, sems.at[0])
-    dealt_copy.start()
-    out_copies = row_copies(out_ref, out_hbm, sems, 1)
+    pairs = (
+        (both_hbm, both_ref), (refl_hbm, refl_ref), (dealt_hbm, dealt_ref),
+        (cols_hbm, cols_ref), (rows_hbm, rows_ref),
+    )
+    copies = [
+        pltpu.make_async_copy(source, target, sems.at[k])
+        for k, (source, target) in enumerate(pairs)
+    ]
+    for copy in copies:
+        copy.start()
+    out_copies = row_copies(out_ref, out_hbm, sems, len(copies))
+    copies[0].wait()
     both = split(both_ref[...])
+    copies[1].wait()
     refl = split(refl_ref[...])
-    dealt_copy.wait()
+    copies[2].wait()
     curved = split(product(both, split(dealt(dealt_ref, TC))))
     half_mixed = split(0.5 * product(curved, refl))
+    copies[3].wait()
     sides = []
     for u in range(TC):
         vectors = split(cols_ref[:, pl.ds(u * NB, NB)])
         update = product(both, split(dealt(dealt_ref, u))) - product(half_mixed, vectors)
         sides.append((vectors, split(update)))
+    copies[4].wait()
     for t in range(TR):
         here = pl.ds(t * NB, NB)
         vectors = split(rows_ref[:, here])
@@ -494,22 +519,24 @@
         summed = panel_cols.reshape(N_ROW, SPAN, LANES)[:, CHUNK * TC * 2 :].sum(0)
         gram = spread(summed, "col", N_COL)
     with jax.named_scope("mirror"):
-        (mirror,) = call(
-            mirror_kernel, [(NB, TC * NB)], n_scalars=1, n_in=2, name="mirror", moved=4 << 20
+        keep, send = call(
+            mirror_kernel, [(NB // 2, TC * NB)] * 2, scratch=[(NB, TC * NB)], n_scalars=1, n_in=2,
+            name="mirror", moved=4 << 20,
         )(place, panel_rows, stored)
+        mirror = keep + lax.ppermute(send, "row", [(r, r ^ 1) for r in range(N_ROW)])
         gram, mirror = lax.optimization_barrier((gram, mirror))
-        from_cols = (
-            lax.all_to_all(mirror, "row", 0, 0, tiled=True).reshape(N_ROW, CHUNK, TC * NB).sum(0)
-        )
+        parities = [list(range(parity, N_ROW, 2)) for parity in range(2)]
+        mirror = lax.all_to_all(mirror, "row", 0, 0, axis_index_groups=parities, tiled=True)
+        from_cols = mirror.reshape(N_ROW // 2, CHUNK, TC * NB).sum(0)
     with jax.named_scope("factor"):
-        band, linv, reflector = call(
-            factor_kernel,
-            [(NB, NB)] * 3,
+        band, linv = call(
+            cholesky,
+            [(NB, NB)] * 2,
             scratch=[(NB, NB)] * 2 + [(BS, NB)] * 2,
             n_in=1,
-            name="factor",
-            flops=10**10,
-            moved=80 << 20,
+            name="cholesky",
+            flops=5 * 10**9,
+            moved=40 << 20,
         )(gram)
     with jax.named_scope("symmetric"):
         (row_terms,) = call(
@@ -519,40 +546,59 @@
             name="symmetric", moved=4 << 20,
         )(place, band, stored, panel_cols)
     with jax.named_scope("vectors"):
-        rows, cols, both, vectors = call(
+        rows, cols, vectors = call(
             vectors_kernel,
-            [(NB, TR * NB), (NB, TC * NB), (NB, NB), (SHARE * TR * 2, LANES)],
+            [(NB, TR * NB), (NB, TC * NB), (SHARE * TR * 2, LANES)],
             n_scalars=1,
-            n_in=4,
+            n_in=3,
             name="vectors",
             moved=4 << 20,
-        )(place, linv, reflector, panel_rows, panel_cols)
+        )(place, linv, panel_rows, panel_cols)
     with jax.named_scope("sums"):
         received = lax.all_to_all(row_terms, "col", 0, 0, tiled=True)
         even, odd = to_rows(from_cols[:SHARE], from_cols[SHARE:], col_index)
-        (payload,) = call(share_kernel, [(PART, NB)], n_in=4, name="share", moved=2 << 20)(
-            received, even, odd, rows
-        )
+        (payload,) = call(
+            share_kernel, [(PART, NB)], scratch=[(NB, TR * NB)] * 2, n_in=2, n_any=2, copies=2,
+            name="share", moved=2 << 20,
+        )(even, odd, received, rows)
         parts = lax.all_gather(payload, "row", tiled=True)
     with jax.named_scope("deal"):
         (deal,) = call(
             deal_kernel, [(N_COL * DEAL, NB)], scratch=[(N_COL * DEAL, NB)], n_in=2, any_out=True,
             copies=4, name="deal", moved=3 << 20,
         )(payload, parts)
+        deal, gram, linv = lax.optimization_barrier((deal, gram, linv))
         deal = lax.all_to_all(deal, "col", 0, 0, tiled=True)
+    with jax.named_scope("reflector"):
+        reflector, both = call(
+            reflector_kernel,
+            [(NB, NB)] * 2,
+            scratch=[(NB, NB), (BS, NB)],
+            n_in=2,
+            name="reflector",
+            flops=5 * 10**9,
+            moved=40 << 20,
+        )(gram, linv)
     with jax.named_scope("update"):
         (updated,) = call(
             update_kernel,
             [(TR * NB * TC * 2, LANES)],
-            scratch=[(N_COL * DEAL, NB), (TR * NB * TC * 2, LANES)],
+            scratch=[
+                (NB, NB),
+                (NB, NB),
+                (N_COL * DEAL, NB),
+                (NB, TC * NB),
+                (NB, TR * NB),
+                (TR * NB * TC * 2, LANES),
+            ],
             n_scalars=1,
-            n_in=5,
-            n_any=1,
+            n_in=1,
+            n_any=5,
             any_out=True,
-            copies=1 + TR,
+            copies=5 + TR,
             name="update",
             moved=8 << 20,
-        )(place, reflector, both, cols, rows, stored, deal)
+        )(place, stored, both, reflector, deal, cols, rows)
     return (updated.reshape(matrix.shape), vectors.reshape(panel_t.shape), band, reflector)
 
 

time: 240 us -> 241 us (level)
  blocking collectives: 107 us -> 62.3 us
  starting transfers between devices: 56.1 us -> 80.5 us
  waiting for transfers between devices: 21.4 us -> 33.9 us
  Pallas kernels: 39.6 us -> 43.4 us
  local copies, waits for them, and re-layouts: 13 us -> 15.8 us
    all_to_all x1 -> x0, blocking collectives: 39.8 us -> none  [body(): deal = lax.all_to_all(deal, 'col', 0, 0, tiled=True)]
    all_to_all x1 -> x2, starting transfers between devices: 7.39 us -> 24.6 us  [the longest x1 16.9 us: body(): deal = lax.all_to_all(deal, 'col', 0, 0, tiled=True)]
    all_to_all x1 -> x2, waiting for transfers between devices: 0.01 us -> 12.4 us  [the longest x1 12.4 us: body(): deal = lax.all_to_all(deal, 'col', 0, 0, tiled=True)]
    all_to_all x2, waiting for transfers between devices: 16 us -> 7.16 us  [spread(): return lax.all_to_all(jnp.tile(value, (count, 1)), axis, 0, 0, tiled=True)]
    ppermute x0 -> x1, waiting for transfers between devices: none -> 5.88 us  [body(): lax.ppermute(send, 'row', [(r, r ^ 1) for r in range(N_ROW)])]
    all_gather x1, blocking collectives: 34.3 us -> 29.5 us  [body(): parts = lax.all_gather(payload, 'row', tiled=True)]
    all_to_all x1, starting transfers between devices: 6.44 us -> 11 us  [body(): received = lax.all_to_all(row_terms, 'col', 0, 0, tiled=True)]
    pallas_call x5 -> x6, Pallas kernels: 34.6 us -> 38.4 us  [the longest x1 13.5 us: body(): call(cholesky, [(NB, NB)] * 2, scratch=[(NB, NB)] * 2 + [(BS, NB)] * 2, n...]
  transfers between devices with their start and end apart: 8 -> 10, of which waited for: 4 -> 6; matrix products, arithmetic and copies ran while one was open for 0% -> 1% of each run, Pallas kernels for 12% -> 13%
where the time goes in v4:
time: 241 us; the launch traced here: 239 us
  starting transfers between devices  80.5 us (33%)
  blocking collectives  62.3 us (26%)
  Pallas kernels  43.4 us (18%)
  waiting for transfers between devices  33.9 us (14%)
  local copies, waits for them, and re-layouts  15.8 us (7%)
    all_gather x1, blocking collectives, body(): panel_cols = lax.all_gather(payload, 'row', tiled=True)  32.8 us
    all_gather x1, blocking collectives, body(): parts = lax.all_gather(payload, 'row', tiled=True)  29.5 us
    all_to_all x2, starting transfers between devices, spread(): return lax.all_to_all(jnp.tile(value, (count, 1)), axis, 0, 0, tiled=True)  28.4 us
    all_to_all x1, starting transfers between devices, body(): deal = lax.all_to_all(deal, 'col', 0, 0, tiled=True)  16.9 us
    pallas_call x1, Pallas kernels, body(): call(cholesky, [(NB, NB)] * 2, scratch=[(NB, NB)] * 2 + [(BS, NB)] * 2, n...  13.5 us
    unnamed x32, local copies, waits for them, and re-layouts  13 us
    all_to_all x1, waiting for transfers between devices, body(): deal = lax.all_to_all(deal, 'col', 0, 0, tiled=True)  12.4 us
    pallas_call x1, Pallas kernels, body(): call(reflector_kernel, [(NB, NB)] * 2, scratch=[(NB, NB), (BS, NB)], n_in...  11.5 us
  transfers between devices with their start and end apart: 10, of which 6 were waited for; matrix products, arithmetic and copies ran while one was open for 1% of the time, Pallas kernels for 13%

profile of v4, /device:TPU:1, one launch (start us, length us, event | category | flops | bytes accessed | tf_op | source)
XLA Modules:
  0.0 238.7 jit_solution(17126327728449038851)
XLA Ops:
  0.6 0.0 copy-start.11
  0.6 1.9 tile.4
  2.5 10.5 %all-to-all-start = ((f32[32,64,128]{2,1,0:T(8,128)}), f32[32,64,128]{2,1,0:T(8,128)S(1)}, u32[]{:S(2)}, u32[]{:S(2)}) async-start(f32[32,64,128]{2,1,0:T(8,128)} %tile.4), calls=%async_computation | async-start | bytes 2097152 | tf_op jit(solution)/shard_map/panel/all_to_all | solution.py:471
  13.0 0.0 copy-start
  13.0 0.0 copy-done.11
  13.1 5.3 %collective-permute-start = (f32[32,128]{1,0:T(8,128)S(1)}, f32[32,128]{1,0:T(8,128)S(1)}, u32[]{:S(2)}, u32[]{:S(2)}) collective-permute-start(f32[32,128]{1,0:T(8,128)S(1)} %bitcast.31), channel_id=1, source_target_pairs={{0,0},{1,16},{2,32},{3,48},{4,64},{5,80},{6,96},{7,112},{8,128},{9... | collective-permute-start | bytes 49160 | tf_op jit(solution)/shard_map/panel/ppermute | solution.py:488
  18.4 1.9 collective-permute-start.1
  20.3 0.1 pad_add_fusion.place
  20.4 0.0 collective-permute-done
  20.4 2.8 %collective-permute-done.1 = f32[32,128]{1,0:T(8,128)S(1)} collective-permute-done((f32[32,128]{1,0:T(8,128)S(1)}, f32[32,128]{1,0:T(8,128)S(1)}, u32[]{:S(2)}, u32[]{:S(2)}) %collective-permute-start.1) | collective-permute-done | bytes 16416 | tf_op jit(solution)/shard_map/panel/ppermute | solution.py:489
  23.1 7.2 %all-to-all-done = f32[32,64,128]{2,1,0:T(8,128)S(1)} async-done(((f32[32,64,128]{2,1,0:T(8,128)}), f32[32,64,128]{2,1,0:T(8,128)S(1)}, u32[]{:S(2)}, u32[]{:S(2)}) %all-to-all-start) | async-done | bytes 1048608 | tf_op jit(solution)/shard_map/panel/all_to_all | solution.py:471
  30.3 1.5 gram.1
  31.8 32.8 %all_gather.6.panel_hbm.panel_cols_ref = f32[1536,128]{1,0:T(8,128)S(1)} all-gather(f32[96,128]{1,0:T(8,128)S(1)} %gram.1), channel_id=1, replica_groups=mesh['row'=16,'col'=32] {'row'}, dimensions={0}, use_global_device_ids=true | all-gather | bytes 835584 | tf_op jit(solution)/shard_map/gram/all_gather | solution.py:518
  64.6 0.0 copy-start.1
  64.6 0.9 copy-done.1
  65.5 0.9 tile.5
  66.3 17.9 %all-to-all-start.1 = ((f32[32,32,128]{2,1,0:T(8,128)}), f32[32,32,128]{2,1,0:T(8,128)}, u32[]{:S(2)}, u32[]{:S(2)}) async-start(f32[32,32,128]{2,1,0:T(8,128)} %tile.5), calls=%async_computation.1 | async-start | bytes 1048576 | tf_op jit(solution)/shard_map/gram/all_to_all | solution.py:471
  84.3 0.0 copy-done
  84.3 2.0 mirror.1
  86.3 3.7 %collective-permute-start.2 = (f32[128,512]{1,0:T(8,128)S(1)}, f32[128,512]{1,0:T(8,128)S(1)}, u32[]{:S(2)}, u32[]{:S(2)}) collective-permute-start(f32[128,512]{1,0:T(8,128)S(1)} %get-tuple-element.25), channel_id=1, source_target_pairs={{0,32},{32,0},{64,96},{96,64},{128,160},{160,128},{192,224},{224,1... | collective-permute-start | bytes 786440 | tf_op jit(solution)/shard_map/mirror/ppermute | solution.py:526
  90.0 5.9 %collective-permute-done.2 = f32[128,512]{1,0:T(8,128)S(1)} collective-permute-done((f32[128,512]{1,0:T(8,128)S(1)}, f32[128,512]{1,0:T(8,128)S(1)}, u32[]{:S(2)}, u32[]{:S(2)}) %collective-permute-start.2) | collective-permute-done | bytes 262176 | tf_op jit(solution)/shard_map/mirror/ppermute | solution.py:526
  95.9 0.7 add.9
  96.7 0.0 all-to-all-done.1
  96.7 7.6 %all-to-all-start.2 = ((f32[8,16,512]{2,1,0:T(8,128)}), f32[8,16,512]{2,1,0:T(8,128)}, u32[]{:S(2)}, u32[]{:S(2)}) async-start(f32[8,16,512]{2,1,0:T(8,128)} %bitcast.10), calls=%async_computation.2 | async-start | bytes 524288 | tf_op jit(solution)/shard_map/mirror/all_to_all | solution.py:529
  104.3 0.0 copy-start.2
  104.3 13.5 %cholesky.1 = (f32[256,256]{1,0:T(8,128)}, f32[256,256]{1,0:T(8,128)S(1)}) custom-call(f32[1024,128]{1,0:T(8,128)} %bitcast.9.g_ref), custom_call_target="tpu_custom_call" | custom-call | flops 5000000000 | bytes 41943040 | tf_op jit(solution)/shard_map/factor/cholesky/pallas_call | solution.py:532
  117.8 0.0 copy-done.2
  117.8 0.0 copy-start.12
  117.8 0.9 copy-done.12
  118.7 2.3 symmetric.1
  121.0 0.0 copy-start.5
  121.1 1.0 copy-done.5
  122.0 0.0 all-to-all-done.2
  122.0 11.0 %all-to-all-start.3 = ((f32[32,8,1024]{2,1,0:T(8,128)}), f32[32,8,1024]{2,1,0:T(8,128)}, u32[]{:S(2)}, u32[]{:S(2)}) async-start(f32[32,8,1024]{2,1,0:T(8,128)} %bitcast.25), calls=%async_computation.3 | async-start | bytes 2097152 | tf_op jit(solution)/shard_map/sums/all_to_all | solution.py:558
  133.0 1.0 reduce_sum.19
  134.0 2.1 collective-permute-start.4
  136.1 3.5 %collective-permute-start.3 = (f32[8,512]{1,0:T(8,128)S(1)}, f32[8,512]{1,0:T(8,128)S(1)}, u32[]{:S(2)}, u32[]{:S(2)}) collective-permute-start(f32[8,512]{1,0:T(8,128)S(1)} %get-tuple-element.45), channel_id=1, source_target_pairs={{16,0},{0,1},{48,2},{32,3},{80,4},{64,5},{112,6},{96,7},{144,8},{1... | collective-permute-start | bytes 49160 | tf_op jit(solution)/shard_map/sums/ppermute | solution.py:497
  139.6 0.0 copy-start.3
  139.6 1.1 copy-done.3
  140.8 2.1 vectors.1
  142.8 0.0 copy-start.6
  142.8 1.0 copy-done.6
  143.8 0.0 copy-start.9
  143.8 0.8 copy-done.9
  144.6 0.3 collective-permute-done.4
  144.8 0.0 collective-permute-done.3
  144.9 5.4 %all-to-all-done.3 = f32[32,8,1024]{2,1,0:T(8,128)} async-done(((f32[32,8,1024]{2,1,0:T(8,128)}), f32[32,8,1024]{2,1,0:T(8,128)}, u32[]{:S(2)}, u32[]{:S(2)}) %all-to-all-start.3) | async-done | bytes 1048608 | tf_op jit(solution)/shard_map/sums/all_to_all | solution.py:558
  150.3 0.0 copy-start.7
  150.3 1.2 copy-done.7
  151.5 1.8 share.1.own_ref
  153.3 29.5 %all_gather.7.part_ref = f32[640,256]{1,0:T(8,128)S(1)} all-gather(f32[40,256]{1,0:T(8,128)S(1)} %share.1.own_ref), channel_id=1, replica_groups=mesh['row'=16,'col'=32] {'row'}, dimensions={0}, use_global_device_ids=true | all-gather | bytes 696320 | tf_op jit(solution)/shard_map/sums/all_gather | solution.py:564
  182.8 1.3 deal.1
  184.1 0.0 copy-start.4
  184.1 1.2 copy-done.4
  185.3 16.9 %all-to-all-start.4 = ((f32[32,56,256]{2,1,0:T(8,128)}), f32[32,56,256]{2,1,0:T(8,128)}, u32[]{:S(2)}, u32[]{:S(2)}) async-start(f32[32,56,256]{2,1,0:T(8,128)} %bitcast.24), calls=%async_computation.4 | async-start | bytes 3670016 | tf_op jit(solution)/shard_map/deal/all_to_all | solution.py:571
  202.3 11.5 %reflector.1 = (f32[256,256]{1,0:T(8,128)}, f32[256,256]{1,0:T(8,128)S(1)}) custom-call(f32[1024,128]{1,0:T(8,128)} %bitcast.9.g_ref, f32[256,256]{1,0:T(8,128)S(1)} %get-tuple-element.32.linv_ref), custom_call_target="tpu_custom_call" | custom-call | flops 5000000000 | bytes 41943040 | tf_op jit(solution)/shard_map/reflector/reflector/pallas_call | solution.py:573
  213.8 0.0 copy-start.14
  213.8 0.7 copy-done.14
  214.5 12.4 %all-to-all-done.4 = f32[32,56,256]{2,1,0:T(8,128)} async-done(((f32[32,56,256]{2,1,0:T(8,128)}), f32[32,56,256]{2,1,0:T(8,128)}, u32[]{:S(2)}, u32[]{:S(2)}) %all-to-all-start.4) | async-done | bytes 1835040 | tf_op jit(solution)/shard_map/deal/all_to_all | solution.py:571
  226.9 1.2 copy-done.8
  228.1 1.0 copy-done.10
  229.2 0.9 copy-done.13
  230.1 0.9 copy-done.15
  231.1 7.5 %update.1 = f32[4096,128]{1,0:T(8,128)} custom-call(s32[2]{0:T(128)S(1)} %pad_add_fusion.place, f32[4096,128]{1,0:T(8,128)S(1)} %bitcast.19, f32[256,256]{1,0:T(8,128)S(1)} %copy-done.15, f32[256,256]{1,0:T(8,128)S(1)} %copy-done.13, f32[1792,256]{1,0:T(8,128)} %bitcast.14.dealt_hbm, f32[256,512]{1,0:T(8,128)S(1)} %copy-done.10, f32[256,1024]{1,0:T(8,128)S(1)} %copy-done.8), custom_call_target="tpu_custom_call" | custom-call | bytes 8388608 | tf_op jit(solution)/shard_map/update/update/pallas_call | solution.py:583
  (9 shorter events, 0.1 us)
Async XLA Ops:
  0.6 12.4 %copy-start.11 = (f32[8,4,1,256]{3,2,1,0:T(1,128)S(1)}, f32[8,4,1,256]{3,2,1,0:T(1,128)}, u32[]{:S(2)}) copy-start(f32[8,4,1,256]{3,2,1,0:T(1,128)} %param.3) | copy-start | bytes 98308
  2.5 27.8 %all-to-all-start = ((f32[32,64,128]{2,1,0:T(8,128)}), f32[32,64,128]{2,1,0:T(8,128)S(1)}, u32[]{:S(2)}, u32[]{:S(2)}) async-start(f32[32,64,128]{2,1,0:T(8,128)} %tile.4), calls=%async_computation | async-start | bytes 2097152 | tf_op jit(solution)/shard_map/panel/all_to_all | solution.py:471
  13.0 71.2 %copy-start = (f32[4,1,256,2,1,256]{5,4,3,2,1,0:T(1,128)S(1)}, f32[4,1,256,2,1,256]{5,4,3,2,1,0:T(1,128)}, u32[]{:S(2)}) copy-start(f32[4,1,256,2,1,256]{5,4,3,2,1,0:T(1,128)} %param.2) | copy-start | bytes 6291460
  13.1 7.3 %collective-permute-start = (f32[32,128]{1,0:T(8,128)S(1)}, f32[32,128]{1,0:T(8,128)S(1)}, u32[]{:S(2)}, u32[]{:S(2)}) collective-permute-start(f32[32,128]{1,0:T(8,128)S(1)} %bitcast.31), channel_id=1, source_target_pairs={{0,0},{1,16},{2,32},{3,48},{4,64},{5,80},{6,96},{7,112},{8,128},{9... | collective-permute-start | bytes 49160 | tf_op jit(solution)/shard_map/panel/ppermute | solution.py:488
  18.4 4.8 %collective-permute-start.1 = (f32[32,128]{1,0:T(8,128)S(1)}, f32[32,128]{1,0:T(8,128)S(1)}, u32[]{:S(2)}, u32[]{:S(2)}) collective-permute-start(f32[32,128]{1,0:T(8,128)S(1)} %bitcast.30), channel_id=1, source_target_pairs={{0,16},{1,0},{2,48},{3,32},{4,80},{5,64},{6,112},{7,96},{8,144},{9... | collective-permute-start | bytes 49160 | tf_op jit(solution)/shard_map/panel/ppermute | solution.py:489
  64.6 0.9 copy-start.1
  66.3 30.3 %all-to-all-start.1 = ((f32[32,32,128]{2,1,0:T(8,128)}), f32[32,32,128]{2,1,0:T(8,128)}, u32[]{:S(2)}, u32[]{:S(2)}) async-start(f32[32,32,128]{2,1,0:T(8,128)} %tile.5), calls=%async_computation.1 | async-start | bytes 1048576 | tf_op jit(solution)/shard_map/gram/all_to_all | solution.py:471
  86.3 9.6 %collective-permute-start.2 = (f32[128,512]{1,0:T(8,128)S(1)}, f32[128,512]{1,0:T(8,128)S(1)}, u32[]{:S(2)}, u32[]{:S(2)}) collective-permute-start(f32[128,512]{1,0:T(8,128)S(1)} %get-tuple-element.25), channel_id=1, source_target_pairs={{0,32},{32,0},{64,96},{96,64},{128,160},{160,128},{192,224},{224,1... | collective-permute-start | bytes 786440 | tf_op jit(solution)/shard_map/mirror/ppermute | solution.py:526
  96.7 25.4 %all-to-all-start.2 = ((f32[8,16,512]{2,1,0:T(8,128)}), f32[8,16,512]{2,1,0:T(8,128)}, u32[]{:S(2)}, u32[]{:S(2)}) async-start(f32[8,16,512]{2,1,0:T(8,128)} %bitcast.10), calls=%async_computation.2 | async-start | bytes 524288 | tf_op jit(solution)/shard_map/mirror/all_to_all | solution.py:529
  104.3 13.5 %copy-start.2 = (f32[1536,128]{1,0:T(8,128)S(1)}, f32[1536,128]{1,0:T(8,128)}, u32[]{:S(2)}) copy-start(f32[1536,128]{1,0:T(8,128)} %copy-done.1) | copy-start | bytes 2359300
  117.8 1.0 copy-start.12
  121.0 1.0 copy-start.5
  122.0 28.2 %all-to-all-start.3 = ((f32[32,8,1024]{2,1,0:T(8,128)}), f32[32,8,1024]{2,1,0:T(8,128)}, u32[]{:S(2)}, u32[]{:S(2)}) async-start(f32[32,8,1024]{2,1,0:T(8,128)} %bitcast.25), calls=%async_computation.3 | async-start | bytes 2097152 | tf_op jit(solution)/shard_map/sums/all_to_all | solution.py:558
  134.0 10.8 %collective-permute-start.4 = (f32[8,512]{1,0:T(8,128)S(1)}, f32[8,512]{1,0:T(8,128)S(1)}, u32[]{:S(2)}, u32[]{:S(2)}) collective-permute-start(f32[8,512]{1,0:T(8,128)S(1)} %get-tuple-element.44), channel_id=1, source_target_pairs={{0,0},{16,1},{32,2},{48,3},{64,4},{80,5},{96,6},{112,7},{128,8},{1... | collective-permute-start | bytes 49160 | tf_op jit(solution)/shard_map/sums/ppermute | solution.py:496
  136.1 8.8 %collective-permute-start.3 = (f32[8,512]{1,0:T(8,128)S(1)}, f32[8,512]{1,0:T(8,128)S(1)}, u32[]{:S(2)}, u32[]{:S(2)}) collective-permute-start(f32[8,512]{1,0:T(8,128)S(1)} %get-tuple-element.45), channel_id=1, source_target_pairs={{16,0},{0,1},{48,2},{32,3},{80,4},{64,5},{112,6},{96,7},{144,8},{1... | collective-permute-start | bytes 49160 | tf_op jit(solution)/shard_map/sums/ppermute | solution.py:497
  139.6 1.1 copy-start.3
  142.8 1.0 copy-start.6
  143.8 0.8 copy-start.9
  150.3 1.2 copy-start.7
  184.1 1.2 copy-start.4
  185.3 41.6 %all-to-all-start.4 = ((f32[32,56,256]{2,1,0:T(8,128)}), f32[32,56,256]{2,1,0:T(8,128)}, u32[]{:S(2)}, u32[]{:S(2)}) async-start(f32[32,56,256]{2,1,0:T(8,128)} %bitcast.24), calls=%async_computation.4 | async-start | bytes 3670016 | tf_op jit(solution)/shard_map/deal/all_to_all | solution.py:571
  213.8 0.7 copy-start.14
  226.9 1.2 copy-start.8
  228.1 1.0 copy-start.10
  229.2 0.9 copy-start.13
  230.1 0.9 copy-start.15

commit v5 on v4

--- a/solution.py
+++ b/solution.py
@@ -24,7 +24,7 @@
 
 def call(
     kernel, outs, scratch=(), n_scalars=0, n_in=1, n_any=0, any_out=False, copies=0,
-    name=None, flops=0, moved=0,
+    name=None, flops=0, moved=0, megabytes=40,
 ):
     buffers = [pltpu.VMEM(shape, F32) for shape in scratch]
     if copies:
@@ -35,7 +35,7 @@
         in_specs=[SMEM] * n_scalars + [VMEM] * n_in + [ANY] * n_any,
         out_specs=[ANY if any_out else VMEM] * len(outs),
         scratch_shapes=buffers,
-        compiler_params=pltpu.CompilerParams(vmem_limit_bytes=40 * 2**20),
+        compiler_params=pltpu.CompilerParams(vmem_limit_bytes=megabytes * 2**20),
         cost_estimate=pl.CostEstimate(flops=flops, bytes_accessed=moved, transcendentals=0),
         name=name,
     )
@@ -158,7 +158,7 @@
     return [jnp.broadcast_to(first[:, k : k + 1], (BS, LANES)) for k in range(BS)]
 
 
-def cholesky(g_ref, band_ref, linv_ref, a_ref, u_ref, row_ref, multiplier_ref):
+def cholesky(g_ref, band_ref, linv_ref, upper_ref, a_ref, u_ref, row_ref, multiplier_ref):
     rows, lanes, wide = block_iotas()
     full_row, full_col = ordering()
     unturned(gathered_columns(g_ref, (0, 1)), a_ref, row_ref)
@@ -199,6 +199,7 @@
     turn(a_ref, a_ref[...], row_ref[...])
     linv_ref[...] = jnp.where(full_col <= full_row, a_ref[...], 0.0)
     band_ref[...] = -u_ref[...]
+    upper_ref[...] = u_ref[...]
 
 
 def reflector_factor(g_ref, linv_ref, refl_ref, a_ref, row_ref):
@@ -292,12 +293,12 @@
 
 
 def symmetric_kernel(
-    place, band_ref, matrix_ref, panel_hbm, out_hbm, panel_ref, out_ref, sems
+    place, upper_ref, matrix_ref, panel_hbm, out_hbm, panel_ref, out_ref, sems
 ):
     panel_copy = pltpu.make_async_copy(panel_hbm, panel_ref, sems.at[0])
     panel_copy.start()
     out_copies = []
-    factor = -jnp.transpose(band_ref[...])
+    factor = jnp.transpose(upper_ref[...])
     out_ref[...] = jnp.zeros((NB, TR * NB), F32)
     panel_copy.wait()
     cols = []
@@ -411,8 +412,8 @@
 
 
 def update_kernel(
-    place, matrix_ref, both_hbm, refl_hbm, dealt_hbm, cols_hbm, rows_hbm, out_hbm,
-    both_ref, refl_ref, dealt_ref, cols_ref, rows_ref, out_ref, sems,
+    place, both_hbm, refl_hbm, dealt_hbm, cols_hbm, rows_hbm, matrix_hbm, out_hbm,
+    both_ref, refl_ref, dealt_ref, cols_ref, rows_ref, matrix_ref, out_ref, sems,
 ):
     pairs = (
         (both_hbm, both_ref), (refl_hbm, refl_ref), (dealt_hbm, dealt_ref),
@@ -422,9 +423,10 @@
         pltpu.make_async_copy(source, target, sems.at[k])
         for k, (source, target) in enumerate(pairs)
     ]
-    for copy in copies:
+    matrix_copies = row_copies(matrix_hbm, matrix_ref, sems, len(copies))
+    out_copies = row_copies(out_ref, out_hbm, sems, len(copies) + TR)
+    for copy in copies + matrix_copies:
         copy.start()
-    out_copies = row_copies(out_ref, out_hbm, sems, len(copies))
     copies[0].wait()
     both = split(both_ref[...])
     copies[1].wait()
@@ -447,6 +449,8 @@
         )
         for u in range(TC):
             i, j = tile_place(place, t, u)
+            if u == 0:
+                matrix_copies[t].wait()
 
             @pl.when(i >= j)
             def _():
@@ -529,9 +533,9 @@
         mirror = lax.all_to_all(mirror, "row", 0, 0, axis_index_groups=parities, tiled=True)
         from_cols = mirror.reshape(N_ROW // 2, CHUNK, TC * NB).sum(0)
     with jax.named_scope("factor"):
-        band, linv = call(
+        band, linv, upper = call(
             cholesky,
-            [(NB, NB)] * 2,
+            [(NB, NB)] * 3,
             scratch=[(NB, NB)] * 2 + [(BS, NB)] * 2,
             n_in=1,
             name="cholesky",
@@ -544,7 +548,7 @@
             scratch=[(N_ROW * SPAN, LANES), (NB, TR * NB)],
             n_scalars=1, n_in=2, n_any=1, any_out=True, copies=1 + TR,
             name="symmetric", moved=4 << 20,
-        )(place, band, stored, panel_cols)
+        )(place, upper, stored, panel_cols)
     with jax.named_scope("vectors"):
         rows, cols, vectors = call(
             vectors_kernel,
@@ -559,7 +563,7 @@
         even, odd = to_rows(from_cols[:SHARE], from_cols[SHARE:], col_index)
         (payload,) = call(
             share_kernel, [(PART, NB)], scratch=[(NB, TR * NB)] * 2, n_in=2, n_any=2, copies=2,
-            name="share", moved=2 << 20,
+            name="share", moved=2 << 20, megabytes=60,
         )(even, odd, received, rows)
         parts = lax.all_gather(payload, "row", tiled=True)
     with jax.named_scope("deal"):
@@ -590,15 +594,17 @@
                 (NB, TC * NB),
                 (NB, TR * NB),
                 (TR * NB * TC * 2, LANES),
+                (TR * NB * TC * 2, LANES),
             ],
             n_scalars=1,
-            n_in=1,
-            n_any=5,
+            n_in=0,
+            n_any=6,
             any_out=True,
-            copies=5 + TR,
+            copies=5 + 2 * TR,
+            megabytes=60,
             name="update",
             moved=8 << 20,
-        )(place, stored, both, reflector, deal, cols, rows)
+        )(place, both, reflector, deal, cols, rows, stored)
     return (updated.reshape(matrix.shape), vectors.reshape(panel_t.shape), band, reflector)
 
 

time: 241 us -> 238 us (0.988)
  local copies, waits for them, and re-layouts: 15.8 us -> 9.11 us
    unnamed x32 -> x24, local copies, waits for them, and re-layouts: 13 us -> 6.34 us
where the time goes in v5:
time: 238 us; the launch traced here: 236 us
  starting transfers between devices  80.5 us (34%)
  blocking collectives  63.1 us (27%)
  Pallas kernels  45.4 us (19%)
  waiting for transfers between devices  34.8 us (15%)
  local copies, waits for them, and re-layouts  9.11 us (4%)
  other arithmetic  2.45 us (1%)
    all_gather x1, blocking collectives, body(): panel_cols = lax.all_gather(payload, 'row', tiled=True)  32.8 us
    all_gather x1, blocking collectives, body(): parts = lax.all_gather(payload, 'row', tiled=True)  30.3 us
    all_to_all x2, starting transfers between devices, spread(): return lax.all_to_all(jnp.tile(value, (count, 1)), axis, 0, 0, tiled=True)  28.4 us
    all_to_all x1, starting transfers between devices, body(): deal = lax.all_to_all(deal, 'col', 0, 0, tiled=True)  16.1 us
    pallas_call x1, Pallas kernels, body(): call(cholesky, [(NB, NB)] * 3, scratch=[(NB, NB)] * 2 + [(BS, NB)] * 2, n...  13.5 us
    all_to_all x1, waiting for transfers between devices, body(): deal = lax.all_to_all(deal, 'col', 0, 0, tiled=True)  12.7 us
    all_to_all x1, starting transfers between devices, body(): received = lax.all_to_all(row_terms, 'col', 0, 0, tiled=True)  12 us
    pallas_call x1, Pallas kernels, body(): call(reflector_kernel, [(NB, NB)] * 2, scratch=[(NB, NB), (BS, NB)], n_in...  11.5 us
  transfers between devices with their start and end apart: 10, of which 6 were waited for; matrix products, arithmetic and copies ran while one was open for 1% of the time, Pallas kernels for 13%

profile of v5, /device:TPU:1, one launch (start us, length us, event | category | flops | bytes accessed | tf_op | source)
XLA Modules:
  0.0 236.4 jit_solution(16660427500587436050)
XLA Ops:
  0.6 0.0 copy-start.8
  0.6 1.9 tile.4
  2.5 10.5 %all-to-all-start = ((f32[32,64,128]{2,1,0:T(8,128)}), f32[32,64,128]{2,1,0:T(8,128)S(1)}, u32[]{:S(2)}, u32[]{:S(2)}) async-start(f32[32,64,128]{2,1,0:T(8,128)} %tile.4), calls=%async_computation | async-start | bytes 2097152 | tf_op jit(solution)/shard_map/panel/all_to_all | solution.py:475
  13.0 0.0 copy-start
  13.0 0.0 copy-done.8
  13.1 5.3 %collective-permute-start = (f32[32,128]{1,0:T(8,128)S(1)}, f32[32,128]{1,0:T(8,128)S(1)}, u32[]{:S(2)}, u32[]{:S(2)}) collective-permute-start(f32[32,128]{1,0:T(8,128)S(1)} %bitcast.31), channel_id=1, source_target_pairs={{0,0},{1,16},{2,32},{3,48},{4,64},{5,80},{6,96},{7,112},{8,128},{9... | collective-permute-start | bytes 49160 | tf_op jit(solution)/shard_map/panel/ppermute | solution.py:492
  18.4 1.9 collective-permute-start.1
  20.3 0.1 pad_add_fusion.place
  20.4 0.0 copy-start.10
  20.4 0.0 collective-permute-done
  20.4 2.8 %collective-permute-done.1 = f32[32,128]{1,0:T(8,128)S(1)} collective-permute-done((f32[32,128]{1,0:T(8,128)S(1)}, f32[32,128]{1,0:T(8,128)S(1)}, u32[]{:S(2)}, u32[]{:S(2)}) %collective-permute-start.1) | collective-permute-done | bytes 16416 | tf_op jit(solution)/shard_map/panel/ppermute | solution.py:493
  23.1 7.2 %all-to-all-done = f32[32,64,128]{2,1,0:T(8,128)S(1)} async-done(((f32[32,64,128]{2,1,0:T(8,128)}), f32[32,64,128]{2,1,0:T(8,128)S(1)}, u32[]{:S(2)}, u32[]{:S(2)}) %all-to-all-start) | async-done | bytes 1048608 | tf_op jit(solution)/shard_map/panel/all_to_all | solution.py:475
  30.3 1.5 gram.1
  31.8 32.8 %all_gather.6.panel_hbm.panel_cols_ref = f32[1536,128]{1,0:T(8,128)S(1)} all-gather(f32[96,128]{1,0:T(8,128)S(1)} %gram.1), channel_id=1, replica_groups=mesh['row'=16,'col'=32] {'row'}, dimensions={0}, use_global_device_ids=true | all-gather | bytes 835584 | tf_op jit(solution)/shard_map/gram/all_gather | solution.py:522
  64.6 0.0 copy-start.1
  64.6 0.9 copy-done.1
  65.5 0.9 tile.5
  66.3 17.9 %all-to-all-start.1 = ((f32[32,32,128]{2,1,0:T(8,128)}), f32[32,32,128]{2,1,0:T(8,128)}, u32[]{:S(2)}, u32[]{:S(2)}) async-start(f32[32,32,128]{2,1,0:T(8,128)} %tile.5), calls=%async_computation.1 | async-start | bytes 1048576 | tf_op jit(solution)/shard_map/gram/all_to_all | solution.py:475
  84.2 0.0 copy-done
  84.3 2.0 mirror.1
  86.3 3.7 %collective-permute-start.2 = (f32[128,512]{1,0:T(8,128)S(1)}, f32[128,512]{1,0:T(8,128)S(1)}, u32[]{:S(2)}, u32[]{:S(2)}) collective-permute-start(f32[128,512]{1,0:T(8,128)S(1)} %get-tuple-element.26), channel_id=1, source_target_pairs={{0,32},{32,0},{64,96},{96,64},{128,160},{160,128},{192,224},{224,1... | collective-permute-start | bytes 786440 | tf_op jit(solution)/shard_map/mirror/ppermute | solution.py:530
  90.0 5.9 %collective-permute-done.2 = f32[128,512]{1,0:T(8,128)S(1)} collective-permute-done((f32[128,512]{1,0:T(8,128)S(1)}, f32[128,512]{1,0:T(8,128)S(1)}, u32[]{:S(2)}, u32[]{:S(2)}) %collective-permute-start.2) | collective-permute-done | bytes 262176 | tf_op jit(solution)/shard_map/mirror/ppermute | solution.py:530
  95.9 0.7 add.9
  96.6 0.0 all-to-all-done.1
  96.6 7.6 %all-to-all-start.2 = ((f32[8,16,512]{2,1,0:T(8,128)}), f32[8,16,512]{2,1,0:T(8,128)}, u32[]{:S(2)}, u32[]{:S(2)}) async-start(f32[8,16,512]{2,1,0:T(8,128)} %bitcast.10), calls=%async_computation.2 | async-start | bytes 524288 | tf_op jit(solution)/shard_map/mirror/all_to_all | solution.py:533
  104.3 0.0 copy-start.2
  104.3 13.5 %cholesky.1 = (f32[256,256]{1,0:T(8,128)}, f32[256,256]{1,0:T(8,128)S(1)}, f32[256,256]{1,0:T(8,128)S(1)}) custom-call(f32[1024,128]{1,0:T(8,128)} %bitcast.8.g_ref), custom_call_target="tpu_custom_call" | custom-call | flops 5000000000 | bytes 41943040 | tf_op jit(solution)/shard_map/factor/cholesky/pallas_call | solution.py:536
  117.8 0.0 copy-done.2
  117.8 2.3 symmetric.1
  120.1 0.0 copy-start.4
  120.1 1.0 copy-done.4
  121.0 0.0 copy-start.3
  121.0 0.0 all-to-all-done.2
  121.0 12.0 %all-to-all-start.3 = ((f32[32,8,1024]{2,1,0:T(8,128)}), f32[32,8,1024]{2,1,0:T(8,128)}, u32[]{:S(2)}, u32[]{:S(2)}) async-start(f32[32,8,1024]{2,1,0:T(8,128)} %bitcast.24), calls=%async_computation.3 | async-start | bytes 2097152 | tf_op jit(solution)/shard_map/sums/all_to_all | solution.py:562
  133.0 1.0 reduce_sum.19
  134.0 2.0 collective-permute-start.4
  136.1 3.5 %collective-permute-start.3 = (f32[8,512]{1,0:T(8,128)S(1)}, f32[8,512]{1,0:T(8,128)S(1)}, u32[]{:S(2)}, u32[]{:S(2)}) collective-permute-start(f32[8,512]{1,0:T(8,128)S(1)} %get-tuple-element.47), channel_id=1, source_target_pairs={{16,0},{0,1},{48,2},{32,3},{80,4},{64,5},{112,6},{96,7},{144,8},{1... | collective-permute-start | bytes 49160 | tf_op jit(solution)/shard_map/sums/ppermute | solution.py:501
  139.6 0.0 copy-done.10
  139.6 0.0 copy-done.3
  139.6 2.1 vectors.1
  141.7 0.0 copy-start.5
  141.7 1.0 copy-done.5
  142.6 0.0 copy-start.6
  142.7 0.8 copy-done.6
  143.4 1.4 collective-permute-done.4
  144.8 0.0 collective-permute-done.3
  144.8 0.6 broadcast_select_fusion.4
  145.4 4.8 %all-to-all-done.3 = f32[32,8,1024]{2,1,0:T(8,128)} async-done(((f32[32,8,1024]{2,1,0:T(8,128)}), f32[32,8,1024]{2,1,0:T(8,128)}, u32[]{:S(2)}, u32[]{:S(2)}) %all-to-all-start.3) | async-done | bytes 1048608 | tf_op jit(solution)/shard_map/sums/all_to_all | solution.py:562
  150.2 3.4 %share.1.own_ref = f32[40,256]{1,0:T(8,128)} custom-call(f32[8,512]{1,0:T(8,128)} %get-tuple-element.45.even_ref, f32[8,512]{1,0:T(8,128)} %get-tuple-element.44.odd_ref, f32[256,1024]{1,0:T(8,128)} %bitcast.12.recv_hbm, f32[256,1024]{1,0:T(8,128)} %copy-done.5), custom_call_target="tpu_custom_call" | custom-call | bytes 2097152 | tf_op jit(solution)/shard_map/sums/share/pallas_call | solution.py:564
  153.7 30.3 %all_gather.7.part_ref = f32[640,256]{1,0:T(8,128)S(1)} all-gather(f32[40,256]{1,0:T(8,128)} %share.1.own_ref), channel_id=1, replica_groups=mesh['row'=16,'col'=32] {'row'}, dimensions={0}, use_global_device_ids=true | all-gather | bytes 696320 | tf_op jit(solution)/shard_map/sums/all_gather | solution.py:568
  184.0 0.0 copy-start.7
  184.0 0.8 copy-done.7
  184.8 1.3 deal.1
  186.1 16.1 %all-to-all-start.4 = ((f32[32,56,256]{2,1,0:T(8,128)}), f32[32,56,256]{2,1,0:T(8,128)S(1)}, u32[]{:S(2)}, u32[]{:S(2)}) async-start(f32[32,56,256]{2,1,0:T(8,128)} %bitcast.13), calls=%async_computation.4 | async-start | bytes 3670016 | tf_op jit(solution)/shard_map/deal/all_to_all | solution.py:575
  202.2 11.5 %reflector.1 = (f32[256,256]{1,0:T(8,128)}, f32[256,256]{1,0:T(8,128)S(1)}) custom-call(f32[1024,128]{1,0:T(8,128)} %bitcast.8.g_ref, f32[256,256]{1,0:T(8,128)S(1)} %get-tuple-element.33.linv_ref), custom_call_target="tpu_custom_call" | custom-call | flops 5000000000 | bytes 41943040 | tf_op jit(solution)/shard_map/reflector/reflector/pallas_call | solution.py:577
  213.7 0.0 copy-start.9
  213.7 0.7 copy-done.9
  214.4 12.7 %all-to-all-done.4 = f32[32,56,256]{2,1,0:T(8,128)S(1)} async-done(((f32[32,56,256]{2,1,0:T(8,128)}), f32[32,56,256]{2,1,0:T(8,128)S(1)}, u32[]{:S(2)}, u32[]{:S(2)}) %all-to-all-start.4) | async-done | bytes 1835040 | tf_op jit(solution)/shard_map/deal/all_to_all | solution.py:575
  227.1 0.0 copy-start.11
  227.1 1.2 copy-done.11
  228.4 7.8 %update.1 = f32[4096,128]{1,0:T(8,128)} custom-call(s32[2]{0:T(128)} %copy-done.10, f32[256,256]{1,0:T(8,128)} %copy-done.9, f32[256,256]{1,0:T(8,128)} %get-tuple-element.43.refl_hbm, f32[1792,256]{1,0:T(8,128)} %bitcast.28, f32[256,512]{1,0:T(8,128)} %copy-done.6, f32[256,1024]{1,0:T(8,128)} %copy-done.5, f32[4096,128]{1,0:T(8,128)} %bitcast.17), custom_call_target="tpu_custom_call" | custom-call | bytes 8388608 | tf_op jit(solution)/shard_map/update/update/pallas_call | solution.py:587
  (4 shorter events, 0.0 us)
Async XLA Ops:
  0.6 12.4 %copy-start.8 = (f32[8,4,1,256]{3,2,1,0:T(1,128)S(1)}, f32[8,4,1,256]{3,2,1,0:T(1,128)}, u32[]{:S(2)}) copy-start(f32[8,4,1,256]{3,2,1,0:T(1,128)} %param.3) | copy-start | bytes 98308
  2.5 27.8 %all-to-all-start = ((f32[32,64,128]{2,1,0:T(8,128)}), f32[32,64,128]{2,1,0:T(8,128)S(1)}, u32[]{:S(2)}, u32[]{:S(2)}) async-start(f32[32,64,128]{2,1,0:T(8,128)} %tile.4), calls=%async_computation | async-start | bytes 2097152 | tf_op jit(solution)/shard_map/panel/all_to_all | solution.py:475
  13.0 71.2 %copy-start = (f32[4,1,256,2,1,256]{5,4,3,2,1,0:T(1,128)S(1)}, f32[4,1,256,2,1,256]{5,4,3,2,1,0:T(1,128)}, u32[]{:S(2)}) copy-start(f32[4,1,256,2,1,256]{5,4,3,2,1,0:T(1,128)} %param.2) | copy-start | bytes 6291460
  13.1 7.3 %collective-permute-start = (f32[32,128]{1,0:T(8,128)S(1)}, f32[32,128]{1,0:T(8,128)S(1)}, u32[]{:S(2)}, u32[]{:S(2)}) collective-permute-start(f32[32,128]{1,0:T(8,128)S(1)} %bitcast.31), channel_id=1, source_target_pairs={{0,0},{1,16},{2,32},{3,48},{4,64},{5,80},{6,96},{7,112},{8,128},{9... | collective-permute-start | bytes 49160 | tf_op jit(solution)/shard_map/panel/ppermute | solution.py:492
  18.4 4.8 %collective-permute-start.1 = (f32[32,128]{1,0:T(8,128)S(1)}, f32[32,128]{1,0:T(8,128)S(1)}, u32[]{:S(2)}, u32[]{:S(2)}) collective-permute-start(f32[32,128]{1,0:T(8,128)S(1)} %bitcast.30), channel_id=1, source_target_pairs={{0,16},{1,0},{2,48},{3,32},{4,80},{5,64},{6,112},{7,96},{8,144},{9... | collective-permute-start | bytes 49160 | tf_op jit(solution)/shard_map/panel/ppermute | solution.py:493
  20.4 119.2 %copy-start.10 = (s32[2]{0:T(128)}, s32[2]{0:T(128)S(1)}, u32[]{:S(2)}) copy-start(s32[2]{0:T(128)S(1)} %pad_add_fusion.place) | copy-start | bytes 28
  64.6 0.9 copy-start.1
  66.3 30.3 %all-to-all-start.1 = ((f32[32,32,128]{2,1,0:T(8,128)}), f32[32,32,128]{2,1,0:T(8,128)}, u32[]{:S(2)}, u32[]{:S(2)}) async-start(f32[32,32,128]{2,1,0:T(8,128)} %tile.5), calls=%async_computation.1 | async-start | bytes 1048576 | tf_op jit(solution)/shard_map/gram/all_to_all | solution.py:475
  86.3 9.6 %collective-permute-start.2 = (f32[128,512]{1,0:T(8,128)S(1)}, f32[128,512]{1,0:T(8,128)S(1)}, u32[]{:S(2)}, u32[]{:S(2)}) collective-permute-start(f32[128,512]{1,0:T(8,128)S(1)} %get-tuple-element.26), channel_id=1, source_target_pairs={{0,32},{32,0},{64,96},{96,64},{128,160},{160,128},{192,224},{224,1... | collective-permute-start | bytes 786440 | tf_op jit(solution)/shard_map/mirror/ppermute | solution.py:530
  96.6 24.4 %all-to-all-start.2 = ((f32[8,16,512]{2,1,0:T(8,128)}), f32[8,16,512]{2,1,0:T(8,128)}, u32[]{:S(2)}, u32[]{:S(2)}) async-start(f32[8,16,512]{2,1,0:T(8,128)} %bitcast.10), calls=%async_computation.2 | async-start | bytes 524288 | tf_op jit(solution)/shard_map/mirror/all_to_all | solution.py:533
  104.3 13.5 %copy-start.2 = (f32[1536,128]{1,0:T(8,128)S(1)}, f32[1536,128]{1,0:T(8,128)}, u32[]{:S(2)}) copy-start(f32[1536,128]{1,0:T(8,128)} %copy-done.1) | copy-start | bytes 2359300
  120.1 1.0 copy-start.4
  121.0 18.6 %copy-start.3 = (f32[1536,128]{1,0:T(8,128)S(1)}, f32[1536,128]{1,0:T(8,128)}, u32[]{:S(2)}) copy-start(f32[1536,128]{1,0:T(8,128)} %copy-done.1) | copy-start | bytes 2359300
  121.0 29.2 %all-to-all-start.3 = ((f32[32,8,1024]{2,1,0:T(8,128)}), f32[32,8,1024]{2,1,0:T(8,128)}, u32[]{:S(2)}, u32[]{:S(2)}) async-start(f32[32,8,1024]{2,1,0:T(8,128)} %bitcast.24), calls=%async_computation.3 | async-start | bytes 2097152 | tf_op jit(solution)/shard_map/sums/all_to_all | solution.py:562
  134.0 10.8 %collective-permute-start.4 = (f32[8,512]{1,0:T(8,128)S(1)}, f32[8,512]{1,0:T(8,128)S(1)}, u32[]{:S(2)}, u32[]{:S(2)}) collective-permute-start(f32[8,512]{1,0:T(8,128)S(1)} %get-tuple-element.46), channel_id=1, source_target_pairs={{0,0},{16,1},{32,2},{48,3},{64,4},{80,5},{96,6},{112,7},{128,8},{1... | collective-permute-start | bytes 49160 | tf_op jit(solution)/shard_map/sums/ppermute | solution.py:500
  136.1 8.8 %collective-permute-start.3 = (f32[8,512]{1,0:T(8,128)S(1)}, f32[8,512]{1,0:T(8,128)S(1)}, u32[]{:S(2)}, u32[]{:S(2)}) collective-permute-start(f32[8,512]{1,0:T(8,128)S(1)} %get-tuple-element.47), channel_id=1, source_target_pairs={{16,0},{0,1},{48,2},{32,3},{80,4},{64,5},{112,6},{96,7},{144,8},{1... | collective-permute-start | bytes 49160 | tf_op jit(solution)/shard_map/sums/ppermute | solution.py:501
  141.7 1.0 copy-start.5
  142.6 0.8 copy-start.6
  184.0 0.8 copy-start.7
  186.1 41.0 %all-to-all-start.4 = ((f32[32,56,256]{2,1,0:T(8,128)}), f32[32,56,256]{2,1,0:T(8,128)S(1)}, u32[]{:S(2)}, u32[]{:S(2)}) async-start(f32[32,56,256]{2,1,0:T(8,128)} %bitcast.13), calls=%async_computation.4 | async-start | bytes 3670016 | tf_op jit(solution)/shard_map/deal/all_to_all | solution.py:575
  213.7 0.7 copy-start.9
  227.1 1.2 copy-start.11

commit v6 on v5

--- a/solution.py
+++ b/solution.py
@@ -14,6 +14,8 @@
 BS = 16
 SHARE = NB // N_COL
 CHUNK = NB // N_ROW
+PAIRS = [(r, r ^ 1) for r in range(N_ROW)]
+PARITIES = [list(range(parity, N_ROW, 2)) for parity in range(2)]
 F32 = jnp.float32
 VMEM = pl.BlockSpec(memory_space=pltpu.VMEM)
 SMEM = pl.BlockSpec(memory_space=pltpu.SMEM)
@@ -380,19 +382,23 @@
     out_ref[pl.ds(TR * SHARE, SHARE), :] = product(split(total), split(rows_ref[...]), 1, 1)
 
 
-def deal_kernel(own_ref, part_ref, out_hbm, out_ref, sems):
-    curved = part_ref[pl.ds(TR * SHARE, SHARE), :]
-    for r in range(1, N_ROW):
-        curved = curved + part_ref[pl.ds(r * PART + TR * SHARE, SHARE), :]
+def deal_kernel(place, own_ref, same_ref, other_ref, out_hbm, out_ref, sems):
+    curved = jnp.zeros((SHARE, NB), F32)
+    for k in range(N_ROW // 2):
+        at = pl.ds(k * PART + TR * SHARE, SHARE)
+        curved = curved + (same_ref[at, :] + other_ref[at, :])
     own = own_ref[: TR * SHARE, :]
+    parity = place[0] % 2
     copies = []
     group = N_COL // 4
     for c in range(N_COL):
         for u in range(TC):
             t = u * (N_COL // N_ROW) + c // N_ROW
-            out_ref[pl.ds(c * DEAL + u * SHARE, SHARE), :] = part_ref[
-                pl.ds((c % N_ROW) * PART + t * SHARE, SHARE), :
-            ]
+            r = c % N_ROW
+            at = pl.ds((r // 2) * PART + t * SHARE, SHARE)
+            out_ref[pl.ds(c * DEAL + u * SHARE, SHARE), :] = jnp.where(
+                parity == r % 2, same_ref[at, :], other_ref[at, :]
+            )
         out_ref[pl.ds(c * DEAL + TC * SHARE, SHARE), :] = curved
         out_ref[pl.ds(c * DEAL + (TC + 1) * SHARE, TR * SHARE), :] = own
         if c % group == group - 1:
@@ -527,10 +533,9 @@
             mirror_kernel, [(NB // 2, TC * NB)] * 2, scratch=[(NB, TC * NB)], n_scalars=1, n_in=2,
             name="mirror", moved=4 << 20,
         )(place, panel_rows, stored)
-        mirror = keep + lax.ppermute(send, "row", [(r, r ^ 1) for r in range(N_ROW)])
+        mirror = keep + lax.ppermute(send, "row", PAIRS)
         gram, mirror = lax.optimization_barrier((gram, mirror))
-        parities = [list(range(parity, N_ROW, 2)) for parity in range(2)]
-        mirror = lax.all_to_all(mirror, "row", 0, 0, axis_index_groups=parities, tiled=True)
+        mirror = lax.all_to_all(mirror, "row", 0, 0, axis_index_groups=PARITIES, tiled=True)
         from_cols = mirror.reshape(N_ROW // 2, CHUNK, TC * NB).sum(0)
     with jax.named_scope("factor"):
         band, linv, upper = call(
@@ -563,14 +568,17 @@
         even, odd = to_rows(from_cols[:SHARE], from_cols[SHARE:], col_index)
         (payload,) = call(
             share_kernel, [(PART, NB)], scratch=[(NB, TR * NB)] * 2, n_in=2, n_any=2, copies=2,
-            name="share", moved=2 << 20, megabytes=60,
+            name="share", moved=2 << 20,
         )(even, odd, received, rows)
-        parts = lax.all_gather(payload, "row", tiled=True)
+        same = lax.all_to_all(
+            jnp.tile(payload, (N_ROW // 2, 1)), "row", 0, 0, axis_index_groups=PARITIES, tiled=True
+        )
+        other = lax.ppermute(same, "row", PAIRS)
     with jax.named_scope("deal"):
         (deal,) = call(
-            deal_kernel, [(N_COL * DEAL, NB)], scratch=[(N_COL * DEAL, NB)], n_in=2, any_out=True,
-            copies=4, name="deal", moved=3 << 20,
-        )(payload, parts)
+            deal_kernel, [(N_COL * DEAL, NB)], scratch=[(N_COL * DEAL, NB)], n_scalars=1, n_in=3,
+            any_out=True, copies=4, name="deal", moved=3 << 20,
+        )(place, payload, same, other)
         deal, gram, linv = lax.optimization_barrier((deal, gram, linv))
         deal = lax.all_to_all(deal, "col", 0, 0, tiled=True)
     with jax.named_scope("reflector"):

time: 238 us -> 245 us (1.029)
  waiting for transfers between devices: 34.8 us -> 41.2 us
  blocking collectives: 63.1 us -> 66.2 us
    all_to_all x0 -> x1, blocking collectives: none -> 33.4 us  [body(): lax.all_to_all(jnp.tile(payload, (N_ROW // 2, 1)), 'row', 0, 0, axis_inde...]
    all_gather x1 -> x0, blocking collectives: 30.3 us -> none  [body(): parts = lax.all_gather(payload, 'row', tiled=True)]
    ppermute x1 -> x2, waiting for transfers between devices: 5.88 us -> 11.8 us  [the longest x1 5.89 us: body(): other = lax.ppermute(same, 'row', PAIRS)]
    all_to_all x1, starting transfers between devices: 16.1 us -> 12.9 us  [body(): deal = lax.all_to_all(deal, 'col', 0, 0, tiled=True)]
    ppermute x1 -> x2, starting transfers between devices: 3.72 us -> 5.64 us  [the longest x1 3.73 us: body(): mirror = keep + lax.ppermute(send, 'row', PAIRS)]
  transfers between devices with their start and end apart: 10 -> 11, of which waited for: 6 -> 7; matrix products, arithmetic and copies ran while one was open for 1% -> 1% of each run, Pallas kernels for 13% -> 13%
where the time goes in v6:
time: 245 us; the launch traced here: 243 us
  starting transfers between devices  79.3 us (32%)
  blocking collectives  66.2 us (27%)
  Pallas kernels  44.3 us (18%)
  waiting for transfers between devices  41.2 us (17%)
  local copies, waits for them, and re-layouts  9.58 us (4%)
    all_to_all x1, blocking collectives, body(): lax.all_to_all(jnp.tile(payload, (N_ROW // 2, 1)), 'row', 0, 0, axis_inde...  33.4 us
    all_gather x1, blocking collectives, body(): panel_cols = lax.all_gather(payload, 'row', tiled=True)  32.8 us
    all_to_all x2, starting transfers between devices, spread(): return lax.all_to_all(jnp.tile(value, (count, 1)), axis, 0, 0, tiled=True)  28.4 us
    pallas_call x1, Pallas kernels, body(): call(cholesky, [(NB, NB)] * 3, scratch=[(NB, NB)] * 2 + [(BS, NB)] * 2, n...  13.5 us
    all_to_all x1, starting transfers between devices, body(): deal = lax.all_to_all(deal, 'col', 0, 0, tiled=True)  12.9 us
    all_to_all x1, waiting for transfers between devices, body(): deal = lax.all_to_all(deal, 'col', 0, 0, tiled=True)  12.7 us
    all_to_all x1, starting transfers between devices, body(): received = lax.all_to_all(row_terms, 'col', 0, 0, tiled=True)  12 us
    pallas_call x1, Pallas kernels, body(): call(reflector_kernel, [(NB, NB)] * 2, scratch=[(NB, NB), (BS, NB)], n_in...  11.5 us
  transfers between devices with their start and end apart: 11, of which 7 were waited for; matrix products, arithmetic and copies ran while one was open for 1% of the time, Pallas kernels for 13%

profile of v6, /device:TPU:1, one launch (start us, length us, event | category | flops | bytes accessed | tf_op | source)
XLA Modules:
  0.0 243.4 jit_solution(10362202689391470881)
XLA Ops:
  0.6 0.0 copy-start.8
  0.6 1.9 tile.6
  2.5 10.5 %all-to-all-start = ((f32[32,64,128]{2,1,0:T(8,128)}), f32[32,64,128]{2,1,0:T(8,128)S(1)}, u32[]{:S(2)}, u32[]{:S(2)}) async-start(f32[32,64,128]{2,1,0:T(8,128)} %tile.6), calls=%async_computation | async-start | bytes 2097152 | tf_op jit(solution)/shard_map/panel/all_to_all | solution.py:481
  13.0 0.0 copy-start
  13.0 0.0 copy-done.8
  13.1 5.3 %collective-permute-start = (f32[32,128]{1,0:T(8,128)S(1)}, f32[32,128]{1,0:T(8,128)S(1)}, u32[]{:S(2)}, u32[]{:S(2)}) collective-permute-start(f32[32,128]{1,0:T(8,128)S(1)} %bitcast.35), channel_id=1, source_target_pairs={{0,0},{1,16},{2,32},{3,48},{4,64},{5,80},{6,96},{7,112},{8,128},{9... | collective-permute-start | bytes 49160 | tf_op jit(solution)/shard_map/panel/ppermute | solution.py:498
  18.4 1.9 collective-permute-start.1
  20.3 0.1 pad_add_fusion.place
  20.4 0.0 copy-start.10
  20.4 0.0 collective-permute-done
  20.4 2.8 %collective-permute-done.1 = f32[32,128]{1,0:T(8,128)S(1)} collective-permute-done((f32[32,128]{1,0:T(8,128)S(1)}, f32[32,128]{1,0:T(8,128)S(1)}, u32[]{:S(2)}, u32[]{:S(2)}) %collective-permute-start.1) | collective-permute-done | bytes 16416 | tf_op jit(solution)/shard_map/panel/ppermute | solution.py:499
  23.1 7.2 %all-to-all-done = f32[32,64,128]{2,1,0:T(8,128)S(1)} async-done(((f32[32,64,128]{2,1,0:T(8,128)}), f32[32,64,128]{2,1,0:T(8,128)S(1)}, u32[]{:S(2)}, u32[]{:S(2)}) %all-to-all-start) | async-done | bytes 1048608 | tf_op jit(solution)/shard_map/panel/all_to_all | solution.py:481
  30.3 1.5 gram.1
  31.8 32.8 %all_gather.3.panel_hbm.panel_cols_ref = f32[1536,128]{1,0:T(8,128)S(1)} all-gather(f32[96,128]{1,0:T(8,128)S(1)} %gram.1), channel_id=1, replica_groups=mesh['row'=16,'col'=32] {'row'}, dimensions={0}, use_global_device_ids=true | all-gather | bytes 835584 | tf_op jit(solution)/shard_map/gram/all_gather | solution.py:528
  64.6 0.0 copy-start.1
  64.6 0.9 copy-done.1
  65.5 0.9 tile.7
  66.3 17.9 %all-to-all-start.1 = ((f32[32,32,128]{2,1,0:T(8,128)}), f32[32,32,128]{2,1,0:T(8,128)}, u32[]{:S(2)}, u32[]{:S(2)}) async-start(f32[32,32,128]{2,1,0:T(8,128)} %tile.7), calls=%async_computation.1 | async-start | bytes 1048576 | tf_op jit(solution)/shard_map/gram/all_to_all | solution.py:481
  84.2 0.0 copy-done
  84.2 2.0 mirror.1
  86.3 3.7 %collective-permute-start.2 = (f32[128,512]{1,0:T(8,128)S(1)}, f32[128,512]{1,0:T(8,128)S(1)}, u32[]{:S(2)}, u32[]{:S(2)}) collective-permute-start(f32[128,512]{1,0:T(8,128)S(1)} %get-tuple-element.26), channel_id=1, source_target_pairs={{0,32},{32,0},{64,96},{96,64},{128,160},{160,128},{192,224},{224,1... | collective-permute-start | bytes 786440 | tf_op jit(solution)/shard_map/mirror/ppermute | solution.py:536
  90.0 5.9 %collective-permute-done.2 = f32[128,512]{1,0:T(8,128)S(1)} collective-permute-done((f32[128,512]{1,0:T(8,128)S(1)}, f32[128,512]{1,0:T(8,128)S(1)}, u32[]{:S(2)}, u32[]{:S(2)}) %collective-permute-start.2) | collective-permute-done | bytes 262176 | tf_op jit(solution)/shard_map/mirror/ppermute | solution.py:536
  95.9 0.7 add.9
  96.6 0.0 all-to-all-done.1
  96.6 7.6 %all-to-all-start.2 = ((f32[8,16,512]{2,1,0:T(8,128)}), f32[8,16,512]{2,1,0:T(8,128)}, u32[]{:S(2)}, u32[]{:S(2)}) async-start(f32[8,16,512]{2,1,0:T(8,128)} %bitcast.33), calls=%async_computation.2 | async-start | bytes 524288 | tf_op jit(solution)/shard_map/mirror/all_to_all | solution.py:538
  104.3 0.0 copy-start.2
  104.3 13.5 %cholesky.1 = (f32[256,256]{1,0:T(8,128)}, f32[256,256]{1,0:T(8,128)S(1)}, f32[256,256]{1,0:T(8,128)S(1)}) custom-call(f32[1024,128]{1,0:T(8,128)} %bitcast.8.g_ref), custom_call_target="tpu_custom_call" | custom-call | flops 5000000000 | bytes 41943040 | tf_op jit(solution)/shard_map/factor/cholesky/pallas_call | solution.py:541
  117.8 0.0 copy-done.2
  117.8 2.3 symmetric.1
  120.1 0.0 copy-start.4
  120.1 1.0 copy-done.4
  121.1 0.0 copy-start.3
  121.1 0.0 all-to-all-done.2
  121.1 12.0 %all-to-all-start.3 = ((f32[32,8,1024]{2,1,0:T(8,128)}), f32[32,8,1024]{2,1,0:T(8,128)}, u32[]{:S(2)}, u32[]{:S(2)}) async-start(f32[32,8,1024]{2,1,0:T(8,128)} %bitcast.25), calls=%async_computation.3 | async-start | bytes 2097152 | tf_op jit(solution)/shard_map/sums/all_to_all | solution.py:567
  133.0 1.0 reduce_sum.19
  134.0 2.1 collective-permute-start.4
  136.1 3.5 %collective-permute-start.3 = (f32[8,512]{1,0:T(8,128)S(1)}, f32[8,512]{1,0:T(8,128)S(1)}, u32[]{:S(2)}, u32[]{:S(2)}) collective-permute-start(f32[8,512]{1,0:T(8,128)S(1)} %get-tuple-element.47), channel_id=1, source_target_pairs={{16,0},{0,1},{48,2},{32,3},{80,4},{64,5},{112,6},{96,7},{144,8},{1... | collective-permute-start | bytes 49160 | tf_op jit(solution)/shard_map/sums/ppermute | solution.py:507
  139.6 0.0 copy-done.3
  139.6 2.1 vectors.1
  141.7 0.0 copy-start.5
  141.7 1.0 copy-done.5
  142.6 0.0 copy-start.7
  142.6 0.8 copy-done.7
  143.4 1.4 collective-permute-done.4
  144.8 0.0 collective-permute-done.3
  144.9 5.4 %all-to-all-done.3 = f32[32,8,1024]{2,1,0:T(8,128)} async-done(((f32[32,8,1024]{2,1,0:T(8,128)}), f32[32,8,1024]{2,1,0:T(8,128)}, u32[]{:S(2)}, u32[]{:S(2)}) %all-to-all-start.3) | async-done | bytes 1048608 | tf_op jit(solution)/shard_map/sums/all_to_all | solution.py:567
  150.3 0.0 copy-start.6
  150.3 1.2 copy-done.6
  151.5 1.8 share.1.own_ref
  153.4 33.4 %all_to_all.57 = f32[8,40,256]{2,1,0:T(8,128)S(1)} all-to-all(f32[8,40,256]{2,1,0:T(8,128)S(1)} %tile.8), channel_id=1, replica_groups={{0,64,128,192,256,320,384,448},{32,96,160,224,288,352,416,480},{1,65,12..., dimensions={0} | all-to-all | bytes 655360 | tf_op jit(solution)/shard_map/sums/all_to_all | solution.py:573
  186.7 1.9 collective-permute-start.5
  188.7 5.9 %collective-permute-done.5.other_ref = f32[320,256]{1,0:T(8,128)S(1)} collective-permute-done((f32[320,256]{1,0:T(8,128)S(1)}, f32[320,256]{1,0:T(8,128)S(1)}, u32[]{:S(2)}, u32[]{:S(2)}) %collective-permute-start.5) | collective-permute-done | bytes 327712 | tf_op jit(solution)/shard_map/sums/ppermute | solution.py:576
  194.6 0.0 copy-done.10
  194.6 1.8 deal.1
  196.4 12.9 %all-to-all-start.5 = ((f32[32,56,256]{2,1,0:T(8,128)}), f32[32,56,256]{2,1,0:T(8,128)S(1)}, u32[]{:S(2)}, u32[]{:S(2)}) async-start(f32[32,56,256]{2,1,0:T(8,128)} %bitcast.14), calls=%async_computation.5 | async-start | bytes 3670016 | tf_op jit(solution)/shard_map/deal/all_to_all | solution.py:583
  209.3 11.5 %reflector.1 = (f32[256,256]{1,0:T(8,128)}, f32[256,256]{1,0:T(8,128)S(1)}) custom-call(f32[1024,128]{1,0:T(8,128)} %bitcast.8.g_ref, f32[256,256]{1,0:T(8,128)S(1)} %get-tuple-element.33.linv_ref), custom_call_target="tpu_custom_call" | custom-call | flops 5000000000 | bytes 41943040 | tf_op jit(solution)/shard_map/reflector/reflector/pallas_call | solution.py:585
  220.8 0.0 copy-start.9
  220.8 0.7 copy-done.9
  221.5 12.7 %all-to-all-done.5 = f32[32,56,256]{2,1,0:T(8,128)S(1)} async-done(((f32[32,56,256]{2,1,0:T(8,128)}), f32[32,56,256]{2,1,0:T(8,128)S(1)}, u32[]{:S(2)}, u32[]{:S(2)}) %all-to-all-start.5) | async-done | bytes 1835040 | tf_op jit(solution)/shard_map/deal/all_to_all | solution.py:583
  234.2 0.0 copy-start.11
  234.2 1.3 copy-done.11
  235.4 7.8 %update.1 = f32[4096,128]{1,0:T(8,128)} custom-call(s32[2]{0:T(128)} %copy-done.10, f32[256,256]{1,0:T(8,128)} %copy-done.9, f32[256,256]{1,0:T(8,128)} %get-tuple-element.43.refl_hbm, f32[1792,256]{1,0:T(8,128)} %bitcast.31, f32[256,512]{1,0:T(8,128)} %copy-done.7, f32[256,1024]{1,0:T(8,128)} %copy-done.5, f32[4096,128]{1,0:T(8,128)} %bitcast.18), custom_call_target="tpu_custom_call" | custom-call | bytes 8388608 | tf_op jit(solution)/shard_map/update/update/pallas_call | solution.py:595
  (6 shorter events, 0.1 us)
Async XLA Ops:
  0.6 12.4 %copy-start.8 = (f32[8,4,1,256]{3,2,1,0:T(1,128)S(1)}, f32[8,4,1,256]{3,2,1,0:T(1,128)}, u32[]{:S(2)}) copy-start(f32[8,4,1,256]{3,2,1,0:T(1,128)} %param.3) | copy-start | bytes 98308
  2.5 27.8 %all-to-all-start = ((f32[32,64,128]{2,1,0:T(8,128)}), f32[32,64,128]{2,1,0:T(8,128)S(1)}, u32[]{:S(2)}, u32[]{:S(2)}) async-start(f32[32,64,128]{2,1,0:T(8,128)} %tile.6), calls=%async_computation | async-start | bytes 2097152 | tf_op jit(solution)/shard_map/panel/all_to_all | solution.py:481
  13.0 71.2 %copy-start = (f32[4,1,256,2,1,256]{5,4,3,2,1,0:T(1,128)S(1)}, f32[4,1,256,2,1,256]{5,4,3,2,1,0:T(1,128)}, u32[]{:S(2)}) copy-start(f32[4,1,256,2,1,256]{5,4,3,2,1,0:T(1,128)} %param.2) | copy-start | bytes 6291460
  13.1 7.3 %collective-permute-start = (f32[32,128]{1,0:T(8,128)S(1)}, f32[32,128]{1,0:T(8,128)S(1)}, u32[]{:S(2)}, u32[]{:S(2)}) collective-permute-start(f32[32,128]{1,0:T(8,128)S(1)} %bitcast.35), channel_id=1, source_target_pairs={{0,0},{1,16},{2,32},{3,48},{4,64},{5,80},{6,96},{7,112},{8,128},{9... | collective-permute-start | bytes 49160 | tf_op jit(solution)/shard_map/panel/ppermute | solution.py:498
  18.4 4.8 %collective-permute-start.1 = (f32[32,128]{1,0:T(8,128)S(1)}, f32[32,128]{1,0:T(8,128)S(1)}, u32[]{:S(2)}, u32[]{:S(2)}) collective-permute-start(f32[32,128]{1,0:T(8,128)S(1)} %bitcast.34), channel_id=1, source_target_pairs={{0,16},{1,0},{2,48},{3,32},{4,80},{5,64},{6,112},{7,96},{8,144},{9... | collective-permute-start | bytes 49160 | tf_op jit(solution)/shard_map/panel/ppermute | solution.py:499
  20.4 174.2 %copy-start.10 = (s32[2]{0:T(128)}, s32[2]{0:T(128)S(1)}, u32[]{:S(2)}) copy-start(s32[2]{0:T(128)S(1)} %pad_add_fusion.place) | copy-start | bytes 28
  64.6 0.9 copy-start.1
  66.3 30.3 %all-to-all-start.1 = ((f32[32,32,128]{2,1,0:T(8,128)}), f32[32,32,128]{2,1,0:T(8,128)}, u32[]{:S(2)}, u32[]{:S(2)}) async-start(f32[32,32,128]{2,1,0:T(8,128)} %tile.7), calls=%async_computation.1 | async-start | bytes 1048576 | tf_op jit(solution)/shard_map/gram/all_to_all | solution.py:481
  86.3 9.6 %collective-permute-start.2 = (f32[128,512]{1,0:T(8,128)S(1)}, f32[128,512]{1,0:T(8,128)S(1)}, u32[]{:S(2)}, u32[]{:S(2)}) collective-permute-start(f32[128,512]{1,0:T(8,128)S(1)} %get-tuple-element.26), channel_id=1, source_target_pairs={{0,32},{32,0},{64,96},{96,64},{128,160},{160,128},{192,224},{224,1... | collective-permute-start | bytes 786440 | tf_op jit(solution)/shard_map/mirror/ppermute | solution.py:536
  96.6 24.4 %all-to-all-start.2 = ((f32[8,16,512]{2,1,0:T(8,128)}), f32[8,16,512]{2,1,0:T(8,128)}, u32[]{:S(2)}, u32[]{:S(2)}) async-start(f32[8,16,512]{2,1,0:T(8,128)} %bitcast.33), calls=%async_computation.2 | async-start | bytes 524288 | tf_op jit(solution)/shard_map/mirror/all_to_all | solution.py:538
  104.3 13.5 %copy-start.2 = (f32[1536,128]{1,0:T(8,128)S(1)}, f32[1536,128]{1,0:T(8,128)}, u32[]{:S(2)}) copy-start(f32[1536,128]{1,0:T(8,128)} %copy-done.1) | copy-start | bytes 2359300
  120.1 1.0 copy-start.4
  121.1 18.6 %copy-start.3 = (f32[1536,128]{1,0:T(8,128)S(1)}, f32[1536,128]{1,0:T(8,128)}, u32[]{:S(2)}) copy-start(f32[1536,128]{1,0:T(8,128)} %copy-done.1) | copy-start | bytes 2359300
  121.1 29.2 %all-to-all-start.3 = ((f32[32,8,1024]{2,1,0:T(8,128)}), f32[32,8,1024]{2,1,0:T(8,128)}, u32[]{:S(2)}, u32[]{:S(2)}) async-start(f32[32,8,1024]{2,1,0:T(8,128)} %bitcast.25), calls=%async_computation.3 | async-start | bytes 2097152 | tf_op jit(solution)/shard_map/sums/all_to_all | solution.py:567
  134.0 10.8 %collective-permute-start.4 = (f32[8,512]{1,0:T(8,128)S(1)}, f32[8,512]{1,0:T(8,128)S(1)}, u32[]{:S(2)}, u32[]{:S(2)}) collective-permute-start(f32[8,512]{1,0:T(8,128)S(1)} %get-tuple-element.46), channel_id=1, source_target_pairs={{0,0},{16,1},{32,2},{48,3},{64,4},{80,5},{96,6},{112,7},{128,8},{1... | collective-permute-start | bytes 49160 | tf_op jit(solution)/shard_map/sums/ppermute | solution.py:506
  136.1 8.8 %collective-permute-start.3 = (f32[8,512]{1,0:T(8,128)S(1)}, f32[8,512]{1,0:T(8,128)S(1)}, u32[]{:S(2)}, u32[]{:S(2)}) collective-permute-start(f32[8,512]{1,0:T(8,128)S(1)} %get-tuple-element.47), channel_id=1, source_target_pairs={{16,0},{0,1},{48,2},{32,3},{80,4},{64,5},{112,6},{96,7},{144,8},{1... | collective-permute-start | bytes 49160 | tf_op jit(solution)/shard_map/sums/ppermute | solution.py:507
  141.7 1.0 copy-start.5
  142.6 0.8 copy-start.7
  150.3 1.2 copy-start.6
  186.7 7.8 %collective-permute-start.5 = (f32[320,256]{1,0:T(8,128)S(1)}, f32[320,256]{1,0:T(8,128)S(1)}, u32[]{:S(2)}, u32[]{:S(2)}) collective-permute-start(f32[320,256]{1,0:T(8,128)S(1)} %bitcast.26), channel_id=1, source_target_pairs={{0,32},{32,0},{64,96},{96,64},{128,160},{160,128},{192,224},{224,1... | collective-permute-start | bytes 983048 | tf_op jit(solution)/shard_map/sums/ppermute | solution.py:576
  196.4 37.8 %all-to-all-start.5 = ((f32[32,56,256]{2,1,0:T(8,128)}), f32[32,56,256]{2,1,0:T(8,128)S(1)}, u32[]{:S(2)}, u32[]{:S(2)}) async-start(f32[32,56,256]{2,1,0:T(8,128)} %bitcast.14), calls=%async_computation.5 | async-start | bytes 3670016 | tf_op jit(solution)/shard_map/deal/all_to_all | solution.py:583
  220.8 0.7 copy-start.9
  234.2 1.3 copy-start.11

commit v7 on v5

--- a/solution.py
+++ b/solution.py
@@ -437,16 +437,17 @@
     copies[3].wait()
     sides = []
     for u in range(TC):
-        vectors = split(cols_ref[:, pl.ds(u * NB, NB)])
-        update = product(both, split(dealt(dealt_ref, u))) - product(half_mixed, vectors)
-        sides.append((vectors, split(update)))
+        vectors = cols_ref[:, pl.ds(u * NB, NB)]
+        update = product(both, split(dealt(dealt_ref, u))) - product(half_mixed, split(vectors))
+        sides.append(split(jnp.concatenate([update, vectors], axis=0)))
     copies[4].wait()
     for t in range(TR):
         here = pl.ds(t * NB, NB)
-        vectors = split(rows_ref[:, here])
-        update = split(
-            product(both, split(dealt(dealt_ref, TC + 1 + t))) - product(half_mixed, vectors)
+        vectors = rows_ref[:, here]
+        update = product(both, split(dealt(dealt_ref, TC + 1 + t))) - product(
+            half_mixed, split(vectors)
         )
+        turned = split(jnp.concatenate([jnp.transpose(vectors), jnp.transpose(update)], axis=1))
         for u in range(TC):
             i, j = tile_place(place, t, u)
             if u == 0:
@@ -454,8 +455,7 @@
 
             @pl.when(i >= j)
             def _():
-                change = product(vectors, sides[u][1], 0, 0) + product(update, sides[u][0], 0, 0)
-                value = matrix_tile(matrix_ref, t, u) - change
+                value = matrix_tile(matrix_ref, t, u) - product(turned, sides[u])
                 r, c = ordering()
                 value = jnp.where((r >= c) | (i > j), value, 0.0)
                 for half in range(2):
@@ -563,7 +563,7 @@
         even, odd = to_rows(from_cols[:SHARE], from_cols[SHARE:], col_index)
         (payload,) = call(
             share_kernel, [(PART, NB)], scratch=[(NB, TR * NB)] * 2, n_in=2, n_any=2, copies=2,
-            name="share", moved=2 << 20, megabytes=60,
+            name="share", moved=2 << 20,
         )(even, odd, received, rows)
         parts = lax.all_gather(payload, "row", tiled=True)
     with jax.named_scope("deal"):

time: 238 us -> 236 us (level)
  no operation moved by 1% of the time
where the time goes in v7:
time: 236 us; the launch traced here: 234 us
  starting transfers between devices  80.5 us (34%)
  blocking collectives  62.3 us (26%)
  Pallas kernels  43.9 us (19%)
  waiting for transfers between devices  35.4 us (15%)
  local copies, waits for them, and re-layouts  9.55 us (4%)
    all_gather x1, blocking collectives, body(): panel_cols = lax.all_gather(payload, 'row', tiled=True)  32.8 us
    all_gather x1, blocking collectives, body(): parts = lax.all_gather(payload, 'row', tiled=True)  29.5 us
    all_to_all x2, starting transfers between devices, spread(): return lax.all_to_all(jnp.tile(value, (count, 1)), axis, 0, 0, tiled=True)  28.4 us
    all_to_all x1, starting transfers between devices, body(): deal = lax.all_to_all(deal, 'col', 0, 0, tiled=True)  16 us
    pallas_call x1, Pallas kernels, body(): call(cholesky, [(NB, NB)] * 3, scratch=[(NB, NB)] * 2 + [(BS, NB)] * 2, n...  13.5 us
    all_to_all x1, waiting for transfers between devices, body(): deal = lax.all_to_all(deal, 'col', 0, 0, tiled=True)  12.8 us
    all_to_all x1, starting transfers between devices, body(): received = lax.all_to_all(row_terms, 'col', 0, 0, tiled=True)  12 us
    pallas_call x1, Pallas kernels, body(): call(reflector_kernel, [(NB, NB)] * 2, scratch=[(NB, NB), (BS, NB)], n_in...  11.5 us
  transfers between devices with their start and end apart: 10, of which 6 were waited for; matrix products, arithmetic and copies ran while one was open for 1% of the time, Pallas kernels for 13%

profile of v7, /device:TPU:1, one launch (start us, length us, event | category | flops | bytes accessed | tf_op | source)
XLA Modules:
  0.0 234.5 jit_solution(3221094236586557133)
XLA Ops:
  0.6 0.0 copy-start.8
  0.6 1.9 tile.4
  2.5 10.5 %all-to-all-start = ((f32[32,64,128]{2,1,0:T(8,128)}), f32[32,64,128]{2,1,0:T(8,128)S(1)}, u32[]{:S(2)}, u32[]{:S(2)}) async-start(f32[32,64,128]{2,1,0:T(8,128)} %tile.4), calls=%async_computation | async-start | bytes 2097152 | tf_op jit(solution)/shard_map/panel/all_to_all | solution.py:475
  13.0 0.0 copy-start
  13.0 0.0 copy-done.8
  13.1 5.3 %collective-permute-start = (f32[32,128]{1,0:T(8,128)S(1)}, f32[32,128]{1,0:T(8,128)S(1)}, u32[]{:S(2)}, u32[]{:S(2)}) collective-permute-start(f32[32,128]{1,0:T(8,128)S(1)} %bitcast.31), channel_id=1, source_target_pairs={{0,0},{1,16},{2,32},{3,48},{4,64},{5,80},{6,96},{7,112},{8,128},{9... | collective-permute-start | bytes 49160 | tf_op jit(solution)/shard_map/panel/ppermute | solution.py:492
  18.4 1.9 collective-permute-start.1
  20.3 0.1 pad_add_fusion.place
  20.4 0.0 copy-start.10
  20.4 0.0 collective-permute-done
  20.4 2.8 %collective-permute-done.1 = f32[32,128]{1,0:T(8,128)S(1)} collective-permute-done((f32[32,128]{1,0:T(8,128)S(1)}, f32[32,128]{1,0:T(8,128)S(1)}, u32[]{:S(2)}, u32[]{:S(2)}) %collective-permute-start.1) | collective-permute-done | bytes 16416 | tf_op jit(solution)/shard_map/panel/ppermute | solution.py:493
  23.1 7.2 %all-to-all-done = f32[32,64,128]{2,1,0:T(8,128)S(1)} async-done(((f32[32,64,128]{2,1,0:T(8,128)}), f32[32,64,128]{2,1,0:T(8,128)S(1)}, u32[]{:S(2)}, u32[]{:S(2)}) %all-to-all-start) | async-done | bytes 1048608 | tf_op jit(solution)/shard_map/panel/all_to_all | solution.py:475
  30.3 1.5 gram.1
  31.8 32.8 %all_gather.6.panel_hbm.panel_cols_ref = f32[1536,128]{1,0:T(8,128)S(1)} all-gather(f32[96,128]{1,0:T(8,128)S(1)} %gram.1), channel_id=1, replica_groups=mesh['row'=16,'col'=32] {'row'}, dimensions={0}, use_global_device_ids=true | all-gather | bytes 835584 | tf_op jit(solution)/shard_map/gram/all_gather | solution.py:522
  64.6 0.0 copy-start.1
  64.6 0.9 copy-done.1
  65.5 0.9 tile.5
  66.3 17.9 %all-to-all-start.1 = ((f32[32,32,128]{2,1,0:T(8,128)}), f32[32,32,128]{2,1,0:T(8,128)}, u32[]{:S(2)}, u32[]{:S(2)}) async-start(f32[32,32,128]{2,1,0:T(8,128)} %tile.5), calls=%async_computation.1 | async-start | bytes 1048576 | tf_op jit(solution)/shard_map/gram/all_to_all | solution.py:475
  84.2 0.0 copy-done
  84.3 2.0 mirror.1
  86.3 3.7 %collective-permute-start.2 = (f32[128,512]{1,0:T(8,128)S(1)}, f32[128,512]{1,0:T(8,128)S(1)}, u32[]{:S(2)}, u32[]{:S(2)}) collective-permute-start(f32[128,512]{1,0:T(8,128)S(1)} %get-tuple-element.26), channel_id=1, source_target_pairs={{0,32},{32,0},{64,96},{96,64},{128,160},{160,128},{192,224},{224,1... | collective-permute-start | bytes 786440 | tf_op jit(solution)/shard_map/mirror/ppermute | solution.py:530
  90.0 5.9 %collective-permute-done.2 = f32[128,512]{1,0:T(8,128)S(1)} collective-permute-done((f32[128,512]{1,0:T(8,128)S(1)}, f32[128,512]{1,0:T(8,128)S(1)}, u32[]{:S(2)}, u32[]{:S(2)}) %collective-permute-start.2) | collective-permute-done | bytes 262176 | tf_op jit(solution)/shard_map/mirror/ppermute | solution.py:530
  95.9 0.7 add.9
  96.6 0.0 all-to-all-done.1
  96.6 7.6 %all-to-all-start.2 = ((f32[8,16,512]{2,1,0:T(8,128)}), f32[8,16,512]{2,1,0:T(8,128)}, u32[]{:S(2)}, u32[]{:S(2)}) async-start(f32[8,16,512]{2,1,0:T(8,128)} %bitcast.10), calls=%async_computation.2 | async-start | bytes 524288 | tf_op jit(solution)/shard_map/mirror/all_to_all | solution.py:533
  104.3 0.0 copy-start.2
  104.3 13.5 %cholesky.1 = (f32[256,256]{1,0:T(8,128)}, f32[256,256]{1,0:T(8,128)S(1)}, f32[256,256]{1,0:T(8,128)S(1)}) custom-call(f32[1024,128]{1,0:T(8,128)} %bitcast.8.g_ref), custom_call_target="tpu_custom_call" | custom-call | flops 5000000000 | bytes 41943040 | tf_op jit(solution)/shard_map/factor/cholesky/pallas_call | solution.py:536
  117.8 0.0 copy-done.2
  117.8 2.3 symmetric.1
  120.1 0.0 copy-start.4
  120.1 1.0 copy-done.4
  121.0 0.0 copy-start.3
  121.0 0.0 all-to-all-done.2
  121.0 12.0 %all-to-all-start.3 = ((f32[32,8,1024]{2,1,0:T(8,128)}), f32[32,8,1024]{2,1,0:T(8,128)}, u32[]{:S(2)}, u32[]{:S(2)}) async-start(f32[32,8,1024]{2,1,0:T(8,128)} %bitcast.24), calls=%async_computation.3 | async-start | bytes 2097152 | tf_op jit(solution)/shard_map/sums/all_to_all | solution.py:562
  133.0 1.0 reduce_sum.19
  134.0 2.0 collective-permute-start.4
  136.1 3.5 %collective-permute-start.3 = (f32[8,512]{1,0:T(8,128)S(1)}, f32[8,512]{1,0:T(8,128)S(1)}, u32[]{:S(2)}, u32[]{:S(2)}) collective-permute-start(f32[8,512]{1,0:T(8,128)S(1)} %get-tuple-element.47), channel_id=1, source_target_pairs={{16,0},{0,1},{48,2},{32,3},{80,4},{64,5},{112,6},{96,7},{144,8},{1... | collective-permute-start | bytes 49160 | tf_op jit(solution)/shard_map/sums/ppermute | solution.py:501
  139.6 0.0 copy-done.10
  139.6 0.0 copy-done.3
  139.6 2.1 vectors.1
  141.7 0.0 copy-start.5
  141.7 1.0 copy-done.5
  142.6 0.0 copy-start.7
  142.7 0.8 copy-done.7
  143.4 1.4 collective-permute-done.4
  144.8 0.0 collective-permute-done.3
  144.8 5.4 %all-to-all-done.3 = f32[32,8,1024]{2,1,0:T(8,128)} async-done(((f32[32,8,1024]{2,1,0:T(8,128)}), f32[32,8,1024]{2,1,0:T(8,128)}, u32[]{:S(2)}, u32[]{:S(2)}) %all-to-all-start.3) | async-done | bytes 1048608 | tf_op jit(solution)/shard_map/sums/all_to_all | solution.py:562
  150.2 0.0 copy-start.6
  150.2 1.2 copy-done.6
  151.5 1.8 share.1.own_ref
  153.3 29.5 %all_gather.7.part_ref = f32[640,256]{1,0:T(8,128)S(1)} all-gather(f32[40,256]{1,0:T(8,128)S(1)} %share.1.own_ref), channel_id=1, replica_groups=mesh['row'=16,'col'=32] {'row'}, dimensions={0}, use_global_device_ids=true | all-gather | bytes 696320 | tf_op jit(solution)/shard_map/sums/all_gather | solution.py:568
  182.8 1.3 deal.1
  184.1 16.0 %all-to-all-start.4 = ((f32[32,56,256]{2,1,0:T(8,128)}), f32[32,56,256]{2,1,0:T(8,128)S(1)}, u32[]{:S(2)}, u32[]{:S(2)}) async-start(f32[32,56,256]{2,1,0:T(8,128)} %bitcast.13), calls=%async_computation.4 | async-start | bytes 3670016 | tf_op jit(solution)/shard_map/deal/all_to_all | solution.py:575
  200.2 11.5 %reflector.1 = (f32[256,256]{1,0:T(8,128)}, f32[256,256]{1,0:T(8,128)S(1)}) custom-call(f32[1024,128]{1,0:T(8,128)} %bitcast.8.g_ref, f32[256,256]{1,0:T(8,128)S(1)} %get-tuple-element.33.linv_ref), custom_call_target="tpu_custom_call" | custom-call | flops 5000000000 | bytes 41943040 | tf_op jit(solution)/shard_map/reflector/reflector/pallas_call | solution.py:577
  211.7 0.0 copy-start.9
  211.7 0.7 copy-done.9
  212.4 12.8 %all-to-all-done.4 = f32[32,56,256]{2,1,0:T(8,128)S(1)} async-done(((f32[32,56,256]{2,1,0:T(8,128)}), f32[32,56,256]{2,1,0:T(8,128)S(1)}, u32[]{:S(2)}, u32[]{:S(2)}) %all-to-all-start.4) | async-done | bytes 1835040 | tf_op jit(solution)/shard_map/deal/all_to_all | solution.py:575
  225.1 0.0 copy-start.11
  225.1 1.2 copy-done.11
  226.4 7.9 %update.1 = f32[4096,128]{1,0:T(8,128)} custom-call(s32[2]{0:T(128)} %copy-done.10, f32[256,256]{1,0:T(8,128)} %copy-done.9, f32[256,256]{1,0:T(8,128)} %get-tuple-element.43.refl_hbm, f32[1792,256]{1,0:T(8,128)} %bitcast.28, f32[256,512]{1,0:T(8,128)} %copy-done.7, f32[256,1024]{1,0:T(8,128)} %copy-done.5, f32[4096,128]{1,0:T(8,128)} %bitcast.17), custom_call_target="tpu_custom_call" | custom-call | bytes 8388608 | tf_op jit(solution)/shard_map/update/update/pallas_call | solution.py:587
  (5 shorter events, 0.1 us)
Async XLA Ops:
  0.6 12.4 %copy-start.8 = (f32[8,4,1,256]{3,2,1,0:T(1,128)S(1)}, f32[8,4,1,256]{3,2,1,0:T(1,128)}, u32[]{:S(2)}) copy-start(f32[8,4,1,256]{3,2,1,0:T(1,128)} %param.3) | copy-start | bytes 98308
  2.5 27.8 %all-to-all-start = ((f32[32,64,128]{2,1,0:T(8,128)}), f32[32,64,128]{2,1,0:T(8,128)S(1)}, u32[]{:S(2)}, u32[]{:S(2)}) async-start(f32[32,64,128]{2,1,0:T(8,128)} %tile.4), calls=%async_computation | async-start | bytes 2097152 | tf_op jit(solution)/shard_map/panel/all_to_all | solution.py:475
  13.0 71.2 %copy-start = (f32[4,1,256,2,1,256]{5,4,3,2,1,0:T(1,128)S(1)}, f32[4,1,256,2,1,256]{5,4,3,2,1,0:T(1,128)}, u32[]{:S(2)}) copy-start(f32[4,1,256,2,1,256]{5,4,3,2,1,0:T(1,128)} %param.2) | copy-start | bytes 6291460
  13.1 7.3 %collective-permute-start = (f32[32,128]{1,0:T(8,128)S(1)}, f32[32,128]{1,0:T(8,128)S(1)}, u32[]{:S(2)}, u32[]{:S(2)}) collective-permute-start(f32[32,128]{1,0:T(8,128)S(1)} %bitcast.31), channel_id=1, source_target_pairs={{0,0},{1,16},{2,32},{3,48},{4,64},{5,80},{6,96},{7,112},{8,128},{9... | collective-permute-start | bytes 49160 | tf_op jit(solution)/shard_map/panel/ppermute | solution.py:492
  18.4 4.8 %collective-permute-start.1 = (f32[32,128]{1,0:T(8,128)S(1)}, f32[32,128]{1,0:T(8,128)S(1)}, u32[]{:S(2)}, u32[]{:S(2)}) collective-permute-start(f32[32,128]{1,0:T(8,128)S(1)} %bitcast.30), channel_id=1, source_target_pairs={{0,16},{1,0},{2,48},{3,32},{4,80},{5,64},{6,112},{7,96},{8,144},{9... | collective-permute-start | bytes 49160 | tf_op jit(solution)/shard_map/panel/ppermute | solution.py:493
  20.4 119.2 %copy-start.10 = (s32[2]{0:T(128)}, s32[2]{0:T(128)S(1)}, u32[]{:S(2)}) copy-start(s32[2]{0:T(128)S(1)} %pad_add_fusion.place) | copy-start | bytes 28
  64.6 0.9 copy-start.1
  66.3 30.3 %all-to-all-start.1 = ((f32[32,32,128]{2,1,0:T(8,128)}), f32[32,32,128]{2,1,0:T(8,128)}, u32[]{:S(2)}, u32[]{:S(2)}) async-start(f32[32,32,128]{2,1,0:T(8,128)} %tile.5), calls=%async_computation.1 | async-start | bytes 1048576 | tf_op jit(solution)/shard_map/gram/all_to_all | solution.py:475
  86.3 9.6 %collective-permute-start.2 = (f32[128,512]{1,0:T(8,128)S(1)}, f32[128,512]{1,0:T(8,128)S(1)}, u32[]{:S(2)}, u32[]{:S(2)}) collective-permute-start(f32[128,512]{1,0:T(8,128)S(1)} %get-tuple-element.26), channel_id=1, source_target_pairs={{0,32},{32,0},{64,96},{96,64},{128,160},{160,128},{192,224},{224,1... | collective-permute-start | bytes 786440 | tf_op jit(solution)/shard_map/mirror/ppermute | solution.py:530
  96.6 24.4 %all-to-all-start.2 = ((f32[8,16,512]{2,1,0:T(8,128)}), f32[8,16,512]{2,1,0:T(8,128)}, u32[]{:S(2)}, u32[]{:S(2)}) async-start(f32[8,16,512]{2,1,0:T(8,128)} %bitcast.10), calls=%async_computation.2 | async-start | bytes 524288 | tf_op jit(solution)/shard_map/mirror/all_to_all | solution.py:533
  104.3 13.5 %copy-start.2 = (f32[1536,128]{1,0:T(8,128)S(1)}, f32[1536,128]{1,0:T(8,128)}, u32[]{:S(2)}) copy-start(f32[1536,128]{1,0:T(8,128)} %copy-done.1) | copy-start | bytes 2359300
  120.1 1.0 copy-start.4
  121.0 18.6 %copy-start.3 = (f32[1536,128]{1,0:T(8,128)S(1)}, f32[1536,128]{1,0:T(8,128)}, u32[]{:S(2)}) copy-start(f32[1536,128]{1,0:T(8,128)} %copy-done.1) | copy-start | bytes 2359300
  121.0 29.2 %all-to-all-start.3 = ((f32[32,8,1024]{2,1,0:T(8,128)}), f32[32,8,1024]{2,1,0:T(8,128)}, u32[]{:S(2)}, u32[]{:S(2)}) async-start(f32[32,8,1024]{2,1,0:T(8,128)} %bitcast.24), calls=%async_computation.3 | async-start | bytes 2097152 | tf_op jit(solution)/shard_map/sums/all_to_all | solution.py:562
  134.0 10.8 %collective-permute-start.4 = (f32[8,512]{1,0:T(8,128)S(1)}, f32[8,512]{1,0:T(8,128)S(1)}, u32[]{:S(2)}, u32[]{:S(2)}) collective-permute-start(f32[8,512]{1,0:T(8,128)S(1)} %get-tuple-element.46), channel_id=1, source_target_pairs={{0,0},{16,1},{32,2},{48,3},{64,4},{80,5},{96,6},{112,7},{128,8},{1... | collective-permute-start | bytes 49160 | tf_op jit(solution)/shard_map/sums/ppermute | solution.py:500
  136.1 8.8 %collective-permute-start.3 = (f32[8,512]{1,0:T(8,128)S(1)}, f32[8,512]{1,0:T(8,128)S(1)}, u32[]{:S(2)}, u32[]{:S(2)}) collective-permute-start(f32[8,512]{1,0:T(8,128)S(1)} %get-tuple-element.47), channel_id=1, source_target_pairs={{16,0},{0,1},{48,2},{32,3},{80,4},{64,5},{112,6},{96,7},{144,8},{1... | collective-permute-start | bytes 49160 | tf_op jit(solution)/shard_map/sums/ppermute | solution.py:501
  141.7 1.0 copy-start.5
  142.6 0.8 copy-start.7
  150.2 1.2 copy-start.6
  184.1 41.0 %all-to-all-start.4 = ((f32[32,56,256]{2,1,0:T(8,128)}), f32[32,56,256]{2,1,0:T(8,128)S(1)}, u32[]{:S(2)}, u32[]{:S(2)}) async-start(f32[32,56,256]{2,1,0:T(8,128)} %bitcast.13), calls=%async_computation.4 | async-start | bytes 3670016 | tf_op jit(solution)/shard_map/deal/all_to_all | solution.py:575
  211.7 0.7 copy-start.9
  225.1 1.2 copy-start.11

commit v8 on v7

--- a/solution.py
+++ b/solution.py
@@ -425,13 +425,15 @@
     ]
     matrix_copies = row_copies(matrix_hbm, matrix_ref, sems, len(copies))
     out_copies = row_copies(out_ref, out_hbm, sems, len(copies) + TR)
-    for copy in copies + matrix_copies:
+    for copy in copies:
         copy.start()
     copies[0].wait()
     both = split(both_ref[...])
     copies[1].wait()
     refl = split(refl_ref[...])
     copies[2].wait()
+    for copy in matrix_copies:
+        copy.start()
     curved = split(product(both, split(dealt(dealt_ref, TC))))
     half_mixed = split(0.5 * product(curved, refl))
     copies[3].wait()

time: 236 us -> 236 us (level)
  no operation moved by 1% of the time
where the time goes in v8:
time: 236 us; the launch traced here: 234 us
  starting transfers between devices  80.5 us (34%)
  blocking collectives  62.3 us (26%)
  Pallas kernels  43.9 us (19%)
  waiting for transfers between devices  35.4 us (15%)
  local copies, waits for them, and re-layouts  9.55 us (4%)
    all_gather x1, blocking collectives, body(): panel_cols = lax.all_gather(payload, 'row', tiled=True)  32.8 us
    all_gather x1, blocking collectives, body(): parts = lax.all_gather(payload, 'row', tiled=True)  29.5 us
    all_to_all x2, starting transfers between devices, spread(): return lax.all_to_all(jnp.tile(value, (count, 1)), axis, 0, 0, tiled=True)  28.4 us
    all_to_all x1, starting transfers between devices, body(): deal = lax.all_to_all(deal, 'col', 0, 0, tiled=True)  16 us
    pallas_call x1, Pallas kernels, body(): call(cholesky, [(NB, NB)] * 3, scratch=[(NB, NB)] * 2 + [(BS, NB)] * 2, n...  13.5 us
    all_to_all x1, waiting for transfers between devices, body(): deal = lax.all_to_all(deal, 'col', 0, 0, tiled=True)  12.8 us
    all_to_all x1, starting transfers between devices, body(): received = lax.all_to_all(row_terms, 'col', 0, 0, tiled=True)  12 us
    pallas_call x1, Pallas kernels, body(): call(reflector_kernel, [(NB, NB)] * 2, scratch=[(NB, NB), (BS, NB)], n_in...  11.5 us
  transfers between devices with their start and end apart: 10, of which 6 were waited for; matrix products, arithmetic and copies ran while one was open for 1% of the time, Pallas kernels for 13%

profile of v8, /device:TPU:1, one launch (start us, length us, event | category | flops | bytes accessed | tf_op | source)
XLA Modules:
  0.0 234.5 jit_solution(7904653364761661890)
XLA Ops:
  0.6 0.0 copy-start.8
  0.6 1.9 tile.4
  2.5 10.5 %all-to-all-start = ((f32[32,64,128]{2,1,0:T(8,128)}), f32[32,64,128]{2,1,0:T(8,128)S(1)}, u32[]{:S(2)}, u32[]{:S(2)}) async-start(f32[32,64,128]{2,1,0:T(8,128)} %tile.4), calls=%async_computation | async-start | bytes 2097152 | tf_op jit(solution)/shard_map/panel/all_to_all | solution.py:477
  13.0 0.0 copy-start
  13.0 0.0 copy-done.8
  13.1 5.3 %collective-permute-start = (f32[32,128]{1,0:T(8,128)S(1)}, f32[32,128]{1,0:T(8,128)S(1)}, u32[]{:S(2)}, u32[]{:S(2)}) collective-permute-start(f32[32,128]{1,0:T(8,128)S(1)} %bitcast.31), channel_id=1, source_target_pairs={{0,0},{1,16},{2,32},{3,48},{4,64},{5,80},{6,96},{7,112},{8,128},{9... | collective-permute-start | bytes 49160 | tf_op jit(solution)/shard_map/panel/ppermute | solution.py:494
  18.4 1.9 collective-permute-start.1
  20.3 0.1 pad_add_fusion.place
  20.4 0.0 copy-start.10
  20.4 0.0 collective-permute-done
  20.4 2.8 %collective-permute-done.1 = f32[32,128]{1,0:T(8,128)S(1)} collective-permute-done((f32[32,128]{1,0:T(8,128)S(1)}, f32[32,128]{1,0:T(8,128)S(1)}, u32[]{:S(2)}, u32[]{:S(2)}) %collective-permute-start.1) | collective-permute-done | bytes 16416 | tf_op jit(solution)/shard_map/panel/ppermute | solution.py:495
  23.1 7.2 %all-to-all-done = f32[32,64,128]{2,1,0:T(8,128)S(1)} async-done(((f32[32,64,128]{2,1,0:T(8,128)}), f32[32,64,128]{2,1,0:T(8,128)S(1)}, u32[]{:S(2)}, u32[]{:S(2)}) %all-to-all-start) | async-done | bytes 1048608 | tf_op jit(solution)/shard_map/panel/all_to_all | solution.py:477
  30.3 1.5 gram.1
  31.8 32.8 %all_gather.6.panel_hbm.panel_cols_ref = f32[1536,128]{1,0:T(8,128)S(1)} all-gather(f32[96,128]{1,0:T(8,128)S(1)} %gram.1), channel_id=1, replica_groups=mesh['row'=16,'col'=32] {'row'}, dimensions={0}, use_global_device_ids=true | all-gather | bytes 835584 | tf_op jit(solution)/shard_map/gram/all_gather | solution.py:524
  64.6 0.0 copy-start.1
  64.6 0.9 copy-done.1
  65.5 0.9 tile.5
  66.3 17.9 %all-to-all-start.1 = ((f32[32,32,128]{2,1,0:T(8,128)}), f32[32,32,128]{2,1,0:T(8,128)}, u32[]{:S(2)}, u32[]{:S(2)}) async-start(f32[32,32,128]{2,1,0:T(8,128)} %tile.5), calls=%async_computation.1 | async-start | bytes 1048576 | tf_op jit(solution)/shard_map/gram/all_to_all | solution.py:477
  84.2 0.0 copy-done
  84.3 2.0 mirror.1
  86.3 3.7 %collective-permute-start.2 = (f32[128,512]{1,0:T(8,128)S(1)}, f32[128,512]{1,0:T(8,128)S(1)}, u32[]{:S(2)}, u32[]{:S(2)}) collective-permute-start(f32[128,512]{1,0:T(8,128)S(1)} %get-tuple-element.26), channel_id=1, source_target_pairs={{0,32},{32,0},{64,96},{96,64},{128,160},{160,128},{192,224},{224,1... | collective-permute-start | bytes 786440 | tf_op jit(solution)/shard_map/mirror/ppermute | solution.py:532
  90.0 5.9 %collective-permute-done.2 = f32[128,512]{1,0:T(8,128)S(1)} collective-permute-done((f32[128,512]{1,0:T(8,128)S(1)}, f32[128,512]{1,0:T(8,128)S(1)}, u32[]{:S(2)}, u32[]{:S(2)}) %collective-permute-start.2) | collective-permute-done | bytes 262176 | tf_op jit(solution)/shard_map/mirror/ppermute | solution.py:532
  95.9 0.7 add.9
  96.6 0.0 all-to-all-done.1
  96.6 7.6 %all-to-all-start.2 = ((f32[8,16,512]{2,1,0:T(8,128)}), f32[8,16,512]{2,1,0:T(8,128)}, u32[]{:S(2)}, u32[]{:S(2)}) async-start(f32[8,16,512]{2,1,0:T(8,128)} %bitcast.10), calls=%async_computation.2 | async-start | bytes 524288 | tf_op jit(solution)/shard_map/mirror/all_to_all | solution.py:535
  104.3 0.0 copy-start.2
  104.3 13.5 %cholesky.1 = (f32[256,256]{1,0:T(8,128)}, f32[256,256]{1,0:T(8,128)S(1)}, f32[256,256]{1,0:T(8,128)S(1)}) custom-call(f32[1024,128]{1,0:T(8,128)} %bitcast.8.g_ref), custom_call_target="tpu_custom_call" | custom-call | flops 5000000000 | bytes 41943040 | tf_op jit(solution)/shard_map/factor/cholesky/pallas_call | solution.py:538
  117.8 0.0 copy-done.2
  117.8 2.3 symmetric.1
  120.1 0.0 copy-start.4
  120.1 1.0 copy-done.4
  121.0 0.0 copy-start.3
  121.0 0.0 all-to-all-done.2
  121.0 12.0 %all-to-all-start.3 = ((f32[32,8,1024]{2,1,0:T(8,128)}), f32[32,8,1024]{2,1,0:T(8,128)}, u32[]{:S(2)}, u32[]{:S(2)}) async-start(f32[32,8,1024]{2,1,0:T(8,128)} %bitcast.24), calls=%async_computation.3 | async-start | bytes 2097152 | tf_op jit(solution)/shard_map/sums/all_to_all | solution.py:564
  133.0 1.0 reduce_sum.19
  134.0 2.0 collective-permute-start.4
  136.1 3.5 %collective-permute-start.3 = (f32[8,512]{1,0:T(8,128)S(1)}, f32[8,512]{1,0:T(8,128)S(1)}, u32[]{:S(2)}, u32[]{:S(2)}) collective-permute-start(f32[8,512]{1,0:T(8,128)S(1)} %get-tuple-element.47), channel_id=1, source_target_pairs={{16,0},{0,1},{48,2},{32,3},{80,4},{64,5},{112,6},{96,7},{144,8},{1... | collective-permute-start | bytes 49160 | tf_op jit(solution)/shard_map/sums/ppermute | solution.py:503
  139.6 0.0 copy-done.10
  139.6 0.0 copy-done.3
  139.6 2.1 vectors.1
  141.7 0.0 copy-start.5
  141.7 1.0 copy-done.5
  142.6 0.0 copy-start.7
  142.7 0.8 copy-done.7
  143.4 1.4 collective-permute-done.4
  144.8 0.0 collective-permute-done.3
  144.8 5.4 %all-to-all-done.3 = f32[32,8,1024]{2,1,0:T(8,128)} async-done(((f32[32,8,1024]{2,1,0:T(8,128)}), f32[32,8,1024]{2,1,0:T(8,128)}, u32[]{:S(2)}, u32[]{:S(2)}) %all-to-all-start.3) | async-done | bytes 1048608 | tf_op jit(solution)/shard_map/sums/all_to_all | solution.py:564
  150.2 0.0 copy-start.6
  150.2 1.2 copy-done.6
  151.5 1.8 share.1.own_ref
  153.3 29.5 %all_gather.7.part_ref = f32[640,256]{1,0:T(8,128)S(1)} all-gather(f32[40,256]{1,0:T(8,128)S(1)} %share.1.own_ref), channel_id=1, replica_groups=mesh['row'=16,'col'=32] {'row'}, dimensions={0}, use_global_device_ids=true | all-gather | bytes 696320 | tf_op jit(solution)/shard_map/sums/all_gather | solution.py:570
  182.8 1.3 deal.1
  184.1 16.0 %all-to-all-start.4 = ((f32[32,56,256]{2,1,0:T(8,128)}), f32[32,56,256]{2,1,0:T(8,128)S(1)}, u32[]{:S(2)}, u32[]{:S(2)}) async-start(f32[32,56,256]{2,1,0:T(8,128)} %bitcast.13), calls=%async_computation.4 | async-start | bytes 3670016 | tf_op jit(solution)/shard_map/deal/all_to_all | solution.py:577
  200.2 11.5 %reflector.1 = (f32[256,256]{1,0:T(8,128)}, f32[256,256]{1,0:T(8,128)S(1)}) custom-call(f32[1024,128]{1,0:T(8,128)} %bitcast.8.g_ref, f32[256,256]{1,0:T(8,128)S(1)} %get-tuple-element.33.linv_ref), custom_call_target="tpu_custom_call" | custom-call | flops 5000000000 | bytes 41943040 | tf_op jit(solution)/shard_map/reflector/reflector/pallas_call | solution.py:579
  211.7 0.0 copy-start.9
  211.7 0.7 copy-done.9
  212.4 12.8 %all-to-all-done.4 = f32[32,56,256]{2,1,0:T(8,128)S(1)} async-done(((f32[32,56,256]{2,1,0:T(8,128)}), f32[32,56,256]{2,1,0:T(8,128)S(1)}, u32[]{:S(2)}, u32[]{:S(2)}) %all-to-all-start.4) | async-done | bytes 1835040 | tf_op jit(solution)/shard_map/deal/all_to_all | solution.py:577
  225.1 0.0 copy-start.11
  225.1 1.2 copy-done.11
  226.4 7.9 %update.1 = f32[4096,128]{1,0:T(8,128)} custom-call(s32[2]{0:T(128)} %copy-done.10, f32[256,256]{1,0:T(8,128)} %copy-done.9, f32[256,256]{1,0:T(8,128)} %get-tuple-element.43.refl_hbm, f32[1792,256]{1,0:T(8,128)} %bitcast.28, f32[256,512]{1,0:T(8,128)} %copy-done.7, f32[256,1024]{1,0:T(8,128)} %copy-done.5, f32[4096,128]{1,0:T(8,128)} %bitcast.17), custom_call_target="tpu_custom_call" | custom-call | bytes 8388608 | tf_op jit(solution)/shard_map/update/update/pallas_call | solution.py:589
  (5 shorter events, 0.1 us)
Async XLA Ops:
  0.6 12.4 %copy-start.8 = (f32[8,4,1,256]{3,2,1,0:T(1,128)S(1)}, f32[8,4,1,256]{3,2,1,0:T(1,128)}, u32[]{:S(2)}) copy-start(f32[8,4,1,256]{3,2,1,0:T(1,128)} %param.3) | copy-start | bytes 98308
  2.5 27.8 %all-to-all-start = ((f32[32,64,128]{2,1,0:T(8,128)}), f32[32,64,128]{2,1,0:T(8,128)S(1)}, u32[]{:S(2)}, u32[]{:S(2)}) async-start(f32[32,64,128]{2,1,0:T(8,128)} %tile.4), calls=%async_computation | async-start | bytes 2097152 | tf_op jit(solution)/shard_map/panel/all_to_all | solution.py:477
  13.0 71.2 %copy-start = (f32[4,1,256,2,1,256]{5,4,3,2,1,0:T(1,128)S(1)}, f32[4,1,256,2,1,256]{5,4,3,2,1,0:T(1,128)}, u32[]{:S(2)}) copy-start(f32[4,1,256,2,1,256]{5,4,3,2,1,0:T(1,128)} %param.2) | copy-start | bytes 6291460
  13.1 7.3 %collective-permute-start = (f32[32,128]{1,0:T(8,128)S(1)}, f32[32,128]{1,0:T(8,128)S(1)}, u32[]{:S(2)}, u32[]{:S(2)}) collective-permute-start(f32[32,128]{1,0:T(8,128)S(1)} %bitcast.31), channel_id=1, source_target_pairs={{0,0},{1,16},{2,32},{3,48},{4,64},{5,80},{6,96},{7,112},{8,128},{9... | collective-permute-start | bytes 49160 | tf_op jit(solution)/shard_map/panel/ppermute | solution.py:494
  18.4 4.8 %collective-permute-start.1 = (f32[32,128]{1,0:T(8,128)S(1)}, f32[32,128]{1,0:T(8,128)S(1)}, u32[]{:S(2)}, u32[]{:S(2)}) collective-permute-start(f32[32,128]{1,0:T(8,128)S(1)} %bitcast.30), channel_id=1, source_target_pairs={{0,16},{1,0},{2,48},{3,32},{4,80},{5,64},{6,112},{7,96},{8,144},{9... | collective-permute-start | bytes 49160 | tf_op jit(solution)/shard_map/panel/ppermute | solution.py:495
  20.4 119.2 %copy-start.10 = (s32[2]{0:T(128)}, s32[2]{0:T(128)S(1)}, u32[]{:S(2)}) copy-start(s32[2]{0:T(128)S(1)} %pad_add_fusion.place) | copy-start | bytes 28
  64.6 0.9 copy-start.1
  66.3 30.3 %all-to-all-start.1 = ((f32[32,32,128]{2,1,0:T(8,128)}), f32[32,32,128]{2,1,0:T(8,128)}, u32[]{:S(2)}, u32[]{:S(2)}) async-start(f32[32,32,128]{2,1,0:T(8,128)} %tile.5), calls=%async_computation.1 | async-start | bytes 1048576 | tf_op jit(solution)/shard_map/gram/all_to_all | solution.py:477
  86.3 9.6 %collective-permute-start.2 = (f32[128,512]{1,0:T(8,128)S(1)}, f32[128,512]{1,0:T(8,128)S(1)}, u32[]{:S(2)}, u32[]{:S(2)}) collective-permute-start(f32[128,512]{1,0:T(8,128)S(1)} %get-tuple-element.26), channel_id=1, source_target_pairs={{0,32},{32,0},{64,96},{96,64},{128,160},{160,128},{192,224},{224,1... | collective-permute-start | bytes 786440 | tf_op jit(solution)/shard_map/mirror/ppermute | solution.py:532
  96.6 24.4 %all-to-all-start.2 = ((f32[8,16,512]{2,1,0:T(8,128)}), f32[8,16,512]{2,1,0:T(8,128)}, u32[]{:S(2)}, u32[]{:S(2)}) async-start(f32[8,16,512]{2,1,0:T(8,128)} %bitcast.10), calls=%async_computation.2 | async-start | bytes 524288 | tf_op jit(solution)/shard_map/mirror/all_to_all | solution.py:535
  104.3 13.5 %copy-start.2 = (f32[1536,128]{1,0:T(8,128)S(1)}, f32[1536,128]{1,0:T(8,128)}, u32[]{:S(2)}) copy-start(f32[1536,128]{1,0:T(8,128)} %copy-done.1) | copy-start | bytes 2359300
  120.1 1.0 copy-start.4
  121.0 18.6 %copy-start.3 = (f32[1536,128]{1,0:T(8,128)S(1)}, f32[1536,128]{1,0:T(8,128)}, u32[]{:S(2)}) copy-start(f32[1536,128]{1,0:T(8,128)} %copy-done.1) | copy-start | bytes 2359300
  121.0 29.2 %all-to-all-start.3 = ((f32[32,8,1024]{2,1,0:T(8,128)}), f32[32,8,1024]{2,1,0:T(8,128)}, u32[]{:S(2)}, u32[]{:S(2)}) async-start(f32[32,8,1024]{2,1,0:T(8,128)} %bitcast.24), calls=%async_computation.3 | async-start | bytes 2097152 | tf_op jit(solution)/shard_map/sums/all_to_all | solution.py:564
  134.0 10.8 %collective-permute-start.4 = (f32[8,512]{1,0:T(8,128)S(1)}, f32[8,512]{1,0:T(8,128)S(1)}, u32[]{:S(2)}, u32[]{:S(2)}) collective-permute-start(f32[8,512]{1,0:T(8,128)S(1)} %get-tuple-element.46), channel_id=1, source_target_pairs={{0,0},{16,1},{32,2},{48,3},{64,4},{80,5},{96,6},{112,7},{128,8},{1... | collective-permute-start | bytes 49160 | tf_op jit(solution)/shard_map/sums/ppermute | solution.py:502
  136.1 8.8 %collective-permute-start.3 = (f32[8,512]{1,0:T(8,128)S(1)}, f32[8,512]{1,0:T(8,128)S(1)}, u32[]{:S(2)}, u32[]{:S(2)}) collective-permute-start(f32[8,512]{1,0:T(8,128)S(1)} %get-tuple-element.47), channel_id=1, source_target_pairs={{16,0},{0,1},{48,2},{32,3},{80,4},{64,5},{112,6},{96,7},{144,8},{1... | collective-permute-start | bytes 49160 | tf_op jit(solution)/shard_map/sums/ppermute | solution.py:503
  141.7 1.0 copy-start.5
  142.6 0.8 copy-start.7
  150.2 1.2 copy-start.6
  184.1 41.0 %all-to-all-start.4 = ((f32[32,56,256]{2,1,0:T(8,128)}), f32[32,56,256]{2,1,0:T(8,128)S(1)}, u32[]{:S(2)}, u32[]{:S(2)}) async-start(f32[32,56,256]{2,1,0:T(8,128)} %bitcast.13), calls=%async_computation.4 | async-start | bytes 3670016 | tf_op jit(solution)/shard_map/deal/all_to_all | solution.py:577
  211.7 0.7 copy-start.9
  225.1 1.2 copy-start.11
